TPU v7x, 32 devices: a whole 2x2x4 slice. The times are simulated.
32 devices in a mesh: row: 8 (over z, y), col: 4 (over x, core).
Axes of the slice: x: 2, y: 2, z: 4, core: 2. Of those that a mesh axis runs over, the one named last changes fastest.
Arguments:
- pair: bfloat16 [2, 512, 512, 128], P(None, 'row', 'col'), may hold values from -6 to 6
- cotangent: bfloat16 [2, 512, 512, 128], P(None, 'row', 'col'), may hold values from -6 to 6
- segments: int32 [2, 512], replicated, may hold values from 0 to 3, never falling along the last dimension, each value on 1 to 256 neighbouring positions
- lengths: int32 [2], replicated, may hold values from 1 to 512, 768 in all
- weights: float32 [5, 16384], P(None, 'row')
- moment_one: float32 [5, 16384], P(None, 'row'), may hold values from -24 to 24
- moment_two: float32 [5, 16384], P(None, 'row'), may hold values from 1.31072 to 5.24288
- gain: float32 [128], replicated, may hold values from 0.5 to 1.5
- gain_m: float32 [128], replicated, may hold values from -512 to 512
- gain_v: float32 [128], replicated, may hold values from 524.288 to 2097.152
- chain_bias: float32 [4], replicated, may hold values from -1.5 to 1.5
- bias_m: float32 [4], replicated, may hold values from -48 to 48
- bias_v: float32 [4], replicated, may hold values from 5.24288 to 20.97152
Outputs:
- pair_out: bfloat16 [2, 512, 512, 128], P(None, 'row', 'col')
- pair_grad: bfloat16 [2, 512, 512, 128], P(None, 'row', 'col')
- new_weights: float32 [5, 16384], P(None, 'row')
- new_moment_one: float32 [5, 16384], P(None, 'row')
- new_moment_two: float32 [5, 16384], P(None, 'row')
- new_gain: float32 [128], replicated
- new_gain_m: float32 [128], replicated
- new_gain_v: float32 [128], replicated
- new_bias: float32 [4], replicated
- new_bias_m: float32 [4], replicated
- new_bias_v: float32 [4], replicated
All inputs are finite; a program needn't handle non-finite values.
Results may differ from a plain program's by a relative error of at most 0.017.
The roundings to bfloat16 on the way count: a program that leaves them out, or rounds other values in their place, can miss the bound.
Values may be sent and summed in bfloat16 or wider, within the bound.
A program may use at most 256 MiB of HBM per device.

v0:
```python
import math

import jax
import jax.numpy as jnp
from jax import lax
from jax.sharding import PartitionSpec as P

STEP = 10


beta_one = 0.9
beta_two = 0.999
epsilon = 1e-06
decay = 0.01
rate = 0.25


def attend_crop(block, block_cot, seg_vals, keymask, wbf, gain, chain_bias):
    total_rows = block.shape[0]
    ncols = block.shape[1]
    width = block.shape[2]
    heads = chain_bias.shape[0]
    hsize = width // heads
    scale = 1.0 / math.sqrt(hsize)
    zval = block.astype(jnp.float32)
    feature_mean = jnp.mean(zval, -1, keepdims=True)
    centered_input = zval - feature_mean
    var = jnp.mean(centered_input * centered_input, -1, keepdims=True)
    inverse_deviation = lax.rsqrt(var + 1e-05)
    standardized_input = centered_input * inverse_deviation
    normalized_output = (standardized_input * gain).astype(jnp.bfloat16)
    proj = jnp.einsum(
        "ijc,kcd->kijd", normalized_output, wbf[0:4], preferred_element_type=jnp.float32
    )
    query = proj[0].astype(jnp.bfloat16).reshape(total_rows, ncols, heads, hsize)
    keys = proj[1].astype(jnp.bfloat16).reshape(total_rows, ncols, heads, hsize)
    values = proj[2].astype(jnp.bfloat16).reshape(total_rows, ncols, heads, hsize)
    gate = jax.nn.sigmoid(proj[3])
    same = (seg_vals[:, None] == seg_vals[None, :]).astype(jnp.float32)
    scores = jnp.einsum("ijhd,kjhd->jhik", query, keys, preferred_element_type=jnp.float32) * scale
    scores = scores + chain_bias[None, :, None, None] * same[None, None]
    scores = jnp.where(keymask[None, None, None, :], scores, -1e30)
    peak = jnp.max(scores, -1, keepdims=True)
    expo = jnp.exp(scores - peak)
    probs32 = expo / jnp.sum(expo, -1, keepdims=True)
    probs = probs32.astype(jnp.bfloat16)
    attended = jnp.einsum(
        "jhik,kjhd->ijhd", probs, values, preferred_element_type=jnp.float32
    ).reshape(total_rows, ncols, width)
    gated = (attended * gate).astype(jnp.bfloat16)
    result = zval + jnp.einsum("ijc,cd->ijd", gated, wbf[4], preferred_element_type=jnp.float32)
    grad_w4 = jnp.einsum("ijc,ijd->cd", gated, block_cot, preferred_element_type=jnp.float32)
    dgated = (
        jnp.einsum("ijd,cd->ijc", block_cot, wbf[4], preferred_element_type=jnp.float32)
        .astype(jnp.bfloat16)
        .astype(jnp.float32)
    )
    dattend = (dgated * gate).astype(jnp.bfloat16)
    dgate_pre = (dgated * attended * gate * (1.0 - gate)).astype(jnp.bfloat16)
    dattend_h = dattend.reshape(total_rows, ncols, heads, hsize)
    dprobs = (
        jnp.einsum("ijhd,kjhd->jhik", dattend_h, values, preferred_element_type=jnp.float32)
        .astype(jnp.bfloat16)
        .astype(jnp.float32)
    )
    dvalues = jnp.einsum(
        "jhik,ijhd->kjhd", probs, dattend_h, preferred_element_type=jnp.float32
    ).astype(jnp.bfloat16)
    dscores = probs32 * (dprobs - jnp.sum(probs32 * dprobs, -1, keepdims=True))
    dbias = jnp.einsum("jhik,ik->h", dscores, same)
    dscore_b = (dscores * scale).astype(jnp.bfloat16)
    dquery = jnp.einsum(
        "jhik,kjhd->ijhd", dscore_b, keys, preferred_element_type=jnp.float32
    ).astype(jnp.bfloat16)
    dkeys = jnp.einsum(
        "jhik,ijhd->kjhd", dscore_b, query, preferred_element_type=jnp.float32
    ).astype(jnp.bfloat16)
    dproj = jnp.stack(
        [
            dquery.reshape(total_rows, ncols, width),
            dkeys.reshape(total_rows, ncols, width),
            dvalues.reshape(total_rows, ncols, width),
            dgate_pre,
        ]
    )
    grad_w03 = jnp.einsum(
        "ijc,kijd->kcd", normalized_output, dproj, preferred_element_type=jnp.float32
    )
    normalized_gradient = jnp.einsum(
        "kijd,kcd->ijc", dproj, wbf[0:4], preferred_element_type=jnp.float32
    )
    gain_gradient = jnp.sum(normalized_gradient * standardized_input, (0, 1))
    standardized_gradient = normalized_gradient * gain
    dzval = inverse_deviation * (
        standardized_gradient
        - jnp.mean(standardized_gradient, -1, keepdims=True)
        - standardized_input
        * jnp.mean(standardized_gradient * standardized_input, -1, keepdims=True)
    )
    grad_in = (block_cot.astype(jnp.float32) + dzval).astype(jnp.bfloat16)
    grad_all = jnp.concatenate([grad_w03, grad_w4[None]], 0)
    return (result.astype(jnp.bfloat16), grad_in, grad_all, gain_gradient, dbias)


def moments(value, grad, first, second):
    first_new = beta_one * first + (1.0 - beta_one) * grad
    second_new = beta_two * second + (1.0 - beta_two) * grad * grad
    step_dir = (
        first_new
        / (1.0 - beta_one**STEP)
        / (jnp.sqrt(second_new / (1.0 - beta_two**STEP)) + epsilon)
        + decay * value
    )
    return (first_new, second_new, step_dir)


def body(
    pair,
    cotangent,
    segments,
    lengths,
    weights,
    moment_one,
    moment_two,
    gain,
    gain_m,
    gain_v,
    chain_bias,
    bias_m,
    bias_v,
):
    width = gain.shape[0]
    flat_weights = lax.all_gather(weights, "row", axis=1, tiled=True)
    wbf = flat_weights.reshape(5, width, width).astype(jnp.bfloat16)
    total_rows = segments.shape[1]
    positions = jnp.arange(total_rows, dtype=jnp.int32)
    columns, column_cots = (
        lax.all_to_all(pair, "row", split_axis=2, concat_axis=1, tiled=True),
        lax.all_to_all(cotangent, "row", split_axis=2, concat_axis=1, tiled=True),
    )

    def per_crop(item):
        block, block_cot, segs, length = item
        return attend_crop(
            block, block_cot, segs.astype(jnp.float32), positions < length, wbf, gain, chain_bias
        )

    outs_col, grads_col, dweights, gain_gradient, dbias = lax.map(
        per_crop, (columns, column_cots, segments, lengths)
    )
    pair_out, pair_grad = (
        lax.all_to_all(outs_col, "row", split_axis=1, concat_axis=2, tiled=True),
        lax.all_to_all(grads_col, "row", split_axis=1, concat_axis=2, tiled=True),
    )
    dweights = jnp.sum(dweights, 0).reshape(5, width * width)
    gain_gradient = jnp.sum(gain_gradient, 0)
    dbias = jnp.sum(dbias, 0)
    shard_w = lax.psum_scatter(dweights, "row", scatter_dimension=1, tiled=True)
    shard_w, gain_part, bias_part = lax.psum((shard_w, gain_gradient, dbias), "col")
    first_w, second_w, step_w = moments(weights, shard_w, moment_one, moment_two)
    squares = jnp.concatenate(
        [jnp.sum(weights * weights, axis=1), jnp.sum(step_w * step_w, axis=1)]
    )
    squares, gain_grad, bias_grad = lax.psum((squares, gain_part, bias_part), "row")
    ratio_w = jnp.sqrt(squares[0:5]) / jnp.sqrt(squares[5:10])
    new_weights = weights - rate * ratio_w[:, None] * step_w
    first_g, second_g, step_g = moments(gain, gain_grad, gain_m, gain_v)
    gain_ratio = jnp.sqrt(jnp.sum(gain * gain)) / jnp.sqrt(jnp.sum(step_g * step_g))
    new_gain = gain - rate * gain_ratio * step_g
    first_b, second_b, step_b = moments(chain_bias, bias_grad, bias_m, bias_v)
    bias_ratio = jnp.sqrt(jnp.sum(chain_bias * chain_bias)) / jnp.sqrt(jnp.sum(step_b * step_b))
    new_bias = chain_bias - rate * bias_ratio * step_b
    return (
        pair_out,
        pair_grad,
        new_weights,
        first_w,
        second_w,
        new_gain,
        first_g,
        second_g,
        new_bias,
        first_b,
        second_b,
    )


def solution(mesh):
    return jax.shard_map(
        body,
        mesh=mesh,
        in_specs=(
            P(None, "row", "col", None),
            P(None, "row", "col", None),
            P(),
            P(),
            P(None, "row"),
            P(None, "row"),
            P(None, "row"),
            P(),
            P(),
            P(),
            P(),
            P(),
            P(),
        ),
        out_specs=(
            P(None, "row", "col", None),
            P(None, "row", "col", None),
            P(None, "row"),
            P(None, "row"),
            P(None, "row"),
            P(),
            P(),
            P(),
            P(),
            P(),
            P(),
        ),
        check_vma=False,
    )
```

profile of v0, /device:TPU:0, one launch (start us, length us, event | category | flops | bytes accessed | tf_op | source)
XLA Modules:
  0.0 1285.0 jit_solution(12999275359556181282)
XLA Ops:
  7.2 6.9 copy.86
  14.1 7.3 all-to-all-start
  21.4 6.8 copy.88
  28.2 86.4 %all-to-all-done = bf16[2,64,128,128]{3,1,0,2:T(8,128)(2,1)} async-done(((bf16[2,64,128,128]{3,1,0,2:T(8,128)(2,1)}), bf16[2,64,128,128]{3,1,0,2:T(8,128)(2,1)}, u32[]{:S(2)}, u32[]{:S(2)}) %all-to-all-start) | async-done | bytes 4194336 | tf_op jit(solution)/shard_map/all_to_all | solution.py:138
  114.6 4.5 all-to-all-start.1
  119.3 112.9 %all_gather.3 = bf16[5,16384]{1,0:T(8,128)(2,1)S(1)} all-gather(bf16[5,2048]{1,0:T(8,128)(2,1)S(1)} %convert.12), channel_id=1, replica_groups=mesh['row'=8,'col'=4] {'row'}, dimensions={1}, use_global_device_ids=true | all-gather | bytes 184320 | tf_op jit(solution)/shard_map/all_gather | solution.py:133
  232.4 5.6 copy.87
  238.0 5.6 copy.89
  243.6 773.7 %while.19 = (s32[]{:T(128)}, bf16[2,512,16,128]{3,2,0,1:T(8,128)(2,1)}, bf16[2,512,16,128]{3,2,0,1:T(8,128)(2,1)}, f32[2,5,128,128]{2,3,1,0:T(8,128)}, f32[2,128...) while((s32[]{:T(128)}, ...), condition=%wide.region_10.11_spmd.clone, body=%wide.region_0.10_spmd.clone.sunk | while | flops 11167000576 | bytes 990959232 | solution.py:148
  269.0 2.2 convert_reduce_fusion.2
  271.2 3.6 fusion.157
  275.2 1.0 copy-done.4
  276.1 2.6 broadcast_multiply_fusion.9
  278.7 5.5 fusion.158
  284.2 10.2 fusion.160
  294.4 3.0 fusion.159
  297.4 37.8 %fusion.161 = (f32[16,4,512]{2,1,0:T(4,128)S(1)}, f32[16,4,512,512]{2,3,1,0:T(8,128)}) fusion(f32[4,512,512]{1,2,0:T(8,128)} %broadcast_multiply_fusion.9, pred[512]{0:T(512)(128)(4,1)S(1)} %iota_compare_fusion.2, bf16[512,16,4,32]{0,3,2,1:T(8,128)(2,1)} %bitcast.303, bf16[512,16,4,32]{0,3,2,1:T(8,128)(2,1)} %bitcast.305), kind=kOutput, calls=%fused_computation.138.clone.1 | convolution fusion | flops 1157628416 | bytes 75629056 | tf_op jit(solution)/shard_map/while/body/eval_jaxpr/sub | solution.py:44
  335.2 26.1 %fusion.162 = (bf16[512,16,4,32]{0,3,2,1:T(8,128)(2,1)}, f32[16,4,32,512]{3,2,1,0:T(8,128)}) fusion(f32[512,16,4,32]{0,3,2,1:T(8,128)} %bitcast.300, bf16[512,16,4,32]{0,3,2,1:T(8,128)(2,1)S(1)} %bitcast.295, f32[16,4,512,512]{2,3,1,0:T(8,128)} %get-tuple-element.323, f32[16,4,512]{2,1,0:T(4,128)S(1)} %get-tuple-element.324), kind=kOutput, calls=%fused_computation.58.clone.1 | convolution fusion | flops 1109393408 | bytes 79822848 | tf_op jit(solution)/shard_map/while/body/eval_jaxpr/jhik,kjhd->ijhd/dot_general | solution.py:47
  361.3 6.7 fusion.163
  368.7 1.6 fusion.170
  370.4 2.2 fusion.169
  372.5 25.4 %fusion.164 = bf16[16,4,32,512]{3,2,1,0:T(8,128)(2,1)} fusion(bf16[512,16,4,32]{0,3,2,1:T(8,128)(2,1)} %bitcast.301, f32[16,4,512,512]{2,3,1,0:T(8,128)} %get-tuple-element.323, f32[16,4,512]{2,1,0:T(4,128)S(1)} %get-tuple-element.324), kind=kOutput, calls=%fused_computation.74.clone.1 | convolution fusion | flops 1108344832 | bytes 71434240 | tf_op jit(solution)/shard_map/while/body/eval_jaxpr/jhik,ijhd->kjhd/dot_general | solution.py:66
  397.9 15.3 %convolution_convert_fusion.2 = bf16[16,4,512,512]{2,3,1,0:T(8,128)(2,1)} fusion(bf16[512,16,4,32]{0,3,2,1:T(8,128)(2,1)} %bitcast.302, bf16[512,16,4,32]{0,3,2,1:T(8,128)(2,1)S(1)} %bitcast.296), kind=kOutput, calls=%fused_computation.16.clone.1 | convolution fusion | flops 1090519040 | bytes 37748736 | tf_op jit(solution)/shard_map/while/body/eval_jaxpr/ijhd,kjhd->jhik/dot_general | solution.py:62
  413.2 64.6 %fusion.166 = bf16[16,4,32,512]{3,2,1,0:T(8,128)(2,1)} fusion(bf16[512,16,4,32]{0,3,2,1:T(8,128)(2,1)} %bitcast.306, bf16[16,4,512,512]{2,3,1,0:T(8,128)(2,1)} %convolution_convert_fusion.2, f32[16,4,512,512]{2,3,1,0:T(8,128)} %get-tuple-element.323, f32[16,4,512]{2,1,0:T(4,128)S(1)} %get-tuple-element.324), kind=kOutput, calls=%fused_computation.72.clone.1 | convolution fusion | flops 1225818624 | bytes 104988672 | tf_op jit(solution)/shard_map/while/body/eval_jaxpr/jhik,kjhd->ijhd/dot_general | solution.py:72
  477.9 63.8 %fusion.165 = bf16[16,4,32,512]{3,2,1,0:T(8,128)(2,1)} fusion(bf16[512,16,4,32]{0,3,2,1:T(8,128)(2,1)S(1)} %bitcast.304, bf16[16,4,512,512]{2,3,1,0:T(8,128)(2,1)} %convolution_convert_fusion.2, f32[16,4,512,512]{2,3,1,0:T(8,128)} %get-tuple-element.323, f32[16,4,512]{2,1,0:T(4,128)S(1)} %get-tuple-element.324), kind=kOutput, calls=%fused_computation.73.clone.1 | convolution fusion | flops 1225818624 | bytes 104988672 | tf_op jit(solution)/shard_map/while/body/eval_jaxpr/jhik,ijhd->kjhd/dot_general | solution.py:75
  541.6 63.5 %fusion.173 = f32[4,512,512]{1,2,0:T(8,128)S(1)} fusion(bf16[16,4,512,512]{2,3,1,0:T(8,128)(2,1)} %convolution_convert_fusion.2, f32[16,4,512,512]{2,3,1,0:T(8,128)} %get-tuple-element.323, f32[16,4,512]{2,1,0:T(4,128)S(1)} %get-tuple-element.324), kind=kOutput, calls=%fused_computation.139.clone.1 | output fusion | flops 133202432 | bytes 104988672 | tf_op jit(solution)/shard_map/while/body/eval_jaxpr/sub | solution.py:69
  606.8 6.8 fusion.171
  613.7 10.2 fusion.167
  624.0 9.6 fusion.168
  633.7 3.4 copy_dynamic-update-slice_fusion.3
  637.2 2.0 copy-done.18
  639.3 1.3 copy-done.20
  642.6 2.2 convert_reduce_fusion.2
  644.8 3.6 fusion.157
  649.7 2.6 broadcast_multiply_fusion.9
  652.3 5.5 fusion.158
  657.8 10.2 fusion.160
  668.0 3.0 fusion.159
  671.0 37.8 %fusion.161 = (f32[16,4,512]{2,1,0:T(4,128)S(1)}, f32[16,4,512,512]{2,3,1,0:T(8,128)}) fusion(f32[4,512,512]{1,2,0:T(8,128)} %broadcast_multiply_fusion.9, pred[512]{0:T(512)(128)(4,1)S(1)} %iota_compare_fusion.2, bf16[512,16,4,32]{0,3,2,1:T(8,128)(2,1)} %bitcast.303, bf16[512,16,4,32]{0,3,2,1:T(8,128)(2,1)} %bitcast.305), kind=kOutput, calls=%fused_computation.138.clone.1 | convolution fusion | flops 1157628416 | bytes 75629056 | tf_op jit(solution)/shard_map/while/body/eval_jaxpr/sub | solution.py:44
  708.8 26.1 %fusion.162 = (bf16[512,16,4,32]{0,3,2,1:T(8,128)(2,1)}, f32[16,4,32,512]{3,2,1,0:T(8,128)}) fusion(f32[512,16,4,32]{0,3,2,1:T(8,128)} %bitcast.300, bf16[512,16,4,32]{0,3,2,1:T(8,128)(2,1)S(1)} %bitcast.295, f32[16,4,512,512]{2,3,1,0:T(8,128)} %get-tuple-element.323, f32[16,4,512]{2,1,0:T(4,128)S(1)} %get-tuple-element.324), kind=kOutput, calls=%fused_computation.58.clone.1 | convolution fusion | flops 1109393408 | bytes 79822848 | tf_op jit(solution)/shard_map/while/body/eval_jaxpr/jhik,kjhd->ijhd/dot_general | solution.py:47
  734.9 6.7 fusion.163
  742.3 1.6 fusion.170
  744.0 2.2 fusion.169
  746.1 25.4 %fusion.164 = bf16[16,4,32,512]{3,2,1,0:T(8,128)(2,1)} fusion(bf16[512,16,4,32]{0,3,2,1:T(8,128)(2,1)} %bitcast.301, f32[16,4,512,512]{2,3,1,0:T(8,128)} %get-tuple-element.323, f32[16,4,512]{2,1,0:T(4,128)S(1)} %get-tuple-element.324), kind=kOutput, calls=%fused_computation.74.clone.1 | convolution fusion | flops 1108344832 | bytes 71434240 | tf_op jit(solution)/shard_map/while/body/eval_jaxpr/jhik,ijhd->kjhd/dot_general | solution.py:66
  771.5 15.3 %convolution_convert_fusion.2 = bf16[16,4,512,512]{2,3,1,0:T(8,128)(2,1)} fusion(bf16[512,16,4,32]{0,3,2,1:T(8,128)(2,1)} %bitcast.302, bf16[512,16,4,32]{0,3,2,1:T(8,128)(2,1)S(1)} %bitcast.296), kind=kOutput, calls=%fused_computation.16.clone.1 | convolution fusion | flops 1090519040 | bytes 37748736 | tf_op jit(solution)/shard_map/while/body/eval_jaxpr/ijhd,kjhd->jhik/dot_general | solution.py:62
  786.8 64.6 %fusion.166 = bf16[16,4,32,512]{3,2,1,0:T(8,128)(2,1)} fusion(bf16[512,16,4,32]{0,3,2,1:T(8,128)(2,1)} %bitcast.306, bf16[16,4,512,512]{2,3,1,0:T(8,128)(2,1)} %convolution_convert_fusion.2, f32[16,4,512,512]{2,3,1,0:T(8,128)} %get-tuple-element.323, f32[16,4,512]{2,1,0:T(4,128)S(1)} %get-tuple-element.324), kind=kOutput, calls=%fused_computation.72.clone.1 | convolution fusion | flops 1225818624 | bytes 104988672 | tf_op jit(solution)/shard_map/while/body/eval_jaxpr/jhik,kjhd->ijhd/dot_general | solution.py:72
  851.5 63.8 %fusion.165 = bf16[16,4,32,512]{3,2,1,0:T(8,128)(2,1)} fusion(bf16[512,16,4,32]{0,3,2,1:T(8,128)(2,1)S(1)} %bitcast.304, bf16[16,4,512,512]{2,3,1,0:T(8,128)(2,1)} %convolution_convert_fusion.2, f32[16,4,512,512]{2,3,1,0:T(8,128)} %get-tuple-element.323, f32[16,4,512]{2,1,0:T(4,128)S(1)} %get-tuple-element.324), kind=kOutput, calls=%fused_computation.73.clone.1 | convolution fusion | flops 1225818624 | bytes 104988672 | tf_op jit(solution)/shard_map/while/body/eval_jaxpr/jhik,ijhd->kjhd/dot_general | solution.py:75
  915.2 63.5 %fusion.173 = f32[4,512,512]{1,2,0:T(8,128)S(1)} fusion(bf16[16,4,512,512]{2,3,1,0:T(8,128)(2,1)} %convolution_convert_fusion.2, f32[16,4,512,512]{2,3,1,0:T(8,128)} %get-tuple-element.323, f32[16,4,512]{2,1,0:T(4,128)S(1)} %get-tuple-element.324), kind=kOutput, calls=%fused_computation.139.clone.1 | output fusion | flops 133202432 | bytes 104988672 | tf_op jit(solution)/shard_map/while/body/eval_jaxpr/sub | solution.py:69
  980.4 6.8 fusion.171
  987.3 10.2 fusion.167
  997.6 9.6 fusion.168
  1007.3 3.4 copy_dynamic-update-slice_fusion.3
  1010.8 2.0 copy-done.18
  1012.9 1.3 copy-done.20
  1017.3 93.0 %all_to_all.72 = bf16[2,512,16,128]{3,2,0,1:T(8,128)(2,1)} all-to-all(bf16[2,512,16,128]{3,2,0,1:T(8,128)(2,1)} %get-tuple-element.424), channel_id=1, replica_groups=mesh['row'=8,'col'=4] {'row'}, dimensions={1} | all-to-all | bytes 8388608 | tf_op jit(solution)/shard_map/all_to_all | solution.py:152
  1110.4 4.7 all-to-all-start.3
  1115.3 1.0 copy.127
  1116.4 112.6 %reduce-scatter.2.cloned.1.call-done = f32[5,2048]{1,0:T(8,128)} async-done(((f32[5,16384]{1,0:T(8,128)}), f32[5,2048]{1,0:T(8,128)}) %reduce-scatter.2.cloned.1.call-update) | async-done | bytes 40976 | tf_op jit(solution)/shard_map/reduce_scatter | solution.py:158
  1229.1 11.4 all-reduce.1
  1240.8 19.4 %all-reduce = (f32[10]{0:T(128)S(1)}, f32[128]{0:T(128)S(1)}, f32[4]{0:T(128)S(1)}) all-reduce(f32[10]{0:T(128)S(1)} %pad_maximum_fusion.5, f32[128]{0:T(128)S(1)} %get-tuple-element.194, f32[4]{0:T(128)S(1)} %get-tuple-element.195), channel_id=1, replica_groups=mesh['row'=8,'col'=4] {'row'}, use_global_device_ids=true, to_apply=%region_16.17 | all-reduce | flops 142 | bytes 1136 | tf_op jit(solution)/shard_map/psum | solution.py:164
  1260.2 1.1 multiply_reduce_fusion.5
  1262.7 1.1 multiply_reduce_fusion.3
  1267.0 5.4 copy.92
  1272.5 5.4 copy.94
  (215 shorter events, 13.3 us)
Async XLA Ops:
  14.1 100.6 %all-to-all-start = ((bf16[2,64,128,128]{3,1,0,2:T(8,128)(2,1)}), bf16[2,64,128,128]{3,1,0,2:T(8,128)(2,1)}, u32[]{:S(2)}, u32[]{:S(2)}) async-start(bf16[2,64,128,128]{3,1,0,2:T(8,128)(2,1)} %copy.86), calls=%async_computation | async-start | bytes 8388608 | tf_op jit(solution)/shard_map/all_to_all | solution.py:138
  28.2 91.0 %copy-start.24 = (f32[5,2048]{1,0:T(8,128)S(1)}, f32[5,2048]{1,0:T(8,128)}, u32[]{:S(2)}) copy-start(f32[5,2048]{1,0:T(8,128)} %param.19) | copy-start | bytes 122884
  114.6 123.4 %all-to-all-start.1 = ((bf16[2,64,128,128]{3,1,0,2:T(8,128)(2,1)}), bf16[2,64,128,128]{3,1,0,2:T(8,128)(2,1)}, u32[]{:S(2)}, u32[]{:S(2)}) async-start(bf16[2,64,128,128]{3,1,0,2:T(8,128)(2,1)} %copy.88), calls=%async_computation.1 | async-start | bytes 8388608 | tf_op jit(solution)/shard_map/all_to_all | solution.py:139
  267.0 11.7 copy-start.10
  271.2 7.5 copy-start.12
  274.8 9.4 copy-start.14
  284.2 10.2 copy-start.3
  361.3 6.7 copy-start.6
  361.3 7.4 copy-start.8
  413.2 64.7 %copy-start.9 = (bf16[1,512,16,128]{1,3,0,2:T(8,128)(2,1)S(1)}, bf16[1,512,16,128]{1,3,0,2:T(8,128)(2,1)}, u32[]{:S(2)}) copy-start(bf16[1,512,16,128]{1,3,0,2:T(8,128)(2,1)} %get-tuple-element.321) | copy-start | bytes 6291460 | tf_op jit(solution)/shard_map/while
  541.6 63.5 %copy-start.5 = (f32[512,512]{0,1:T(8,128)S(1)}, f32[512,512]{0,1:T(8,128)}, u32[]{:S(2)}) copy-start(f32[512,512]{0,1:T(8,128)} %copy-done.4) | copy-start | bytes 3145732 | tf_op jit(solution)/shard_map/while
  606.8 6.8 copy-start.37
  606.8 6.8 copy-start.2
  606.8 6.8 copy-start.11
  606.8 6.9 copy-start.49
  606.8 6.9 copy-start.50
  606.8 6.9 copy-start.51
  613.7 10.2 copy-start.39
  613.7 19.9 %copy-start.21 = (f32[2,5,128,128]{2,3,1,0:T(8,128)S(1)}, f32[2,5,128,128]{2,3,1,0:T(8,128)}, u32[]{:S(2)}) copy-start(f32[2,5,128,128]{2,3,1,0:T(8,128)} %get-tuple-element.353) | copy-start | bytes 1966084 | tf_op jit(solution)/shard_map/while
  623.9 9.7 copy-start.40
  623.9 9.7 copy-start.16
  623.9 9.7 copy-start.7
  623.9 9.7 copy-start.17
  624.0 9.7 copy-start.19
  633.7 6.9 copy-start.29
  633.7 6.9 copy-start.34
  633.7 6.9 copy-start.47
  640.6 11.7 copy-start.10
  644.8 7.5 copy-start.12
  648.4 9.4 copy-start.14
  657.8 10.2 copy-start.3
  734.9 6.7 copy-start.6
  734.9 7.4 copy-start.8
  786.8 64.7 %copy-start.9 = (bf16[1,512,16,128]{1,3,0,2:T(8,128)(2,1)S(1)}, bf16[1,512,16,128]{1,3,0,2:T(8,128)(2,1)}, u32[]{:S(2)}) copy-start(bf16[1,512,16,128]{1,3,0,2:T(8,128)(2,1)} %get-tuple-element.321) | copy-start | bytes 6291460 | tf_op jit(solution)/shard_map/while
  915.2 63.5 %copy-start.5 = (f32[512,512]{0,1:T(8,128)S(1)}, f32[512,512]{0,1:T(8,128)}, u32[]{:S(2)}) copy-start(f32[512,512]{0,1:T(8,128)} %copy-done.4) | copy-start | bytes 3145732 | tf_op jit(solution)/shard_map/while
  980.4 6.8 copy-start.37
  980.4 6.8 copy-start.2
  980.4 6.8 copy-start.11
  980.4 6.9 copy-start.49
  980.4 6.9 copy-start.50
  980.4 6.9 copy-start.51
  987.3 10.2 copy-start.39
  987.3 19.9 %copy-start.21 = (f32[2,5,128,128]{2,3,1,0:T(8,128)S(1)}, f32[2,5,128,128]{2,3,1,0:T(8,128)}, u32[]{:S(2)}) copy-start(f32[2,5,128,128]{2,3,1,0:T(8,128)} %get-tuple-element.353) | copy-start | bytes 1966084 | tf_op jit(solution)/shard_map/while
  997.5 9.7 copy-start.40
  997.5 9.7 copy-start.16
  997.5 9.7 copy-start.7
  997.5 9.7 copy-start.17
  997.6 9.7 copy-start.19
  1007.3 6.9 copy-start.29
  1007.3 6.9 copy-start.34
  1007.3 6.9 copy-start.47
  1110.3 130.2 %copy-start.25 = (f32[5,2048]{1,0:T(8,128)S(1)}, f32[5,2048]{1,0:T(8,128)}, u32[]{:S(2)}) copy-start(f32[5,2048]{1,0:T(8,128)} %param.19) | copy-start | bytes 122884
  1110.3 130.2 %copy-start.31 = (f32[5,2048]{1,0:T(8,128)S(1)}, f32[5,2048]{1,0:T(8,128)}, u32[]{:S(2)}) copy-start(f32[5,2048]{1,0:T(8,128)} %param.20) | copy-start | bytes 122884
  1110.3 130.2 %copy-start.32 = (f32[5,2048]{1,0:T(8,128)S(1)}, f32[5,2048]{1,0:T(8,128)}, u32[]{:S(2)}) copy-start(f32[5,2048]{1,0:T(8,128)} %param.21) | copy-start | bytes 122884
  1110.3 149.9 %copy-start.30 = (f32[128]{0:T(128)S(1)}, f32[128]{0:T(128)}, u32[]{:S(2)}) copy-start(f32[128]{0:T(128)} %param.22) | copy-start | bytes 1540
  1110.3 149.9 %copy-start.42 = (f32[128]{0:T(128)S(1)}, f32[128]{0:T(128)}, u32[]{:S(2)}) copy-start(f32[128]{0:T(128)} %param.23) | copy-start | bytes 1540
  1110.3 149.8 %copy-start.43 = (f32[128]{0:T(128)S(1)}, f32[128]{0:T(128)}, u32[]{:S(2)}) copy-start(f32[128]{0:T(128)} %param.24) | copy-start | bytes 1540
  1110.3 152.3 %copy-start.35 = (f32[4]{0:T(128)S(1)}, f32[4]{0:T(128)}, u32[]{:S(2)}) copy-start(f32[4]{0:T(128)} %param.25) | copy-start | bytes 52
  1110.3 152.3 %copy-start.44 = (f32[4]{0:T(128)S(1)}, f32[4]{0:T(128)}, u32[]{:S(2)}) copy-start(f32[4]{0:T(128)} %param.26) | copy-start | bytes 52
  1110.4 152.3 %copy-start.45 = (f32[4]{0:T(128)S(1)}, f32[4]{0:T(128)}, u32[]{:S(2)}) copy-start(f32[4]{0:T(128)} %param.27) | copy-start | bytes 52
  1110.4 162.1 %all-to-all-start.3 = ((bf16[2,512,16,128]{3,2,0,1:T(8,128)(2,1)}), bf16[2,512,16,128]{3,2,0,1:T(8,128)(2,1)}, u32[]{:S(2)}, u32[]{:S(2)}) async-start(bf16[2,512,16,128]{3,2,0,1:T(8,128)(2,1)} %get-tuple-element.425), calls=%async_computation.3 | async-start | bytes 8388608 | tf_op jit(solution)/shard_map/all_to_all | solution.py:153
  1115.1 114.0 %reduce-scatter.2.cloned.1.call-start = ((), (), s32[]{:S(2)}) async-start(), calls=%async_computation.5 | async-start | bytes 589824 | tf_op jit(solution)/shard_map/reduce_scatter | solution.py:158
  1240.7 31.8 %copy-start.26 = (f32[5,2048]{1,0:T(8,128)}, f32[5,2048]{1,0:T(8,128)S(1)}, u32[]{:S(2)}) copy-start(f32[5,2048]{1,0:T(8,128)S(1)} %get-tuple-element.204) | copy-start | bytes 122884
  1240.7 31.8 %copy-start.27 = (f32[5,2048]{1,0:T(8,128)}, f32[5,2048]{1,0:T(8,128)S(1)}, u32[]{:S(2)}) copy-start(f32[5,2048]{1,0:T(8,128)S(1)} %get-tuple-element.205) | copy-start | bytes 122884
  (26 other events, 73.5 us)
Sparse Core Ops, SparseCore 0:
  1119.8 109.1 reduce-scatter.1
where the time goes:
time: 1290 us; the launch traced here: 1280 us
  matrix products  532 us (41%)
  blocking collectives  237 us (18%)
  waiting for transfers between devices  199 us (15%)
  other arithmetic  178 us (14%)
  local copies, waits for them, and re-layouts  78.4 us (6%)
  loops' own time  27.3 us (2%)
  between operations  17.3 us (1%)
  starting transfers between devices  16.6 us (1%)
    dot_general x2, matrix products, attend_crop(): jnp.einsum('jhik,kjhd->ijhd', dscore_b, keys, preferred_element_type=jnp....  129 us
    dot_general x2, matrix products, attend_crop(): jnp.einsum('jhik,ijhd->kjhd', dscore_b, query, preferred_element_type=jnp...  128 us
    sub x2, other arithmetic, attend_crop(): dscores = probs32 * (dprobs - jnp.sum(probs32 * dprobs, -1, keepdims=True))  127 us
    all_gather x1, blocking collectives, body(): flat_weights = lax.all_gather(weights, 'row', axis=1, tiled=True)  113 us
    reduce_scatter x1, waiting for transfers between devices, body(): shard_w = lax.psum_scatter(dweights, 'row', scatter_dimension=1, tiled=True)  113 us
    all_to_all x1, blocking collectives, body(): lax.all_to_all(outs_col, 'row', split_axis=1, concat_axis=2, tiled=True)  93 us
    all_to_all x1, waiting for transfers between devices, body(): lax.all_to_all(pair, 'row', split_axis=2, concat_axis=1, tiled=True)  86.4 us
    sub x2, matrix products, attend_crop(): expo = jnp.exp(scores - peak)  75.6 us
  transfers between devices with their start and end apart: 4, of which 2 were waited for; matrix products, arithmetic and copies ran while one was open for 2% of the time, Pallas kernels for 0%

commit v1 on v0

v1 whole, which is shorter than its diff:
```python
import functools
import math

import jax
import jax.numpy as jnp
from jax import lax
from jax.experimental import pallas as pl
from jax.experimental.pallas import tpu as pltpu
from jax.sharding import PartitionSpec as P

STEP = 10
beta_one = 0.9
beta_two = 0.999
epsilon = 1e-06
decay = 0.01
rate = 0.25

BF = jnp.bfloat16
F32 = jnp.float32
MESH = pl.DeviceIdType.MESH
NT = ((1,), (1,))
TN = ((0,), (0,))
LOG2E = math.log2(math.e)
SEGS = 4


def dot(a, b, dims=((1,), (0,))):
    return lax.dot_general(a, b, (dims, ((), ())), preferred_element_type=F32)


def column(z, co, wallt, wkv, w4, wcat, gain, augk, augq, hot, e_ref, heads, tile):
    total, width = z.shape
    hsize = width // heads
    scale = 1.0 / math.sqrt(hsize)
    cob = co.astype(BF)
    mean = jnp.mean(z, -1, keepdims=True)
    cen = z - mean
    var = jnp.mean(cen * cen, -1, keepdims=True)
    inv = lax.rsqrt(var + 1e-05)
    xhat = cen * inv
    y = (xhat * gain).astype(BF)
    projT = dot(wallt, y, NT)
    kv = dot(y, wkv)
    k = kv[:, :width].astype(BF)
    v = kv[:, width:].astype(BF)
    qT = projT[:width].astype(BF)
    kT = projT[width : 2 * width].astype(BF)
    vT = projT[2 * width : 3 * width].astype(BF)
    gT = jax.nn.sigmoid(projT[3 * width :])
    head_of = lax.broadcasted_iota(jnp.int32, (width, 1), 0) // hsize
    kaug = jnp.concatenate([k, augk], 1)
    ones = jnp.ones((16, total), BF)
    heads_a, heads_r = [], []
    for h in range(heads):
        rows = slice(h * hsize, (h + 1) * hsize)
        qaug = jnp.concatenate([jnp.where(head_of == h, qT, jnp.zeros_like(qT)), augq[h]], 0)
        lhs = jnp.concatenate([vT[rows], ones], 0)
        tiles_a, tiles_r = [], []
        for t in range(0, total, tile):
            s = dot(kaug, qaug[:, t : t + tile]) * (scale * LOG2E)
            e = jnp.exp2(s - jnp.max(s, 0, keepdims=True)).astype(BF)
            e_ref[h, :, t : t + tile] = e
            a = dot(lhs, e)
            r = 1.0 / a[hsize : hsize + 1]
            tiles_a.append(a[:hsize] * r)
            tiles_r.append(r)
        heads_a.append(jnp.concatenate(tiles_a, 1))
        heads_r.append(jnp.broadcast_to(jnp.concatenate(tiles_r, 1), (hsize, total)))
    aT = jnp.concatenate(heads_a, 0)
    oT = (aT * gT).astype(BF)
    out = z + dot(oT, w4, TN)
    dw4 = dot(oT, cob)
    doT = dot(w4, cob, NT).astype(BF).astype(F32)
    daT = (doT * gT).astype(BF).astype(F32)
    dgT = (doT * aT * gT * (1.0 - gT)).astype(BF)
    dnT = (daT * jnp.concatenate(heads_r, 0) * scale).astype(BF)
    prod = aT * dnT.astype(F32)
    dq, dk, dv, db = [], [], [], []
    for h in range(heads):
        rows = slice(h * hsize, (h + 1) * hsize)
        shift = jnp.sum(prod[rows], 0, keepdims=True)
        masked = jnp.where(head_of == h, dnT, jnp.zeros_like(dnT))
        lhs = jnp.concatenate([kT[rows], hot], 0)
        tiles_q, dk_h, dv_h, db_h = [], 0.0, 0.0, 0.0
        for t in range(0, total, tile):
            part = slice(t, t + tile)
            e = e_ref[h, :, part]
            dp = dot(v, masked[:, part]) - shift[:, part]
            ds = (e.astype(F32) * dp).astype(BF)
            x = dot(lhs, ds)
            tiles_q.append(x[:hsize])
            db_h = db_h + x[hsize : hsize + 8] * hot[:8, part].astype(F32)
            dk_h = dk_h + dot(qT[rows, part], ds, NT)
            dv_h = dv_h + dot(dnT[rows, part], e, NT)
        dq.append(jnp.concatenate(tiles_q, 1).astype(BF))
        dk.append(dk_h.astype(BF))
        dv.append((dv_h * (1.0 / scale)).astype(BF))
        db.append(db_h)
    dprojT = jnp.concatenate(dq + dk + dv + [dgT], 0)
    dwt = dot(dprojT, y)
    dy = jnp.transpose(dot(wcat, dprojT))
    dgain = jnp.sum(dy * xhat, 0, keepdims=True)
    dx = dy * gain
    back = dx - jnp.mean(dx, -1, keepdims=True) - xhat * jnp.mean(dx * xhat, -1, keepdims=True)
    return out, co + inv * back, dwt, dw4, dgain, db


def moments(value, grad, first, second):
    first_new = beta_one * first + (1.0 - beta_one) * grad
    second_new = beta_two * second + (1.0 - beta_two) * grad * grad
    step_dir = (
        first_new
        / (1.0 - beta_one**STEP)
        / (jnp.sqrt(second_new / (1.0 - beta_two**STEP)) + epsilon)
        + decay * value
    )
    return (first_new, second_new, step_dir)


def main_kernel(
    dims,
    pair_t,
    cot_t,
    seg_ref,
    len_ref,
    w_ref,
    m1_ref,
    m2_ref,
    gain_ref,
    bias_ref,
    outc,
    gradc,
    red_ref,
    nrm_ref,
    zin,
    obuf,
    e_ref,
    wsend,
    wrecv,
    gsend,
    grecv,
    csend,
    crecv,
    nsend,
    nrecv,
    wallt_ref,
    wkv_ref,
    w4_ref,
    wcat_ref,
    augk_ref,
    augq_ref,
    hot_ref,
    dwt_acc,
    dw4_acc,
    dg_acc,
    db_acc,
    in_sem,
    send_sem,
    out_sem,
    osend_sem,
    misc_recv,
    misc_send,
    loc_sem,
):
    nrow, ncol, crops, cb, cpc, rl, width, heads, wr, tile = dims
    total = nrow * rl
    hsize = width // heads
    scale = 1.0 / math.sqrt(hsize)
    per_crop = cb // cpc
    chunks = crops * per_crop
    me = lax.axis_index("row")
    mc = lax.axis_index("col")

    def row_peer(d):
        return lax.rem(me + d, nrow)

    def col_peer(d):
        return lax.rem(mc + d, ncol)

    barrier = pltpu.get_barrier_semaphore()

    def greet_row(d, _):
        pl.semaphore_signal(barrier, inc=1, device_id=(row_peer(d), mc), device_id_type=MESH)
        return 0

    def greet_col(d, _):
        pl.semaphore_signal(barrier, inc=1, device_id=(me, col_peer(d)), device_id_type=MESH)
        return 0

    lax.fori_loop(1, nrow, greet_row, 0)
    lax.fori_loop(1, ncol, greet_col, 0)
    pl.semaphore_wait(barrier, nrow - 1 + ncol - 1)

    def exchange_row(src_of, dst, stage):
        def push(d, _):
            p = row_peer(d)
            pltpu.make_async_remote_copy(
                src_of(p),
                dst.at[me],
                misc_send.at[stage],
                misc_recv.at[stage],
                device_id=(p, mc),
                device_id_type=MESH,
            ).start()
            return 0

        lax.fori_loop(1, nrow, push, 0)
        pltpu.make_async_copy(src_of(me), dst.at[me], misc_recv.at[stage]).start()

    def exchange_wait(dst, stage):
        pltpu.make_async_copy(dst, dst, misc_recv.at[stage]).wait()

    for j in range(wr):
        wsend[j] = jnp.zeros((8, width), F32)
        wsend[j, 0:5, :] = w_ref[:, j * width : (j + 1) * width]
    exchange_row(lambda p: wsend, wrecv, 0)

    def push_chunk(i, _):
        c = i // per_crop
        j0 = lax.rem(i, per_crop) * cpc

        def push(d, _):
            p = row_peer(d)
            for a, src in enumerate((pair_t, cot_t)):
                pltpu.make_async_remote_copy(
                    src.at[c, p, pl.ds(j0, cpc)],
                    zin.at[i, a, :, me],
                    send_sem.at[a],
                    in_sem.at[i],
                    device_id=(p, mc),
                    device_id_type=MESH,
                ).start()
            return 0

        lax.fori_loop(1, nrow, push, 0)
        for a, src in enumerate((pair_t, cot_t)):
            pltpu.make_async_copy(
                src.at[c, me, pl.ds(j0, cpc)], zin.at[i, a, :, me], in_sem.at[i]
            ).start()
        return 0

    lax.fori_loop(0, chunks, push_chunk, 0)

    lane = lax.broadcasted_iota(jnp.int32, (1, total), 1)
    line = lax.broadcasted_iota(jnp.int32, (width, 1), 0)
    for c in range(crops):
        segs = seg_ref[c : c + 1, :]
        same = (lax.rem(line, SEGS) == segs).astype(F32)
        hot_ref[c] = jnp.where(line[:16] < SEGS, same[:16], 0.0).astype(BF)
        pad = jnp.where(lane >= len_ref[c], -1e30, 0.0)
        rowsk = jnp.where(line < 3 * SEGS, same, jnp.where(line == 3 * SEGS, pad, 0.0))
        augk_ref[c] = jnp.transpose(rowsk).astype(BF)
        for h in range(heads):
            full = jnp.full((width, 1), bias_ref[h] * (1.0 / scale), F32)
            high = full.astype(BF).astype(F32)
            mid = (full - high).astype(BF).astype(F32)
            low = full - high - mid
            part = jnp.where(line < SEGS, high, jnp.where(line < 2 * SEGS, mid, low))
            rowsq = jnp.where(line < 3 * SEGS, same * part, jnp.where(line == 3 * SEGS, 1.0, 0.0))
            augq_ref[c, h] = rowsq.astype(BF)

    dwt_acc[...] = jnp.zeros_like(dwt_acc)
    dw4_acc[...] = jnp.zeros_like(dw4_acc)
    dg_acc[...] = jnp.zeros_like(dg_acc)
    db_acc[...] = jnp.zeros_like(db_acc)

    exchange_wait(wrecv, 0)
    for kk in range(5):
        w = wrecv[:, :, kk, :].reshape(width, width)
        wb = w.astype(BF)
        if kk < 4:
            wallt_ref[kk * width : (kk + 1) * width, :] = jnp.transpose(w).astype(BF)
            wcat_ref[:, kk * width : (kk + 1) * width] = wb
        if kk in (1, 2):
            wkv_ref[:, (kk - 1) * width : kk * width] = wb
        if kk == 4:
            w4_ref[...] = wb

    def work(i, _):
        c = i // per_crop
        j0 = lax.rem(i, per_crop) * cpc
        pltpu.make_async_copy(zin.at[i], zin.at[i], in_sem.at[i]).wait()

        def one(j, _):
            z = zin[i, 0, j].astype(F32).reshape(total, width)
            co = zin[i, 1, j].astype(F32).reshape(total, width)
            out, grad, dwt, dw4, dgain, db = column(
                z,
                co,
                wallt_ref[...],
                wkv_ref[...],
                w4_ref[...],
                wcat_ref[...],
                gain_ref[...],
                augk_ref[c],
                [augq_ref[c, h] for h in range(heads)],
                hot_ref[c],
                e_ref,
                heads,
                tile,
            )
            obuf[i, 0, j] = out.reshape(nrow, rl, width).astype(BF)
            obuf[i, 1, j] = grad.reshape(nrow, rl, width).astype(BF)
            dwt_acc[...] += dwt
            dw4_acc[...] += dw4
            dg_acc[0:1] += dgain
            for h in range(heads):
                db_acc[h] += db[h]
            return 0

        lax.fori_loop(0, cpc, one, 0)

        def push(d, _):
            p = row_peer(d)
            for a, dst in enumerate((outc, gradc)):
                pltpu.make_async_remote_copy(
                    obuf.at[i, a, :, p],
                    dst.at[c, me, pl.ds(j0, cpc)],
                    osend_sem.at[a],
                    out_sem.at[a],
                    device_id=(p, mc),
                    device_id_type=MESH,
                ).start()
            return 0

        lax.fori_loop(1, nrow, push, 0)
        for a, dst in enumerate((outc, gradc)):
            pltpu.make_async_copy(
                obuf.at[i, a, :, me], dst.at[c, me, pl.ds(j0, cpc)], out_sem.at[a]
            ).start()
        return 0

    lax.fori_loop(0, chunks, work, 0)

    for kk in range(4):
        gsend[:, kk, :] = jnp.transpose(dwt_acc[kk * width : (kk + 1) * width, :])
    gsend[:, 4, :] = dw4_acc[...]
    gsend[:, 5, :] = jnp.broadcast_to(dg_acc[0:1], (width, width))
    spot = lax.broadcasted_iota(jnp.int32, (1, width), 1)
    dbias = jnp.zeros((1, width), F32)
    for h in range(heads):
        one_h = jnp.sum(jnp.sum(db_acc[h], 0, keepdims=True), 1, keepdims=True) * (1.0 / scale)
        dbias = jnp.where(spot == h, one_h, dbias)
    gsend[:, 6, :] = jnp.broadcast_to(dbias, (width, width))
    gsend[:, 7, :] = jnp.zeros((width, width), F32)
    exchange_row(lambda p: gsend.at[pl.ds(p * wr, wr)], grecv, 1)
    exchange_wait(grecv, 1)
    csend[...] = lax.fori_loop(1, nrow, lambda r, s: s + grecv[r], grecv[0])

    def push_col(d, _):
        pltpu.make_async_remote_copy(
            csend,
            crecv.at[mc],
            misc_send.at[2],
            misc_recv.at[2],
            device_id=(me, col_peer(d)),
            device_id_type=MESH,
        ).start()
        return 0

    lax.fori_loop(1, ncol, push_col, 0)
    pltpu.make_async_copy(csend, crecv.at[mc], misc_recv.at[2]).start()
    exchange_wait(crecv, 2)
    grads = lax.fori_loop(1, ncol, lambda r, s: s + crecv[r], crecv[0])
    red = jnp.concatenate([grads[j] for j in range(wr)], 1)
    red_ref[...] = red
    wval = w_ref[...]
    step_w = moments(wval, red[0:5], m1_ref[...], m2_ref[...])[2]
    nsend[...] = jnp.zeros_like(nsend)
    nsend[0:5, :] = jnp.where(
        spot == 0,
        jnp.sum(wval * wval, 1, keepdims=True),
        jnp.where(spot == 1, jnp.sum(step_w * step_w, 1, keepdims=True), 0.0),
    )
    exchange_row(lambda p: nsend, nrecv, 3)
    exchange_wait(nrecv, 3)
    nrm_ref[...] = lax.fori_loop(1, nrow, lambda r, s: s + nrecv[r], nrecv[0])

    for a, (src, dst) in enumerate(((pair_t, outc), (cot_t, gradc))):
        sent = src.at[:, pl.ds(0, nrow - 1)]
        pltpu.make_async_copy(sent, sent, send_sem.at[a]).wait()
        gone = dst.at[:, pl.ds(0, nrow - 1)]
        pltpu.make_async_copy(gone, gone, osend_sem.at[a]).wait()
        pltpu.make_async_copy(dst, dst, out_sem.at[a]).wait()
    for stage, dst in ((0, wrecv), (1, grecv), (3, nrecv)):
        sent = dst.at[pl.ds(0, nrow - 1)]
        pltpu.make_async_copy(sent, sent, misc_send.at[stage]).wait()
    sent = crecv.at[pl.ds(0, ncol - 1)]
    pltpu.make_async_copy(sent, sent, misc_send.at[2]).wait()


def step_kernel(
    red_ref,
    nrm_ref,
    w_ref,
    m1_ref,
    m2_ref,
    gain_ref,
    gm_ref,
    gv_ref,
    bias_ref,
    bm_ref,
    bv_ref,
    nw_ref,
    n1_ref,
    n2_ref,
    ng_ref,
    ngm_ref,
    ngv_ref,
    nb_ref,
    nbm_ref,
    nbv_ref,
):
    width = gain_ref.shape[1]
    heads = bias_ref.shape[1]
    wval = w_ref[...]
    first, second, step_w = moments(wval, red_ref[0:5], m1_ref[...], m2_ref[...])
    ratio = jnp.sqrt(nrm_ref[0:5, 0:1]) / jnp.sqrt(nrm_ref[0:5, 1:2])
    nw_ref[...] = wval - rate * ratio * step_w
    n1_ref[...] = first
    n2_ref[...] = second
    for row, n, refs in (
        (5, width, (gain_ref, gm_ref, gv_ref, ng_ref, ngm_ref, ngv_ref)),
        (6, heads, (bias_ref, bm_ref, bv_ref, nb_ref, nbm_ref, nbv_ref)),
    ):
        val = refs[0][...]
        first, second, step_v = moments(val, red_ref[row : row + 1, 0:n], refs[1][...], refs[2][...])
        ratio = jnp.sqrt(jnp.sum(val * val, 1, keepdims=True)) / jnp.sqrt(
            jnp.sum(step_v * step_v, 1, keepdims=True)
        )
        refs[3][...] = val - rate * ratio * step_v
        refs[4][...] = first
        refs[5][...] = second


def body(
    nrow,
    ncol,
    pair,
    cotangent,
    segments,
    lengths,
    weights,
    moment_one,
    moment_two,
    gain,
    gain_m,
    gain_v,
    chain_bias,
    bias_m,
    bias_v,
):
    crops, rl, cl, width = pair.shape
    heads = chain_bias.shape[0]
    cb = cl // nrow
    cpc = min(2, cb)
    wr = weights.shape[1] // width
    total = nrow * rl
    tile = min(256, total)
    chunks = crops * (cb // cpc)
    dims = (nrow, ncol, crops, cb, cpc, rl, width, heads, wr, tile)
    pair_t = jnp.swapaxes(pair, 1, 2).reshape(crops, nrow, cb, rl, width)
    cot_t = jnp.swapaxes(cotangent, 1, 2).reshape(crops, nrow, cb, rl, width)
    hbm = pl.BlockSpec(memory_space=pl.ANY)
    vmem = pl.BlockSpec(memory_space=pltpu.VMEM)
    smem = pl.BlockSpec(memory_space=pltpu.SMEM)
    dma = pltpu.SemaphoreType.DMA
    outc, gradc, red, nrm = pl.pallas_call(
        functools.partial(main_kernel, dims),
        out_shape=(
            jax.ShapeDtypeStruct((crops, nrow, cb, rl, width), BF),
            jax.ShapeDtypeStruct((crops, nrow, cb, rl, width), BF),
            jax.ShapeDtypeStruct((8, wr * width), F32),
            jax.ShapeDtypeStruct((8, width), F32),
        ),
        in_specs=[hbm, hbm, vmem, smem, vmem, vmem, vmem, vmem, smem],
        out_specs=(hbm, hbm, vmem, vmem),
        scratch_shapes=[
            pltpu.VMEM((chunks, 2, cpc, nrow, rl, width), BF),
            pltpu.VMEM((chunks, 2, cpc, nrow, rl, width), BF),
            pltpu.VMEM((heads, total, total), BF),
            pltpu.VMEM((wr, 8, width), F32),
            pltpu.VMEM((nrow, wr, 8, width), F32),
            pltpu.VMEM((nrow * wr, 8, width), F32),
            pltpu.VMEM((nrow, wr, 8, width), F32),
            pltpu.VMEM((wr, 8, width), F32),
            pltpu.VMEM((ncol, wr, 8, width), F32),
            pltpu.VMEM((8, width), F32),
            pltpu.VMEM((nrow, 8, width), F32),
            pltpu.VMEM((4 * width, width), BF),
            pltpu.VMEM((width, 2 * width), BF),
            pltpu.VMEM((width, width), BF),
            pltpu.VMEM((width, 4 * width), BF),
            pltpu.VMEM((crops, total, width), BF),
            pltpu.VMEM((crops, heads, width, total), BF),
            pltpu.VMEM((crops, 16, total), BF),
            pltpu.VMEM((4 * width, width), F32),
            pltpu.VMEM((width, width), F32),
            pltpu.VMEM((8, width), F32),
            pltpu.VMEM((heads, 8, tile), F32),
            dma((chunks,)),
            dma((2,)),
            dma((2,)),
            dma((2,)),
            dma((4,)),
            dma((4,)),
            dma((1,)),
        ],
        compiler_params=pltpu.CompilerParams(
            collective_id=0, has_side_effects=True, vmem_limit_bytes=56 << 20
        ),
        name="column_attention",
    )(
        pair_t,
        cot_t,
        segments,
        lengths,
        weights,
        moment_one,
        moment_two,
        gain.reshape(1, width),
        chain_bias,
    )
    pair_out = jnp.swapaxes(outc.reshape(crops, cl, rl, width), 1, 2)
    pair_grad = jnp.swapaxes(gradc.reshape(crops, cl, rl, width), 1, 2)
    small = (gain, gain_m, gain_v, chain_bias, bias_m, bias_v)
    ops = [red, nrm, weights, moment_one, moment_two] + [a.reshape(1, -1) for a in small]
    res = pl.pallas_call(
        step_kernel,
        out_shape=[jax.ShapeDtypeStruct(weights.shape, F32)] * 3
        + [jax.ShapeDtypeStruct((1, width), F32)] * 3
        + [jax.ShapeDtypeStruct((1, heads), F32)] * 3,
        in_specs=[vmem] * len(ops),
        out_specs=[vmem] * 9,
        name="lamb_step",
    )(*ops)
    return (pair_out, pair_grad, *res[:3], *[a.reshape(-1) for a in res[3:]])


def solution(mesh):
    big = P(None, "row", "col", None)
    shard = P(None, "row")
    return jax.shard_map(
        functools.partial(body, mesh.shape["row"], mesh.shape["col"]),
        mesh=mesh,
        in_specs=(big, big, P(), P(), shard, shard, shard) + (P(),) * 6,
        out_specs=(big, big, shard, shard, shard) + (P(),) * 6,
        check_vma=False,
    )
```

time: 1290 us -> 426 us (0.33)
  matrix products: 532 us -> 0 us
  Pallas kernels: 0 us -> 402 us
  blocking collectives: 237 us -> 0 us
  waiting for transfers between devices: 199 us -> 0 us
  other arithmetic: 178 us -> 0 us
  local copies, waits for them, and re-layouts: 78.4 us -> 22.8 us
  loops' own time: 27.3 us -> 0 us
  starting transfers between devices: 16.6 us -> 0 us
  between operations: 17.3 us -> 0.82 us
    dot_general x22 -> x0, matrix products: 456 us -> none  [the longest x2 129 us: attend_crop(): jnp.einsum('jhik,kjhd->ijhd', dscore_b, keys, preferred_element_type=jnp....]
    pallas_call x0 -> x2, Pallas kernels: none -> 402 us  [the longest x1 400 us: body(): pl.pallas_call(functools.partial(main_kernel, dims), out_shape=(jax.Shape...]
    sub x5 -> x0, other arithmetic: 129 us -> none  [the longest x2 127 us: attend_crop(): dscores = probs32 * (dprobs - jnp.sum(probs32 * dprobs, -1, keepdims=True))]
    all_gather x1 -> x0, blocking collectives: 113 us -> none  [body(): flat_weights = lax.all_gather(weights, 'row', axis=1, tiled=True)]
    reduce_scatter x1 -> x0, waiting for transfers between devices: 113 us -> none  [body(): shard_w = lax.psum_scatter(dweights, 'row', scatter_dimension=1, tiled=True)]
    all_to_all x1 -> x0, blocking collectives: 93 us -> none  [body(): lax.all_to_all(outs_col, 'row', split_axis=1, concat_axis=2, tiled=True)]
    all_to_all x3 -> x0, waiting for transfers between devices: 86.4 us -> none  [the longest x1 86.4 us: body(): lax.all_to_all(pair, 'row', split_axis=2, concat_axis=1, tiled=True)]
    sub x2 -> x0, matrix products: 75.6 us -> none  [attend_crop(): expo = jnp.exp(scores - peak)]
  transfers between devices with their start and end apart: 4 -> 0, of which waited for: 2 -> 0; matrix products, arithmetic and copies ran while one was open for 2% -> 0% of each run, Pallas kernels for 0% -> 0%
where the time goes in v1:
time: 426 us
  Pallas kernels  402 us (94%)
  local copies, waits for them, and re-layouts  22.8 us (5%)
    pallas_call x1, Pallas kernels, body(): pl.pallas_call(functools.partial(main_kernel, dims), out_shape=(jax.Shape...  400 us
    transpose x1, local copies, waits for them, and re-layouts, body(): pair_grad = jnp.swapaxes(gradc.reshape(crops, cl, rl, width), 1, 2)  11 us

profile of v1, /device:TPU:0, one launch (start us, length us, event | category | flops | bytes accessed | tf_op | source)
XLA Modules:
  0.0 425.6 jit_solution(15694897292935157551)
XLA Ops:
  0.6 0.0 copy-start
  0.7 7.1 %copy.24 = bf16[2,128,64,128]{3,2,1,0:T(8,128)(2,1)} copy(bf16[2,128,64,128]{3,1,2,0:T(8,128)(2,1)} %bitcast.24) | data formatting | bytes 8388608 | tf_op jit(solution)/shard_map/transpose | solution.py:462
  7.7 0.0 copy-done
  7.7 4.7 %copy.25 = bf16[2,128,64,128]{3,2,1,0:T(8,128)(2,1)} copy(bf16[2,128,64,128]{3,1,2,0:T(8,128)(2,1)S(1)} %bitcast.25) | data formatting | bytes 8388608 | tf_op jit(solution)/shard_map/transpose | solution.py:463
  12.4 400.2 %column_attention.1 = (bf16[2,8,16,64,128]{4,3,2,1,0:T(8,128)(2,1)}, bf16[2,8,16,64,128]{4,3,2,1,0:T(8,128)(2,1)}, f32[8,2048]{1,0:T(8,128)}, f32[8,128]{1,0:T(8,128)}) custom-call(bf16[2,8,16,64,128]{4,3,2,1,0:T(8,128)(2,1)} %bitcast.22, bf16[2,8,16,64,128]{4,3,2,1,0:T(8,128)(2,1)} %bitcast.23, s32[2,512]{1,0:T(2,128)} %seg_ref.1, s32[2]{0:T(128)} %len_ref.1, ...), custom_call_target="tpu_custom_call" | custom-call | tf_op jit(solution)/shard_map/column_attention/pallas_call | solution.py:468
  412.6 11.0 %copy_bitcast_fusion = (bf16[2,64,128,128]{3,2,1,0:T(8,128)(2,1)}, bf16[2,64,128,128]{3,2,1,0:T(8,128)(2,1)}) fusion(bf16[2,128,64,128]{3,2,1,0:T(8,128)(2,1)} %bitcast.27, bf16[2,128,64,128]{3,2,1,0:T(8,128)(2,1)} %bitcast.26), kind=kLoop, calls=%fused_computation | loop fusion | bytes 16777216 | tf_op jit(solution)/shard_map/transpose | solution.py:525
  423.6 1.8 lamb_step.1
Async XLA Ops:
  0.6 7.1 %copy-start = (bf16[2,64,128,128]{3,2,1,0:T(8,128)(2,1)S(1)}, bf16[2,64,128,128]{3,2,1,0:T(8,128)(2,1)}, u32[]{:S(2)}) copy-start(bf16[2,64,128,128]{3,2,1,0:T(8,128)(2,1)} %param.14) | copy-start | bytes 12582916

commit v2 on v1

v2 whole, which is shorter than its diff:
```python
import functools
import math

import jax
import jax.numpy as jnp
from jax import lax
from jax.experimental import pallas as pl
from jax.experimental.pallas import tpu as pltpu
from jax.sharding import PartitionSpec as P

STEP = 10
beta_one = 0.9
beta_two = 0.999
epsilon = 1e-06
decay = 0.01
rate = 0.25

BF = jnp.bfloat16
F32 = jnp.float32
MESH = pl.DeviceIdType.MESH
NT = ((1,), (1,))
TN = ((0,), (0,))
LOG2E = math.log2(math.e)
SEGS = 4


def dot(a, b, dims=((1,), (0,))):
    return lax.dot_general(a, b, (dims, ((), ())), preferred_element_type=F32)


def column(z, co, wallt, wkv, w4, wcat, gain, augk, augq, hot, e_ref, heads, tile):
    total, width = z.shape
    hsize = width // heads
    scale = 1.0 / math.sqrt(hsize)
    cob = co.astype(BF)
    mean = jnp.mean(z, -1, keepdims=True)
    cen = z - mean
    var = jnp.mean(cen * cen, -1, keepdims=True)
    inv = lax.rsqrt(var + 1e-05)
    xhat = cen * inv
    y = (xhat * gain).astype(BF)
    projT = dot(wallt, y, NT)
    kv = dot(y, wkv)
    k = kv[:, :width].astype(BF)
    v = kv[:, width:].astype(BF)
    qT = projT[:width].astype(BF)
    kT = projT[width : 2 * width].astype(BF)
    vT = projT[2 * width : 3 * width].astype(BF)
    gT = jax.nn.sigmoid(projT[3 * width :])
    head_of = lax.broadcasted_iota(jnp.int32, (width, 1), 0) // hsize
    kaug = jnp.concatenate([k, augk], 1)
    ones = jnp.ones((16, total), BF)
    heads_a, heads_r = [], []
    for h in range(heads):
        rows = slice(h * hsize, (h + 1) * hsize)
        qaug = jnp.concatenate([jnp.where(head_of == h, qT, jnp.zeros_like(qT)), augq[h]], 0)
        lhs = jnp.concatenate([vT[rows], ones], 0)
        tiles_a, tiles_r = [], []
        for t in range(0, total, tile):
            s = dot(kaug, qaug[:, t : t + tile]) * (scale * LOG2E)
            e = jnp.exp2(s - jnp.max(s, 0, keepdims=True)).astype(BF)
            e_ref[h, :, t : t + tile] = e
            a = dot(lhs, e)
            r = 1.0 / a[hsize : hsize + 1]
            tiles_a.append(a[:hsize] * r)
            tiles_r.append(r)
        heads_a.append(jnp.concatenate(tiles_a, 1))
        heads_r.append(jnp.broadcast_to(jnp.concatenate(tiles_r, 1), (hsize, total)))
    aT = jnp.concatenate(heads_a, 0)
    oT = (aT * gT).astype(BF)
    out = z + dot(oT, w4, TN)
    dw4 = dot(oT, cob)
    doT = dot(w4, cob, NT).astype(BF).astype(F32)
    daT = (doT * gT).astype(BF).astype(F32)
    dgT = (doT * aT * gT * (1.0 - gT)).astype(BF)
    dnT = (daT * jnp.concatenate(heads_r, 0) * scale).astype(BF)
    prod = aT * dnT.astype(F32)
    dq, dk, dv, db = [], [], [], []
    for h in range(heads):
        rows = slice(h * hsize, (h + 1) * hsize)
        shift = jnp.sum(prod[rows], 0, keepdims=True)
        masked = jnp.where(head_of == h, dnT, jnp.zeros_like(dnT))
        lhs = jnp.concatenate([kT[rows], hot], 0)
        tiles_q, dk_h, dv_h, db_h = [], 0.0, 0.0, 0.0
        for t in range(0, total, tile):
            part = slice(t, t + tile)
            e = e_ref[h, :, part]
            dp = dot(v, masked[:, part]) - shift[:, part]
            ds = (e.astype(F32) * dp).astype(BF)
            x = dot(lhs, ds)
            tiles_q.append(x[:hsize])
            db_h = db_h + x[hsize : hsize + 8] * hot[:8, part].astype(F32)
            dk_h = dk_h + dot(qT[rows, part], ds, NT)
            dv_h = dv_h + dot(dnT[rows, part], e, NT)
        dq.append(jnp.concatenate(tiles_q, 1).astype(BF))
        dk.append(dk_h.astype(BF))
        dv.append((dv_h * (1.0 / scale)).astype(BF))
        db.append(db_h)
    dprojT = jnp.concatenate(dq + dk + dv + [dgT], 0)
    dwt = dot(dprojT, y)
    dy = jnp.transpose(dot(wcat, dprojT))
    dgain = jnp.sum(dy * xhat, 0, keepdims=True)
    dx = dy * gain
    back = dx - jnp.mean(dx, -1, keepdims=True) - xhat * jnp.mean(dx * xhat, -1, keepdims=True)
    return out, co + inv * back, dwt, dw4, dgain, db


def moments(value, grad, first, second):
    first_new = beta_one * first + (1.0 - beta_one) * grad
    second_new = beta_two * second + (1.0 - beta_two) * grad * grad
    step_dir = (
        first_new
        / (1.0 - beta_one**STEP)
        / (jnp.sqrt(second_new / (1.0 - beta_two**STEP)) + epsilon)
        + decay * value
    )
    return (first_new, second_new, step_dir)


def main_kernel(dims, names, *refs):
    nrow, ncol, crops, cb, rl, width, heads, wr, tile, direct = dims
    pair_ref, cot_ref, seg_ref, len_ref, w_ref, m1_ref, m2_ref, gain_ref, bias_ref = refs[:9]
    fins, red_ref, nrm_ref = refs[9:11], refs[11], refs[12]
    s = dict(zip(names, refs[13:]))
    zin, obuf = s["zin"], s["obuf"]
    in_sem, send_sem, out_sem, osend_sem = s["in_sem"], s["send_sem"], s["out_sem"], s["osend_sem"]
    misc_recv, misc_send = s["misc_recv"], s["misc_send"]
    if direct:
        stage, sbuf, raw_sem = s["stage"], s["sbuf"], s["raw_sem"]
    srcs = (pair_ref, cot_ref)
    total = nrow * rl
    hsize = width // heads
    scale = 1.0 / math.sqrt(hsize)
    slots = s["wrow"].shape[1]
    me = lax.axis_index("row")
    mc = lax.axis_index("col")

    def row_peer(d):
        return lax.rem(me + d, nrow)

    def col_peer(d):
        return lax.rem(mc + d, ncol)

    def cols_of(p):
        return pl.ds(pl.multiple_of(p * cb, cb), cb)

    if direct:
        def load(n, _):
            c, p = n // nrow, row_peer(lax.rem(n + 1, nrow))
            for a in range(2):
                pltpu.make_async_copy(
                    srcs[a].at[c, :, cols_of(p), :], obuf.at[c, a, p], raw_sem.at[c, a, p]
                ).start()
            return 0

        lax.fori_loop(0, crops * nrow, load, 0)

    barrier = pltpu.get_barrier_semaphore()

    def greet_row(d, _):
        pl.semaphore_signal(barrier, inc=1, device_id=(row_peer(d), mc), device_id_type=MESH)
        return 0

    def greet_col(d, _):
        pl.semaphore_signal(barrier, inc=1, device_id=(me, col_peer(d)), device_id_type=MESH)
        return 0

    lax.fori_loop(1, nrow, greet_row, 0)
    lax.fori_loop(1, ncol, greet_col, 0)
    pl.semaphore_wait(barrier, nrow - 1 + ncol - 1)

    def remote(src, dst, send, recv, peer):
        pltpu.make_async_remote_copy(
            src, dst, send, recv, device_id=peer, device_id_type=MESH
        ).start()

    def exchange_row(src_of, dst, n):
        def push(d, _):
            p = row_peer(d)
            remote(src_of(p), dst.at[me], misc_send.at[n], misc_recv.at[n], (p, mc))
            return 0

        lax.fori_loop(1, nrow, push, 0)
        pltpu.make_async_copy(src_of(me), dst.at[me], misc_recv.at[n]).start()

    def exchange_col(src_of, dst, n):
        def push(d, _):
            p = col_peer(d)
            remote(src_of(p), dst.at[mc], misc_send.at[n], misc_recv.at[n], (me, p))
            return 0

        lax.fori_loop(1, ncol, push, 0)
        pltpu.make_async_copy(src_of(mc), dst.at[mc], misc_recv.at[n]).start()

    def landed(dst, n):
        pltpu.make_async_copy(dst, dst, misc_recv.at[n]).wait()

    def total_of(ref, n):
        return lax.fori_loop(1, n, lambda r, s: s + ref[r], ref[0])

    for j in range(wr):
        s["wtmp"][0:5, j, :] = w_ref[:, j * width : (j + 1) * width]
    for k in range(slots * ncol):
        s["wsend"][k] = (s["wtmp"][k] if k < 5 else jnp.zeros((wr, width), F32)).astype(s["wsend"].dtype)
    exchange_row(lambda p: s["wsend"].at[pl.ds(mc * slots, slots)], s["wrow"], 0)

    def push_column(c, j, d):
        p = row_peer(d)
        i = c * cb + j
        for a in range(2):
            src = sbuf.at[c, a, j, p] if direct else srcs[a].at[c, p, j]
            remote(src, zin.at[i, a, me], send_sem.at[a], in_sem.at[i], (p, mc))

    def keep_column(c, j):
        i = c * cb + j
        for a in range(2):
            src = sbuf.at[c, a, j, me] if direct else srcs[a].at[c, me, j]
            pltpu.make_async_copy(src, zin.at[i, a, me], in_sem.at[i]).start()

    def push_columns(c, first):
        def at_column(j, _):
            def to_peer(d, _):
                push_column(c, j, d)
                return 0

            lax.fori_loop(1, nrow, to_peer, 0)
            keep_column(c, j)
            return 0

        lax.fori_loop(first, cb, at_column, 0)

    def turn(c, d):
        p = row_peer(d)
        for a in range(2):
            here = obuf.at[c, a, p]
            pltpu.make_async_copy(here, here, raw_sem.at[c, a, p]).wait()
            stage[a] = obuf[c, a, p].astype(F32).reshape(rl * cb, width)
            for j in range(cb):
                sbuf[c, a, j, p] = stage[a, pl.ds(j, rl, stride=cb), :].astype(BF)

    if direct:

        def first_blocks(d, _):
            turn(0, d)
            push_column(0, 0, d)
            return 0

        lax.fori_loop(1, nrow, first_blocks, 0)
        turn(0, 0)
        keep_column(0, 0)
        push_columns(0, 1)
    else:
        for c in range(crops):
            push_columns(c, 0)

    landed(s["wrow"], 0)
    exchange_col(lambda p: s["wrow"], s["wall"], 1)

    if direct:

        def later_blocks(d, _):
            for c in range(1, crops):
                turn(c, d)
            return 0

        lax.fori_loop(0, nrow, later_blocks, 0)
        for c in range(1, crops):
            push_columns(c, 0)

    lane = lax.broadcasted_iota(jnp.int32, (1, total), 1)
    line = lax.broadcasted_iota(jnp.int32, (width, 1), 0)
    for c in range(crops):
        segs = seg_ref[c : c + 1, :]
        same = (lax.rem(line, SEGS) == segs).astype(F32)
        s["hot"][c] = jnp.where(line[:16] < SEGS, same[:16], 0.0).astype(BF)
        pad = jnp.where(lane >= len_ref[c], -1e30, 0.0)
        rowsk = jnp.where(line < 3 * SEGS, same, jnp.where(line == 3 * SEGS, pad, 0.0))
        s["augk"][c] = jnp.transpose(rowsk).astype(BF)
        for h in range(heads):
            full = jnp.full((width, 1), bias_ref[h] * (1.0 / scale), F32)
            high = full.astype(BF).astype(F32)
            mid = (full - high).astype(BF).astype(F32)
            low = full - high - mid
            part = jnp.where(line < SEGS, high, jnp.where(line < 2 * SEGS, mid, low))
            rowsq = jnp.where(line < 3 * SEGS, same * part, jnp.where(line == 3 * SEGS, 1.0, 0.0))
            s["augq"][c, h] = rowsq.astype(BF)

    s["dwt_acc"][...] = jnp.zeros_like(s["dwt_acc"])
    s["dw4_acc"][...] = jnp.zeros_like(s["dw4_acc"])
    s["dg_acc"][...] = jnp.zeros_like(s["dg_acc"])
    s["db_acc"][...] = jnp.zeros_like(s["db_acc"])

    landed(s["wall"], 1)
    for k in range(5):
        wb = s["wall"][k // slots, :, k % slots].astype(F32).reshape(width, width)
        if k < 4:
            s["wallt"][k * width : (k + 1) * width, :] = jnp.transpose(wb).astype(BF)
            s["wcat"][:, k * width : (k + 1) * width] = wb.astype(BF)
        if k in (1, 2):
            s["wkv"][:, (k - 1) * width : k * width] = wb.astype(BF)
        if k == 4:
            s["w4"][...] = wb.astype(BF)

    def work(c, j):
        i = c * cb + j
        pltpu.make_async_copy(zin.at[i], zin.at[i], in_sem.at[i]).wait()
        out, grad, dwt, dw4, dgain, db = column(
            zin[i, 0].astype(F32).reshape(total, width),
            zin[i, 1].astype(F32).reshape(total, width),
            s["wallt"][...],
            s["wkv"][...],
            s["w4"][...],
            s["wcat"][...],
            gain_ref[...],
            s["augk"][c],
            [s["augq"][c, h] for h in range(heads)],
            s["hot"][c],
            s["prob"],
            heads,
            tile,
        )
        s["dwt_acc"][...] += dwt
        s["dw4_acc"][...] += dw4
        s["dg_acc"][0:1] += dgain
        for h in range(heads):
            s["db_acc"][h] += db[h]
        if direct:
            zin[i, 0] = out.reshape(nrow, rl, width).astype(BF)
            zin[i, 1] = grad.reshape(nrow, rl, width).astype(BF)
        else:
            obuf[i, 0] = out.reshape(nrow, rl, width).astype(BF)
            obuf[i, 1] = grad.reshape(nrow, rl, width).astype(BF)

            def push(d, _):
                p = row_peer(d)
                for a in range(2):
                    remote(
                        obuf.at[i, a, p], fins[a].at[c, me, j], osend_sem.at[a], out_sem.at[a], (p, mc)
                    )
                return 0

            lax.fori_loop(1, nrow, push, 0)
            for a in range(2):
                pltpu.make_async_copy(obuf.at[i, a, me], fins[a].at[c, me, j], out_sem.at[a]).start()

    def work_crop(c, _):
        def work_column(j, _):
            work(c, j)
            return 0

        lax.fori_loop(0, cb, work_column, 0)
        return 0

    def give_back(c, a, first, last):
        here = fins[a].at[c, :, cols_of(me), :]

        def give(d, _):
            p = row_peer(d)
            for j in range(cb):
                stage[a, pl.ds(j, rl, stride=cb), :] = zin[c * cb + j, a, p].astype(F32)
            obuf[c, a, p] = stage[a].reshape(rl, cb, width).astype(BF)

            @pl.when(d > 0)
            def _():
                remote(obuf.at[c, a, p], here, osend_sem.at[a], out_sem.at[a], (p, mc))

            @pl.when(d == 0)
            def _():
                pltpu.make_async_copy(obuf.at[c, a, p], here, out_sem.at[a]).start()

            return 0

        lax.fori_loop(first, last, give, 0)

    if direct:

        def most(c, _):
            work_crop(c, 0)
            give_back(c, 0, 0, nrow)
            give_back(c, 1, 0, nrow)
            return 0

        lax.fori_loop(0, crops - 1, most, 0)
        work_crop(crops - 1, 0)
    else:
        lax.fori_loop(0, crops, work_crop, 0)

    gsend = s["gsend"]
    for k in range(4):
        gsend[k] = jnp.transpose(s["dwt_acc"][k * width : (k + 1) * width, :])
    gsend[4] = s["dw4_acc"][...]
    gsend[5] = jnp.broadcast_to(s["dg_acc"][0:1], (width, width))
    spot = lax.broadcasted_iota(jnp.int32, (1, width), 1)
    dbias = jnp.zeros((1, width), F32)
    for h in range(heads):
        total_h = jnp.sum(jnp.sum(s["db_acc"][h], 0, keepdims=True), 1, keepdims=True)
        dbias = jnp.where(spot == h, total_h * (1.0 / scale), dbias)
    gsend[6] = jnp.broadcast_to(dbias, (width, width))
    for k in range(7, slots * ncol):
        gsend[k] = jnp.zeros((width, width), F32)
    exchange_col(lambda p: gsend.at[pl.ds(p * slots, slots)], s["grecv"], 2)
    if direct:
        give_back(crops - 1, 0, 0, nrow)
    landed(s["grecv"], 2)
    share = total_of(s["grecv"], ncol)
    for p in range(nrow):
        s["ssend"][p] = share[:, p * wr : (p + 1) * wr, :]
    exchange_row(lambda p: s["ssend"].at[p], s["srecv"], 3)
    if direct:
        give_back(crops - 1, 1, 0, nrow)
    landed(s["srecv"], 3)
    s["csend"][...] = total_of(s["srecv"], nrow)
    exchange_col(lambda p: s["csend"], s["crecv"], 4)
    landed(s["crecv"], 4)
    for j in range(wr):
        red_ref[:, j * width : (j + 1) * width] = s["crecv"][:, :, j, :].reshape(slots * ncol, width)
    wval = w_ref[...]
    step_w = moments(wval, red_ref[0:5, :], m1_ref[...], m2_ref[...])[2]
    place = lax.broadcasted_iota(jnp.int32, (5, 1), 0)
    squares = jnp.where(spot == place, jnp.sum(wval * wval, 1, keepdims=True), 0.0)
    squares += jnp.where(spot == place + 8, jnp.sum(step_w * step_w, 1, keepdims=True), 0.0)
    s["nsend"][...] = jnp.sum(squares, 0, keepdims=True)
    exchange_row(lambda p: s["nsend"], s["nrecv"], 5)
    landed(s["nrecv"], 5)
    nrm_ref[...] = total_of(s["nrecv"], nrow)

    most_rows = pl.ds(0, nrow - 1)
    for a in range(2):
        sent = sbuf.at[:, a, :, most_rows] if direct else srcs[a].at[:, most_rows]
        pltpu.make_async_copy(sent, sent, send_sem.at[a]).wait()
        gone = obuf.at[:, a, most_rows]
        pltpu.make_async_copy(gone, gone, osend_sem.at[a]).wait()
        pltpu.make_async_copy(fins[a], fins[a], out_sem.at[a]).wait()
    for n, name in enumerate(("wrow", "wall", "grecv", "srecv", "crecv", "nrecv")):
        sent = s[name].at[pl.ds(0, s[name].shape[0] - 1)]
        pltpu.make_async_copy(sent, sent, misc_send.at[n]).wait()


def step_kernel(direct, *refs):
    if direct:
        fins, refs = refs[0:2], refs[2:]
    red_ref, nrm_ref, w_ref, m1_ref, m2_ref, gain_ref, gm_ref, gv_ref, bias_ref, bm_ref, bv_ref = refs[:11]
    refs = refs[11:]
    if direct:
        bigs, refs, sem = refs[0:2], refs[2:11], refs[11]
        copies = [pltpu.make_async_copy(fins[a], bigs[a], sem.at[a]) for a in range(2)]
        for copy in copies:
            copy.start()
    nw_ref, n1_ref, n2_ref, ng_ref, ngm_ref, ngv_ref, nb_ref, nbm_ref, nbv_ref = refs
    width = gain_ref.shape[1]
    heads = bias_ref.shape[1]
    wval = w_ref[...]
    first, second, step_w = moments(wval, red_ref[0:5, :], m1_ref[...], m2_ref[...])
    spot = lax.broadcasted_iota(jnp.int32, (1, width), 1)
    place = lax.broadcasted_iota(jnp.int32, (5, 1), 0)
    value_sq = jnp.sum(jnp.where(spot == place, nrm_ref[...], 0.0), 1, keepdims=True)
    step_sq = jnp.sum(jnp.where(spot == place + 8, nrm_ref[...], 0.0), 1, keepdims=True)
    nw_ref[...] = wval - rate * (jnp.sqrt(value_sq) / jnp.sqrt(step_sq)) * step_w
    n1_ref[...] = first
    n2_ref[...] = second
    for row, n, own in (
        (5, width, (gain_ref, gm_ref, gv_ref, ng_ref, ngm_ref, ngv_ref)),
        (6, heads, (bias_ref, bm_ref, bv_ref, nb_ref, nbm_ref, nbv_ref)),
    ):
        val = own[0][...]
        first, second, step_v = moments(val, red_ref[row : row + 1, 0:n], own[1][...], own[2][...])
        ratio = jnp.sqrt(jnp.sum(val * val, 1, keepdims=True)) / jnp.sqrt(
            jnp.sum(step_v * step_v, 1, keepdims=True)
        )
        own[3][...] = val - rate * ratio * step_v
        own[4][...] = first
        own[5][...] = second
    if direct:
        for copy in copies:
            copy.wait()


def body(
    nrow,
    ncol,
    pair,
    cotangent,
    segments,
    lengths,
    weights,
    moment_one,
    moment_two,
    gain,
    gain_m,
    gain_v,
    chain_bias,
    bias_m,
    bias_v,
):
    crops, rl, cl, width = pair.shape
    heads = chain_bias.shape[0]
    cb = cl // nrow
    wr = weights.shape[1] // width
    total = nrow * rl
    tile = min(256, total)
    slots = -(-8 // ncol)
    direct = cb % 16 == 0 and rl % 16 == 0
    dims = (nrow, ncol, crops, cb, rl, width, heads, wr, tile, direct)
    wtype = BF if wr % 16 == 0 else F32
    hbm = pl.BlockSpec(memory_space=pl.ANY)
    vmem = pl.BlockSpec(memory_space=pltpu.VMEM)
    smem = pl.BlockSpec(memory_space=pltpu.SMEM)
    dma = pltpu.SemaphoreType.DMA
    parts = (crops, nrow, cb, rl, width)
    if direct:
        sources = (pair, cotangent)
        fin = jax.ShapeDtypeStruct(pair.shape, BF)
        obuf = (crops, 2, nrow, rl, cb, width)
    else:
        sources = tuple(jnp.swapaxes(x, 1, 2).reshape(parts) for x in (pair, cotangent))
        fin = jax.ShapeDtypeStruct(parts, BF)
        obuf = (crops * cb, 2, nrow, rl, width)
    scratch = {
        "zin": pltpu.VMEM((crops * cb, 2, nrow, rl, width), BF),
        "obuf": pltpu.VMEM(obuf, BF),
        "prob": pltpu.VMEM((heads, total, total), BF),
        "wtmp": pltpu.VMEM((8, wr, width), F32),
        "wsend": pltpu.VMEM((slots * ncol, wr, width), wtype),
        "wrow": pltpu.VMEM((nrow, slots, wr, width), wtype),
        "wall": pltpu.VMEM((ncol, nrow, slots, wr, width), wtype),
        "gsend": pltpu.VMEM((slots * ncol, width, width), F32),
        "grecv": pltpu.VMEM((ncol, slots, width, width), F32),
        "ssend": pltpu.VMEM((nrow, slots, wr, width), F32),
        "srecv": pltpu.VMEM((nrow, slots, wr, width), F32),
        "csend": pltpu.VMEM((slots, wr, width), F32),
        "crecv": pltpu.VMEM((ncol, slots, wr, width), F32),
        "nsend": pltpu.VMEM((1, width), F32),
        "nrecv": pltpu.VMEM((nrow, 1, width), F32),
        "wallt": pltpu.VMEM((4 * width, width), BF),
        "wkv": pltpu.VMEM((width, 2 * width), BF),
        "w4": pltpu.VMEM((width, width), BF),
        "wcat": pltpu.VMEM((width, 4 * width), BF),
        "augk": pltpu.VMEM((crops, total, width), BF),
        "augq": pltpu.VMEM((crops, heads, width, total), BF),
        "hot": pltpu.VMEM((crops, 16, total), BF),
        "dwt_acc": pltpu.VMEM((4 * width, width), F32),
        "dw4_acc": pltpu.VMEM((width, width), F32),
        "dg_acc": pltpu.VMEM((8, width), F32),
        "db_acc": pltpu.VMEM((heads, 8, tile), F32),
        "in_sem": dma((crops * cb,)),
        "send_sem": dma((2,)),
        "out_sem": dma((2,)),
        "osend_sem": dma((2,)),
        "misc_recv": dma((6,)),
        "misc_send": dma((6,)),
    }
    if direct:
        scratch["stage"] = pltpu.VMEM((2, rl * cb, width), F32)
        scratch["sbuf"] = pltpu.VMEM((crops, 2, cb, nrow, rl, width), BF)
        scratch["raw_sem"] = dma((crops, 2, nrow))
    *fins, red, nrm = pl.pallas_call(
        functools.partial(main_kernel, dims, tuple(scratch)),
        out_shape=(
            pltpu.VMEM(fin.shape, BF) if direct else fin,
            pltpu.VMEM(fin.shape, BF) if direct else fin,
            pltpu.VMEM((slots * ncol, wr * width), F32),
            pltpu.VMEM((1, width), F32),
        ),
        in_specs=[hbm, hbm, vmem, smem, vmem, vmem, vmem, vmem, smem],
        out_specs=(hbm, hbm, vmem, vmem),
        scratch_shapes=list(scratch.values()),
        compiler_params=pltpu.CompilerParams(
            collective_id=0, has_side_effects=True, vmem_limit_bytes=44 << 20
        ),
        name="column_attention",
    )(
        *(
            pltpu.with_memory_space_constraint(x, pltpu.HBM)
            for x in (
                *sources,
                segments,
                lengths,
                weights,
                moment_one,
                moment_two,
                gain.reshape(1, width),
                chain_bias,
            )
        )
    )
    small = (gain, gain_m, gain_v, chain_bias, bias_m, bias_v)
    ops = [red, nrm, weights, moment_one, moment_two] + [a.reshape(1, -1) for a in small]
    bigs = [fin, fin] if direct else []
    res = pl.pallas_call(
        functools.partial(step_kernel, direct),
        out_shape=bigs
        + [jax.ShapeDtypeStruct(weights.shape, F32)] * 3
        + [jax.ShapeDtypeStruct((1, width), F32)] * 3
        + [jax.ShapeDtypeStruct((1, heads), F32)] * 3,
        in_specs=[vmem] * (len(bigs) + len(ops)),
        out_specs=[hbm] * len(bigs) + [vmem] * 9,
        scratch_shapes=[dma((2,))] if direct else [],
        compiler_params=pltpu.CompilerParams(vmem_limit_bytes=12 << 20),
        name="lamb_step",
    )(*(fins if direct else ()), *ops)
    if direct:
        fins, res = res[:2], res[2:]
    else:
        fins = [jnp.swapaxes(x.reshape(crops, cl, rl, width), 1, 2) for x in fins]
    return (*fins, *res[:3], *[a.reshape(-1) for a in res[3:]])


def solution(mesh):
    big = P(None, "row", "col", None)
    shard = P(None, "row")
    return jax.shard_map(
        functools.partial(body, mesh.shape["row"], mesh.shape["col"]),
        mesh=mesh,
        in_specs=(big, big, P(), P(), shard, shard, shard) + (P(),) * 6,
        out_specs=(big, big, shard, shard, shard) + (P(),) * 6,
        check_vma=False,
    )
```

time: 426 us -> 383 us (0.90)
  Pallas kernels: 402 us -> 378 us
  local copies, waits for them, and re-layouts: 22.8 us -> 0.04 us
    pallas_call x2, Pallas kernels: 402 us -> 378 us  [the longest x1 374 us: body(): pl.pallas_call(functools.partial(main_kernel, dims, tuple(scratch)), out_...]
    transpose x3 -> x0, local copies, waits for them, and re-layouts: 22.8 us -> none  [the longest x1 11 us: body(): pair_grad = jnp.swapaxes(gradc.reshape(crops, cl, rl, width), 1, 2)]
where the time goes in v2:
time: 383 us; the launch traced here: 379 us
  Pallas kernels  378 us (99%)
    pallas_call x1, Pallas kernels, body(): pl.pallas_call(functools.partial(main_kernel, dims, tuple(scratch)), out_...  374 us

profile of v2, /device:TPU:0, one launch (start us, length us, event | category | flops | bytes accessed | tf_op | source)
XLA Modules:
  0.0 379.3 jit_solution(17469611073867389475)
XLA Ops:
  0.6 0.0 copy-start
  0.7 0.0 copy-start.1
  0.7 0.0 copy-start.2
  0.7 0.0 copy-start.3
  0.7 0.0 copy-start.4
  0.7 0.0 copy-start.5
  0.7 0.0 copy-start.6
  0.7 0.0 copy-start.7
  0.7 0.0 copy-start.8
  0.7 374.2 %column_attention.1 = (bf16[2,64,128,128]{3,2,1,0:T(8,128)(2,1)S(1)}, bf16[2,64,128,128]{3,2,1,0:T(8,128)(2,1)S(1)}, f32[8,2048]{1,0:T(8,128)S(1)}, f32[1,128]{1,0:T(1,128)S(1)}) custom-call(bf16[2,64,128,128]{3,2,1,0:T(8,128)(2,1)} %refs_0_.1, bf16[2,64,128,128]{3,2,1,0:T(8,128)(2,1)} %refs_1_.1, s32[2,512]{1,0:T(2,128)} %refs_2_.1, s32[2]{0:T(128)} %refs_3_.1, ...), custom_call_target="tpu_custom_call" | custom-call | tf_op jit(solution)/shard_map/column_attention/pallas_call | solution.py:556
  374.9 0.0 copy-done
  374.9 0.0 copy-done.1
  375.0 0.0 copy-done.2
  375.0 0.0 copy-done.3
  375.0 0.0 copy-done.4
  375.0 0.0 copy-done.5
  375.0 0.0 copy-done.6
  375.0 0.0 copy-done.7
  375.0 0.0 copy-done.8
  375.0 4.1 %lamb_step.1 = (bf16[2,64,128,128]{3,2,1,0:T(8,128)(2,1)}, bf16[2,64,128,128]{3,2,1,0:T(8,128)(2,1)}, f32[5,2048]{1,0:T(8,128)}, f32[5,2048]{1,0:T(8,128)}, f32[...) custom-call(bf16[2,64,128,128]{3,2,1,0:T(8,128)(2,1)S(1)} %get-tuple, ...), custom_call_target="tpu_custom_call" | custom-call | tf_op jit(solution)/shard_map/lamb_step/pallas_call | solution.py:589
Async XLA Ops:
  0.6 374.3 %copy-start = (f32[5,2048]{1,0:T(8,128)S(1)}, f32[5,2048]{1,0:T(8,128)}, u32[]{:S(2)}) copy-start(f32[5,2048]{1,0:T(8,128)} %refs_4_.3) | copy-start | bytes 122884
  0.7 374.3 %copy-start.1 = (f32[5,2048]{1,0:T(8,128)S(1)}, f32[5,2048]{1,0:T(8,128)}, u32[]{:S(2)}) copy-start(f32[5,2048]{1,0:T(8,128)} %refs_5_.3) | copy-start | bytes 122884
  0.7 374.3 %copy-start.2 = (f32[5,2048]{1,0:T(8,128)S(1)}, f32[5,2048]{1,0:T(8,128)}, u32[]{:S(2)}) copy-start(f32[5,2048]{1,0:T(8,128)} %refs_6_.3) | copy-start | bytes 122884
  0.7 374.3 %copy-start.3 = (f32[128]{0:T(128)S(1)}, f32[128]{0:T(128)}, u32[]{:S(2)}) copy-start(f32[128]{0:T(128)} %param.20) | copy-start | bytes 1540
  0.7 374.3 %copy-start.4 = (f32[4]{0:T(128)S(1)}, f32[4]{0:T(128)}, u32[]{:S(2)}) copy-start(f32[4]{0:T(128)} %refs_8_.1) | copy-start | bytes 52
  0.7 374.3 %copy-start.5 = (f32[128]{0:T(128)S(1)}, f32[128]{0:T(128)}, u32[]{:S(2)}) copy-start(f32[128]{0:T(128)} %param.21) | copy-start | bytes 1540
  0.7 374.3 %copy-start.6 = (f32[128]{0:T(128)S(1)}, f32[128]{0:T(128)}, u32[]{:S(2)}) copy-start(f32[128]{0:T(128)} %param.22) | copy-start | bytes 1540
  0.7 374.3 %copy-start.7 = (f32[4]{0:T(128)S(1)}, f32[4]{0:T(128)}, u32[]{:S(2)}) copy-start(f32[4]{0:T(128)} %param.24) | copy-start | bytes 52
  0.7 374.3 %copy-start.8 = (f32[4]{0:T(128)S(1)}, f32[4]{0:T(128)}, u32[]{:S(2)}) copy-start(f32[4]{0:T(128)} %param.25) | copy-start | bytes 52

commit v3 on v2

v3 whole, which is shorter than its diff:
```python
import functools
import math

import jax
import jax.numpy as jnp
from jax import lax
from jax.experimental import pallas as pl
from jax.experimental.pallas import tpu as pltpu
from jax.sharding import PartitionSpec as P

STEP = 10
beta_one = 0.9
beta_two = 0.999
epsilon = 1e-06
decay = 0.01
rate = 0.25

BF = jnp.bfloat16
F32 = jnp.float32
MESH = pl.DeviceIdType.MESH
NT = ((1,), (1,))
TN = ((0,), (0,))
LOG2E = math.log2(math.e)
SEGS = 4
LEAD, AHEAD, LAG = 8, 2, 2


def dot(a, b, dims=((1,), (0,))):
    return lax.dot_general(a, b, (dims, ((), ())), preferred_element_type=F32)


def normed(z, gain):
    mean = jnp.mean(z, -1, keepdims=True)
    cen = z - mean
    var = jnp.mean(cen * cen, -1, keepdims=True)
    inv = lax.rsqrt(var + 1e-05)
    xhat = cen * inv
    return xhat, inv, (xhat * gain).astype(BF)


def attend(z, co, yown, yall, wqg_t, wkv, wkv_t, w4, wqg, augk, augq, hotk, hotq, e_ref, heads):
    qn, width = z[0].shape
    hsize = width // heads
    scale = 1.0 / math.sqrt(hsize)
    kv = dot(yall, wkv).astype(BF)
    kvT = dot(wkv_t, yall, NT).astype(BF)
    head_of = lax.broadcasted_iota(jnp.int32, (width, 1), 0) // hsize
    ones = jnp.ones((16, 2 * qn), BF)
    outs, dqgT, dkA, dkP = [], [], [], None
    dw4, db = 0.0, [0.0] * heads
    for c in range(2):
        first, packed = slice(c * qn, (c + 1) * qn), slice(2 * qn, 3 * qn)
        k = jnp.concatenate([kv[first, :width], kv[packed, :width]], 0)
        v = jnp.concatenate([kv[first, width:], kv[packed, width:]], 0)
        bothT = jnp.concatenate([kvT[:, first], kvT[:, packed]], 1)
        kT, vT = bothT[:width], bothT[width:]
        projT = dot(wqg_t, yown[c], NT)
        qT = projT[:width].astype(BF)
        gT = jax.nn.sigmoid(projT[width:])
        kaug = jnp.concatenate([k, augk[c]], 1)
        heads_a, heads_r = [], []
        for h in range(heads):
            rows = slice(h * hsize, (h + 1) * hsize)
            qaug = jnp.concatenate([jnp.where(head_of == h, qT, jnp.zeros_like(qT)), augq[c][h]], 0)
            s = dot(kaug, qaug) * (scale * LOG2E)
            e = jnp.exp2(s - jnp.max(s, 0, keepdims=True)).astype(BF)
            e_ref[h] = e
            a = dot(jnp.concatenate([vT[rows], ones], 0), e)
            r = 1.0 / a[hsize : hsize + 1]
            heads_a.append(a[:hsize] * r)
            heads_r.append(jnp.broadcast_to(r, (hsize, qn)))
        aT = jnp.concatenate(heads_a, 0)
        oT = (aT * gT).astype(BF)
        outs.append(z[c] + dot(oT, w4, TN))
        dw4 = dw4 + dot(oT, co[c])
        doT = dot(w4, co[c], NT).astype(BF).astype(F32)
        daT = (doT * gT).astype(BF).astype(F32)
        dgT = (doT * aT * gT * (1.0 - gT)).astype(BF)
        dnT = (daT * jnp.concatenate(heads_r, 0) * scale).astype(BF)
        prod = aT * dnT.astype(F32)
        dq, dk, dv = [], [], []
        for h in range(heads):
            rows = slice(h * hsize, (h + 1) * hsize)
            shift = jnp.sum(prod[rows], 0, keepdims=True)
            masked = jnp.where(head_of == h, dnT, jnp.zeros_like(dnT))
            e = e_ref[h]
            ds = (e.astype(F32) * (dot(v, masked) - shift)).astype(BF)
            x = dot(jnp.concatenate([kT[rows], hotk[c]], 0), ds)
            dq.append(x[:hsize].astype(BF))
            db[h] = db[h] + x[hsize : hsize + 8] * hotq[c][:8].astype(F32)
            dk.append(dot(qT[rows], ds, NT))
            dv.append(dot(dnT[rows], e, NT) * (1.0 / scale))
        dqgT.append(jnp.concatenate(dq + [dgT], 0))
        dkv = jnp.concatenate(dk + dv, 0)
        dkA.append(dkv[:, :qn].astype(BF))
        dkP = dkv[:, qn:] if dkP is None else dkP + dkv[:, qn:]
    dqgT = jnp.concatenate(dqgT, 1)
    dkvT = jnp.concatenate(dkA + [dkP.astype(BF)], 1)
    dwqg = dot(dqgT, jnp.concatenate(yown, 0))
    dwkv = dot(dkvT, yall)
    dy_own = jnp.transpose(dot(wqg, dqgT))
    dy_all = jnp.transpose(dot(wkv, dkvT))
    return outs, dy_own, dy_all, dwqg, dwkv, dw4, db


def moments(value, grad, first, second):
    first_new = beta_one * first + (1.0 - beta_one) * grad
    second_new = beta_two * second + (1.0 - beta_two) * grad * grad
    step_dir = (
        first_new
        / (1.0 - beta_one**STEP)
        / (jnp.sqrt(second_new / (1.0 - beta_two**STEP)) + epsilon)
        + decay * value
    )
    return (first_new, second_new, step_dir)


def main_kernel(dims, names, *refs):
    nrow, ncol, crops, cpd, gc, rl, width, heads, wr, direct = dims
    pair_ref, cot_ref, seg_ref, len_ref, w_ref, m1_ref, m2_ref, gain_ref, bias_ref = refs[:9]
    srcs = (pair_ref, cot_ref)
    s = dict(zip(names, refs[9:]))
    zin, y3, d3, own, xring, iring, yring = (s[n] for n in ("zin", "y3", "d3", "own", "xring", "iring", "yring"))
    in_sem, send_sem, ret_sem, rsend_sem = s["in_sem"], s["send_sem"], s["ret_sem"], s["rsend_sem"]
    misc_recv, misc_send, y_sem, d_sem, x_send = (
        s[n] for n in ("misc_recv", "misc_send", "y_sem", "d_sem", "x_send")
    )
    red_ref, nrm_ref = s["red"], s["nrm"]
    half = nrow // 2
    qn = half * rl
    groups = cpd // gc
    ring = xring.shape[0]
    cols = [s["col%d" % g] for g in range(groups)]
    hsize = width // heads
    scale = 1.0 / math.sqrt(hsize)
    slots = s["wrow"].shape[1]
    me = lax.axis_index("row")
    mc = lax.axis_index("col")
    side = me // half
    place = lax.rem(me, half)
    partner = (lax.rem(me + half, nrow), mc)

    def row_peer(d):
        return lax.rem(me + d, nrow)

    def col_peer(d):
        return lax.rem(mc + d, ncol)

    def near(d):
        return lax.rem(place + d, half)

    def device(w):
        return (side * half + w, mc)

    def load_group(g):
        def load(w, _):
            first = pl.multiple_of(w * cpd, gc) + g * gc
            for c in range(crops):
                for a in range(2):
                    pltpu.make_async_copy(
                        srcs[a].at[c, :, pl.ds(pl.multiple_of(first, gc), gc), :],
                        s["raw"].at[w, c, a],
                        s["raw_sem"].at[w, c, a],
                    ).start()
            return 0

        lax.fori_loop(0, half, load, 0)

    if direct:
        load_group(0)

    barrier = pltpu.get_barrier_semaphore()

    def greet_row(d, _):
        pl.semaphore_signal(barrier, inc=1, device_id=(row_peer(d), mc), device_id_type=MESH)
        return 0

    def greet_col(d, _):
        pl.semaphore_signal(barrier, inc=1, device_id=(me, col_peer(d)), device_id_type=MESH)
        return 0

    lax.fori_loop(1, nrow, greet_row, 0)
    lax.fori_loop(1, ncol, greet_col, 0)
    for j in range(wr):
        s["wtmp"][0:5, j, :] = w_ref[:, j * width : (j + 1) * width]
    for k in range(slots * ncol):
        s["wsend"][k] = (s["wtmp"][k] if k < 5 else jnp.zeros((wr, width), F32)).astype(s["wsend"].dtype)
    pl.semaphore_wait(barrier, nrow - 1 + ncol - 1)

    def remote(src, dst, send, recv, peer):
        pltpu.make_async_remote_copy(
            src, dst, send, recv, device_id=peer, device_id_type=MESH
        ).start()

    def exchange_row(src_of, dst, n):
        def push(d, _):
            p = row_peer(d)
            remote(src_of(p), dst.at[me], misc_send.at[n], misc_recv.at[n], (p, mc))
            return 0

        lax.fori_loop(1, nrow, push, 0)
        pltpu.make_async_copy(src_of(me), dst.at[me], misc_recv.at[n]).start()

    def exchange_col(src_of, dst, n):
        def push(d, _):
            p = col_peer(d)
            remote(src_of(p), dst.at[mc], misc_send.at[n], misc_recv.at[n], (me, p))
            return 0

        lax.fori_loop(1, ncol, push, 0)
        pltpu.make_async_copy(src_of(mc), dst.at[mc], misc_recv.at[n]).start()

    def landed(dst, n):
        pltpu.make_async_copy(dst, dst, misc_recv.at[n]).wait()

    def total_of(ref, n):
        return lax.fori_loop(1, n, lambda r, t: t + ref[r], ref[0])

    exchange_row(lambda p: s["wsend"].at[pl.ds(mc * slots, slots)], s["wrow"], 0)

    def column_of(u, w):
        return s["sbuf"].at[lax.rem(u, gc), :, :, w] if direct else pair_ref.at[u, :, :, w]

    def push_to(u, d):
        w = near(d)
        remote(column_of(u, w), zin.at[u, :, :, place], send_sem.at[u // gc], in_sem.at[u], device(w))

    def push_column(u):
        def to_peer(d, _):
            push_to(u, d)
            return 0

        lax.fori_loop(1, half, to_peer, 0)
        if not direct:
            pltpu.make_async_copy(column_of(u, place), zin.at[u, :, :, place], in_sem.at[u]).start()

    def push_columns(first, last):
        def at_column(u, _):
            push_column(u)
            return 0

        lax.fori_loop(first, last, at_column, 0)

    def turn(g, w, mine):
        for c in range(crops):
            for a in range(2):
                here = s["raw"].at[w, c, a]
                pltpu.make_async_copy(here, here, s["raw_sem"].at[w, c, a]).wait()
                s["stage"][a] = s["raw"][w, c, a].astype(F32).reshape(rl * gc, width)
                for j in range(gc):
                    turned = s["stage"][a, pl.ds(j, rl, stride=gc), :].astype(BF)
                    if mine:
                        zin[g * gc + j, c, a, w] = turned
                    else:
                        s["sbuf"][j, c, a, w] = turned

    if direct:

        def first_blocks(d, _):
            turn(0, near(d), False)
            push_to(0, d)
            return 0

        lax.fori_loop(1, half, first_blocks, 0)
        turn(0, place, True)
        push_columns(1, LEAD - AHEAD)
        if groups > 1:
            load_group(1)
    else:
        push_columns(0, min(LEAD - AHEAD, cpd))

    landed(s["wrow"], 0)
    exchange_col(lambda p: s["wrow"], s["wall"], 1)

    back = lax.broadcasted_iota(jnp.int32, (qn, qn), 0) + lax.broadcasted_iota(jnp.int32, (qn, qn), 1)
    s["rev"][...] = jnp.where(back == qn - 1, 1.0, 0.0).astype(BF)
    lane = lax.broadcasted_iota(jnp.int32, (1, qn), 1)
    line = lax.broadcasted_iota(jnp.int32, (width, 1), 0)
    for c in range(crops):
        low_seg, high_seg = seg_ref[c : c + 1, :qn], seg_ref[c : c + 1, qn:]
        own_seg = jnp.where(side == 0, low_seg, high_seg)
        same_low = (lax.rem(line, SEGS) == low_seg).astype(F32)
        same_high = (lax.rem(line, SEGS) == high_seg).astype(F32)
        pad = jnp.where(lane + qn >= len_ref[c], -1e30, 0.0)
        if c == 1:
            same_high = dot(same_high.astype(BF), s["rev"][...])
            pad = jnp.where(2 * qn - 1 - lane >= len_ref[c], -1e30, 0.0)
        same = jnp.concatenate([same_low, same_high], 1)
        pad = jnp.concatenate([jnp.zeros((1, qn), F32), pad], 1)
        s["hotk"][c] = jnp.where(line[:16] < SEGS, same[:16], 0.0).astype(BF)
        rowsk = jnp.where(line < 3 * SEGS, same, jnp.where(line == 3 * SEGS, pad, 0.0))
        s["augk"][c] = jnp.transpose(rowsk).astype(BF)
        same = (lax.rem(line, SEGS) == own_seg).astype(F32)
        s["hotq"][c] = jnp.where(line[:16] < SEGS, same[:16], 0.0).astype(BF)
        for h in range(heads):
            full = jnp.full((width, 1), bias_ref[h] * (1.0 / scale), F32)
            high = full.astype(BF).astype(F32)
            mid = (full - high).astype(BF).astype(F32)
            low = full - high - mid
            part = jnp.where(line < SEGS, high, jnp.where(line < 2 * SEGS, mid, low))
            rowsq = jnp.where(line < 3 * SEGS, same * part, jnp.where(line == 3 * SEGS, 1.0, 0.0))
            s["augq"][c, h] = rowsq.astype(BF)

    for name in ("dwqg_acc", "dwkv_acc", "dw4_acc", "dg_acc", "db_acc"):
        s[name][...] = jnp.zeros_like(s[name])

    landed(s["wall"], 1)
    for k in range(5):
        w = s["wall"][k // slots, :, k % slots].astype(F32).reshape(width, width)
        if k == 4:
            s["w4"][...] = w.astype(BF)
        else:
            name, at = {0: ("wqg", 0), 3: ("wqg", 1), 1: ("wkv", 0), 2: ("wkv", 1)}[k]
            s[name][:, at * width : (at + 1) * width] = w.astype(BF)
            s[name + "_t"][at * width : (at + 1) * width, :] = jnp.transpose(w).astype(BF)

    where_t = lax.broadcasted_iota(jnp.int32, (qn, 1), 0)

    def prepare(u):
        new = zin.at[u, :, :, pl.ds(0, half - 1)] if direct else zin.at[u]
        pltpu.make_async_copy(new, new, in_sem.at[u]).wait()
        at = lax.rem(u, ring)
        for c in range(crops):
            rows = slice(c * qn, (c + 1) * qn)
            xhat, inv, y = normed(zin[u, c, 0].astype(F32).reshape(qn, width), gain_ref[...])
            xring[at, rows, :] = xhat
            iring[at, rows, :] = jnp.broadcast_to(inv, (qn, width))
            yring[at, rows, :] = y

        @pl.when(side == 0)
        def _():
            y3[u, 0 : 2 * qn, :] = yring[at]
            part = y3.at[u, pl.ds(0, 2 * qn)]
            remote(part, part, x_send.at[0], y_sem.at[u], partner)

        @pl.when(side == 1)
        def _():
            y1 = dot(s["rev"][...], yring[at, qn : 2 * qn, :])
            y0 = yring[at, 0:qn, :].astype(F32)
            y3[u, 2 * qn : 3 * qn, :] = jnp.where(where_t < len_ref[0] - qn, y0, y1).astype(BF)
            part = y3.at[u, pl.ds(2 * qn, qn)]
            remote(part, part, x_send.at[0], y_sem.at[u], partner)

    def give(u, a):
        g = u // gc
        for n in range(groups):

            @pl.when(g == n)
            def _():
                here = cols[n].at[a, :, place, u - n * gc]

                def to_peer(d, _):
                    w = near(d)
                    remote(zin.at[u, :, a, w], here, rsend_sem.at[n], ret_sem.at[n], device(w))
                    return 0

                lax.fori_loop(1, half, to_peer, 0)
                pltpu.make_async_copy(zin.at[u, :, a, place], here, ret_sem.at[n]).start()

    def work(u):
        @pl.when(side == 0)
        def _():
            part = y3.at[u, pl.ds(2 * qn, qn)]
            pltpu.make_async_copy(part, part, y_sem.at[u]).wait()

        @pl.when(side == 1)
        def _():
            part = y3.at[u, pl.ds(0, 2 * qn)]
            pltpu.make_async_copy(part, part, y_sem.at[u]).wait()

        at = lax.rem(u, ring)
        outs, dy_own, dy_all, dwqg, dwkv, dw4, db = attend(
            [zin[u, c, 0].astype(F32).reshape(qn, width) for c in range(crops)],
            [zin[u, c, 1].astype(F32).reshape(qn, width).astype(BF) for c in range(crops)],
            [yring[at, c * qn : (c + 1) * qn, :] for c in range(crops)],
            y3[u],
            s["wqg_t"][...],
            s["wkv"][...],
            s["wkv_t"][...],
            s["w4"][...],
            s["wqg"][...],
            [s["augk"][c] for c in range(crops)],
            [[s["augq"][c, h] for h in range(heads)] for c in range(crops)],
            [s["hotk"][c] for c in range(crops)],
            [s["hotq"][c] for c in range(crops)],
            s["prob"],
            heads,
        )
        s["dwqg_acc"][...] += dwqg
        s["dwkv_acc"][...] += dwkv
        s["dw4_acc"][...] += dw4
        for h in range(heads):
            s["db_acc"][h] += db[h]
        for c in range(crops):
            zin[u, c, 0] = outs[c].reshape(half, rl, width).astype(BF)
        give(u, 0)

        @pl.when(side == 0)
        def _():
            own[at, 0 : 2 * qn, :] = dy_own + dy_all[0 : 2 * qn]
            d3[u, 2 * qn : 3 * qn, :] = dy_all[2 * qn :].astype(BF)
            part = d3.at[u, pl.ds(2 * qn, qn)]
            remote(part, part, x_send.at[1], d_sem.at[u], partner)

        @pl.when(side == 1)
        def _():
            own[at, 0 : 2 * qn, :] = dy_own
            own[at, 2 * qn : 3 * qn, :] = dy_all[2 * qn :]
            d3[u, 0 : 2 * qn, :] = dy_all[0 : 2 * qn].astype(BF)
            part = d3.at[u, pl.ds(0, 2 * qn)]
            remote(part, part, x_send.at[1], d_sem.at[u], partner)

    def finish(u):
        at = lax.rem(u, ring)

        @pl.when(side == 0)
        def _():
            part = d3.at[u, pl.ds(0, 2 * qn)]
            pltpu.make_async_copy(part, part, d_sem.at[u]).wait()
            own[at, 0 : 2 * qn, :] += d3[u, 0 : 2 * qn, :].astype(F32)

        @pl.when(side == 1)
        def _():
            part = d3.at[u, pl.ds(2 * qn, qn)]
            pltpu.make_async_copy(part, part, d_sem.at[u]).wait()
            both = own[at, 2 * qn : 3 * qn, :] + d3[u, 2 * qn : 3 * qn, :].astype(F32)
            mine = where_t < len_ref[0] - qn
            own[at, 0:qn, :] += jnp.where(mine, both, 0.0)
            own[at, qn : 2 * qn, :] += dot(s["rev"][...], jnp.where(mine, 0.0, both).astype(BF))

        for c in range(crops):
            rows = slice(c * qn, (c + 1) * qn)
            dy, xhat = own[at, rows, :], xring[at, rows, :]
            s["dg_acc"][0:1] += jnp.sum(dy * xhat, 0, keepdims=True)
            dx = dy * gain_ref[...]
            rest = dx - jnp.mean(dx, -1, keepdims=True) - xhat * jnp.mean(dx * xhat, -1, keepdims=True)
            grad = zin[u, c, 1].astype(F32).reshape(qn, width) + iring[at, rows, :] * rest
            zin[u, c, 1] = grad.reshape(half, rl, width).astype(BF)
        give(u, 1)

    def refill():
        sent = s["sbuf"].at[:, :, :, pl.ds(0, half - 1)]
        pltpu.make_async_copy(sent, sent, send_sem.at[0]).wait()

        def block(d, _):
            turn(1, near(d), False)
            return 0

        lax.fori_loop(1, half, block, 0)
        turn(1, place, True)

    def turn_back():
        pltpu.make_async_copy(cols[0], cols[0], ret_sem.at[0]).wait()

        def block(w, _):
            for c in range(crops):
                for a in range(2):
                    for j in range(gc):
                        s["stage"][a, pl.ds(j, rl, stride=gc), :] = cols[0][a, c, w, j].astype(F32)
                    s["fin0"][a, c, w] = s["stage"][a].reshape(rl, gc, width).astype(BF)
            return 0

        lax.fori_loop(0, half, block, 0)

    turn_at = gc + LAG + 5
    refill_at = gc - 5

    def step(n, _):
        it = n - AHEAD
        nxt = it + LEAD
        limit = gc if direct else cpd

        @pl.when(nxt < limit)
        def _():
            push_column(nxt)

        if direct and groups > 1:

            @pl.when(it == refill_at)
            def _():
                refill()
                push_columns(gc, refill_at + LEAD + 1)

            @pl.when((it > refill_at) & (nxt < cpd))
            def _():
                push_column(nxt)

        @pl.when(it + AHEAD < cpd)
        def _():
            prepare(it + AHEAD)

        @pl.when((it >= 0) & (it < cpd))
        def _():
            work(it)

        @pl.when(it >= LAG)
        def _():
            finish(it - LAG)

        if direct and groups > 1:

            @pl.when(it == turn_at)
            def _():
                turn_back()

        return 0

    lax.fori_loop(0, cpd + AHEAD + LAG, step, 0)

    gsend = s["gsend"]
    for k, (name, at) in enumerate((("dwqg_acc", 0), ("dwkv_acc", 0), ("dwkv_acc", 1), ("dwqg_acc", 1))):
        gsend[k] = jnp.transpose(s[name][at * width : (at + 1) * width, :])
    gsend[4] = s["dw4_acc"][...]
    gsend[5] = jnp.broadcast_to(s["dg_acc"][0:1], (width, width))
    spot = lax.broadcasted_iota(jnp.int32, (1, width), 1)
    dbias = jnp.zeros((1, width), F32)
    for h in range(heads):
        total_h = jnp.sum(jnp.sum(s["db_acc"][h], 0, keepdims=True), 1, keepdims=True)
        dbias = jnp.where(spot == h, total_h * (1.0 / scale), dbias)
    gsend[6] = jnp.broadcast_to(dbias, (width, width))
    for k in range(7, slots * ncol):
        gsend[k] = jnp.zeros((width, width), F32)
    exchange_col(lambda p: gsend.at[pl.ds(p * slots, slots)], s["grecv"], 2)
    landed(s["grecv"], 2)
    share = total_of(s["grecv"], ncol)
    for p in range(nrow):
        s["ssend"][p] = share[:, p * wr : (p + 1) * wr, :]
    exchange_row(lambda p: s["ssend"].at[p], s["srecv"], 3)
    landed(s["srecv"], 3)
    s["csend"][...] = total_of(s["srecv"], nrow)
    exchange_col(lambda p: s["csend"], s["crecv"], 4)
    landed(s["crecv"], 4)
    for j in range(wr):
        red_ref[:, j * width : (j + 1) * width] = s["crecv"][:, :, j, :].reshape(slots * ncol, width)
    wval = w_ref[...]
    step_w = moments(wval, red_ref[0:5, :], m1_ref[...], m2_ref[...])[2]
    row5 = lax.broadcasted_iota(jnp.int32, (5, 1), 0)
    squares = jnp.where(spot == row5, jnp.sum(wval * wval, 1, keepdims=True), 0.0)
    squares += jnp.where(spot == row5 + 8, jnp.sum(step_w * step_w, 1, keepdims=True), 0.0)
    s["nsend"][...] = jnp.sum(squares, 0, keepdims=True)
    exchange_row(lambda p: s["nsend"], s["nrecv"], 5)
    landed(s["nrecv"], 5)
    nrm_ref[...] = total_of(s["nrecv"], nrow)

    most = pl.ds(0, half - 1)
    for g in range(groups):
        if not direct or g == groups - 1:
            sent = s["sbuf"].at[:, :, :, most] if direct else pair_ref.at[:, :, :, most]
            pltpu.make_async_copy(sent, sent, send_sem.at[g]).wait()
        gone = cols[g].at[:, :, most]
        pltpu.make_async_copy(gone, gone, rsend_sem.at[g]).wait()
        if not direct or groups == 1 or g > 0:
            pltpu.make_async_copy(cols[g], cols[g], ret_sem.at[g]).wait()

    @pl.when(side == 0)
    def _():
        part = y3.at[:, pl.ds(0, 2 * qn)]
        pltpu.make_async_copy(part, part, x_send.at[0]).wait()
        part = d3.at[:, pl.ds(2 * qn, qn)]
        pltpu.make_async_copy(part, part, x_send.at[1]).wait()

    @pl.when(side == 1)
    def _():
        part = y3.at[:, pl.ds(2 * qn, qn)]
        pltpu.make_async_copy(part, part, x_send.at[0]).wait()
        part = d3.at[:, pl.ds(0, 2 * qn)]
        pltpu.make_async_copy(part, part, x_send.at[1]).wait()

    for n, name in enumerate(("wrow", "wall", "grecv", "srecv", "crecv", "nrecv")):
        sent = s[name].at[pl.ds(0, s[name].shape[0] - 1)]
        pltpu.make_async_copy(sent, sent, misc_send.at[n]).wait()


def step_kernel(direct, *refs):
    if direct:
        fins, refs = refs[0:2], refs[2:]
    red_ref, nrm_ref, w_ref, m1_ref, m2_ref, gain_ref, gm_ref, gv_ref, bias_ref, bm_ref, bv_ref = refs[:11]
    refs = refs[11:]
    if direct:
        bigs, refs = refs[0:2], refs[2:11] + refs[11:]
        refs, (slot, stage, sem) = refs[:9], refs[9:]
        _, crops, half, rl, gc, width = fins[0].shape
        cpd = 2 * gc
        copies = []

        def put(n, src, a, c, w, g):
            there = bigs[a].at[c, :, pl.ds(w * cpd + g * gc, gc), :]
            copy = pltpu.make_async_copy(src, there, sem.at[n])
            copy.start()
            copies.append(copy)

        blocks = [(a, c, w) for w in range(half) for c in range(crops) for a in range(2)]
        for n, (a, c, w) in enumerate(blocks):
            put(n, fins[0].at[a, c, w], a, c, w, 0)
        for n, (a, c, w) in enumerate(blocks):
            for j in range(gc):
                stage[n % 2, pl.ds(j, rl, stride=gc), :] = fins[1][a, c, w, j].astype(F32)
            slot[n] = stage[n % 2].reshape(rl, gc, width).astype(BF)
            put(len(blocks) + n, slot.at[n], a, c, w, 1)
    nw_ref, n1_ref, n2_ref, ng_ref, ngm_ref, ngv_ref, nb_ref, nbm_ref, nbv_ref = refs
    width = gain_ref.shape[1]
    heads = bias_ref.shape[1]
    wval = w_ref[...]
    first, second, step_w = moments(wval, red_ref[0:5, :], m1_ref[...], m2_ref[...])
    spot = lax.broadcasted_iota(jnp.int32, (1, width), 1)
    place = lax.broadcasted_iota(jnp.int32, (5, 1), 0)
    value_sq = jnp.sum(jnp.where(spot == place, nrm_ref[...], 0.0), 1, keepdims=True)
    step_sq = jnp.sum(jnp.where(spot == place + 8, nrm_ref[...], 0.0), 1, keepdims=True)
    nw_ref[...] = wval - rate * (jnp.sqrt(value_sq) / jnp.sqrt(step_sq)) * step_w
    n1_ref[...] = first
    n2_ref[...] = second
    for row, n, own in (
        (5, width, (gain_ref, gm_ref, gv_ref, ng_ref, ngm_ref, ngv_ref)),
        (6, heads, (bias_ref, bm_ref, bv_ref, nb_ref, nbm_ref, nbv_ref)),
    ):
        val = own[0][...]
        first, second, step_v = moments(val, red_ref[row : row + 1, 0:n], own[1][...], own[2][...])
        ratio = jnp.sqrt(jnp.sum(val * val, 1, keepdims=True)) / jnp.sqrt(
            jnp.sum(step_v * step_v, 1, keepdims=True)
        )
        own[3][...] = val - rate * ratio * step_v
        own[4][...] = first
        own[5][...] = second
    if direct:
        for copy in copies:
            copy.wait()


def body(
    nrow,
    ncol,
    pair,
    cotangent,
    segments,
    lengths,
    weights,
    moment_one,
    moment_two,
    gain,
    gain_m,
    gain_v,
    chain_bias,
    bias_m,
    bias_v,
):
    crops, rl, cl, width = pair.shape
    heads = chain_bias.shape[0]
    half = nrow // 2
    qn = half * rl
    cpd = cl // half
    wr = weights.shape[1] // width
    slots = -(-8 // ncol)
    direct = cpd == 32 and rl % 16 == 0
    gc = 16 if direct else cpd
    groups = cpd // gc
    dims = (nrow, ncol, crops, cpd, gc, rl, width, heads, wr, direct)
    wtype = BF if wr % 16 == 0 else F32
    ring = AHEAD + LAG + 1
    hbm = pl.BlockSpec(memory_space=pl.ANY)
    vmem = pl.BlockSpec(memory_space=pltpu.VMEM)
    smem = pl.BlockSpec(memory_space=pltpu.SMEM)
    dma = pltpu.SemaphoreType.DMA
    held = (2, crops, half, gc, rl, width)
    outs = {"red": pltpu.VMEM((slots * ncol, wr * width), F32), "nrm": pltpu.VMEM((1, width), F32)}
    scratch = {
        "zin": pltpu.VMEM((cpd, crops, 2, half, rl, width), BF),
        "y3": pltpu.VMEM((cpd, 3 * qn, width), BF),
        "d3": pltpu.VMEM((cpd, 3 * qn, width), BF),
        "own": pltpu.VMEM((ring, 3 * qn, width), F32),
        "xring": pltpu.VMEM((ring, 2 * qn, width), F32),
        "iring": pltpu.VMEM((ring, 2 * qn, width), F32),
        "yring": pltpu.VMEM((ring, 2 * qn, width), BF),
        "prob": pltpu.VMEM((heads, 2 * qn, qn), BF),
        "rev": pltpu.VMEM((qn, qn), BF),
        "wtmp": pltpu.VMEM((8, wr, width), F32),
        "wsend": pltpu.VMEM((slots * ncol, wr, width), wtype),
        "wrow": pltpu.VMEM((nrow, slots, wr, width), wtype),
        "wall": pltpu.VMEM((ncol, nrow, slots, wr, width), wtype),
        "gsend": pltpu.VMEM((slots * ncol, width, width), F32),
        "grecv": pltpu.VMEM((ncol, slots, width, width), F32),
        "ssend": pltpu.VMEM((nrow, slots, wr, width), F32),
        "srecv": pltpu.VMEM((nrow, slots, wr, width), F32),
        "csend": pltpu.VMEM((slots, wr, width), F32),
        "crecv": pltpu.VMEM((ncol, slots, wr, width), F32),
        "nsend": pltpu.VMEM((1, width), F32),
        "nrecv": pltpu.VMEM((nrow, 1, width), F32),
        "wqg": pltpu.VMEM((width, 2 * width), BF),
        "wkv": pltpu.VMEM((width, 2 * width), BF),
        "wqg_t": pltpu.VMEM((2 * width, width), BF),
        "wkv_t": pltpu.VMEM((2 * width, width), BF),
        "w4": pltpu.VMEM((width, width), BF),
        "augk": pltpu.VMEM((crops, 2 * qn, width), BF),
        "augq": pltpu.VMEM((crops, heads, width, qn), BF),
        "hotk": pltpu.VMEM((crops, 16, 2 * qn), BF),
        "hotq": pltpu.VMEM((crops, 16, qn), BF),
        "dwqg_acc": pltpu.VMEM((2 * width, width), F32),
        "dwkv_acc": pltpu.VMEM((2 * width, width), F32),
        "dw4_acc": pltpu.VMEM((width, width), F32),
        "dg_acc": pltpu.VMEM((8, width), F32),
        "db_acc": pltpu.VMEM((heads, 8, qn), F32),
        "in_sem": dma((cpd,)),
        "y_sem": dma((cpd,)),
        "d_sem": dma((cpd,)),
        "send_sem": dma((groups,)),
        "ret_sem": dma((groups,)),
        "rsend_sem": dma((groups,)),
        "x_send": dma((2,)),
        "misc_recv": dma((6,)),
        "misc_send": dma((6,)),
    }
    if direct:
        sources = (pair, cotangent)
        outs["fin0"] = pltpu.VMEM((2, crops, half, rl, gc, width), BF)
        outs["col1"] = pltpu.VMEM(held, BF)
        scratch["col0"] = pltpu.VMEM(held, BF)
        scratch["raw"] = pltpu.VMEM((half, crops, 2, rl, gc, width), BF)
        scratch["sbuf"] = pltpu.VMEM((gc, crops, 2, half, rl, width), BF)
        scratch["stage"] = pltpu.VMEM((2, rl * gc, width), F32)
        scratch["raw_sem"] = dma((half, crops, 2))
    else:
        both = jnp.stack([pair, cotangent], 1).reshape(crops, 2, rl, half, cpd, width)
        sources = (jnp.transpose(both, (4, 0, 1, 3, 2, 5)), cotangent)
        outs["col0"] = pltpu.VMEM(held, BF)
    names = tuple(outs) + tuple(scratch)
    res1 = pl.pallas_call(
        functools.partial(main_kernel, dims, names),
        out_shape=tuple(outs.values()),
        in_specs=[hbm, hbm, vmem, smem, vmem, vmem, vmem, vmem, smem],
        out_specs=(vmem,) * len(outs),
        scratch_shapes=list(scratch.values()),
        compiler_params=pltpu.CompilerParams(
            collective_id=0, has_side_effects=True, vmem_limit_bytes=50 << 20
        ),
        name="column_attention",
    )(
        *(
            pltpu.with_memory_space_constraint(x, pltpu.HBM)
            for x in (
                *sources,
                segments,
                lengths,
                weights,
                moment_one,
                moment_two,
                gain.reshape(1, width),
                chain_bias,
            )
        )
    )
    res1 = dict(zip(outs, res1))
    small = (gain, gain_m, gain_v, chain_bias, bias_m, bias_v)
    ops = [res1["red"], res1["nrm"], weights, moment_one, moment_two] + [a.reshape(1, -1) for a in small]
    fin = jax.ShapeDtypeStruct(pair.shape, BF)
    bigs = [fin, fin] if direct else []
    count = 2 * crops * half
    res = pl.pallas_call(
        functools.partial(step_kernel, direct),
        out_shape=bigs
        + [jax.ShapeDtypeStruct(weights.shape, F32)] * 3
        + [jax.ShapeDtypeStruct((1, width), F32)] * 3
        + [jax.ShapeDtypeStruct((1, heads), F32)] * 3,
        in_specs=[vmem] * (len(bigs) + len(ops)),
        out_specs=[hbm] * len(bigs) + [vmem] * 9,
        scratch_shapes=[
            pltpu.VMEM((count, rl, gc, width), BF),
            pltpu.VMEM((2, rl * gc, width), F32),
            dma((2 * count,)),
        ]
        if direct
        else [],
        compiler_params=pltpu.CompilerParams(vmem_limit_bytes=16 << 20),
        name="lamb_step",
    )(*((res1["fin0"], res1["col1"]) if direct else ()), *ops)
    if direct:
        fins, res = res[:2], res[2:]
    else:
        back = res1["col0"].reshape(2, crops, cl, rl, width)
        fins = [jnp.swapaxes(back[a], 1, 2) for a in range(2)]
    return (*fins, *res[:3], *[a.reshape(-1) for a in res[3:]])


def solution(mesh):
    big = P(None, "row", "col", None)
    shard = P(None, "row")
    return jax.shard_map(
        functools.partial(body, mesh.shape["row"], mesh.shape["col"]),
        mesh=mesh,
        in_specs=(big, big, P(), P(), shard, shard, shard) + (P(),) * 6,
        out_specs=(big, big, shard, shard, shard) + (P(),) * 6,
        check_vma=False,
    )
```

time: 383 us -> 362 us (0.945)
  Pallas kernels: 378 us -> 361 us
    pallas_call x1, Pallas kernels: 374 us -> 355 us  [body(): pl.pallas_call(functools.partial(main_kernel, dims, names), out_shape=tup...]
where the time goes in v3:
time: 362 us
  Pallas kernels  361 us (100%)
    pallas_call x1, Pallas kernels, body(): pl.pallas_call(functools.partial(main_kernel, dims, names), out_shape=tup...  355 us

profile of v3, /device:TPU:0, one launch (start us, length us, event | category | flops | bytes accessed | tf_op | source)
XLA Modules:
  0.0 361.8 jit_solution(14294940971650565491)
XLA Ops:
  0.6 0.0 copy-start
  0.7 0.0 copy-start.1
  0.7 0.0 copy-start.2
  0.7 0.0 copy-start.3
  0.7 0.0 copy-start.4
  0.7 0.0 copy-start.5
  0.7 0.0 copy-start.6
  0.7 0.0 copy-start.7
  0.7 0.0 copy-start.8
  0.7 354.7 %column_attention.1 = (f32[8,2048]{1,0:T(8,128)S(1)}, f32[1,128]{1,0:T(1,128)S(1)}, bf16[2,2,4,64,16,128]{5,4,3,2,1,0:T(8,128)(2,1)S(1)}, bf16[2,2,4,16,64,128]{5,4,3,2,1,0:T(8,128)(2,1)S(1)}) custom-call(bf16[2,64,128,128]{3,2,1,0:T(8,128)(2,1)} %refs_0_.1, bf16[2,64,128,128]{3,2,1,0:T(8,128)(2,1)} %refs_1_.1, s32[2,512]{1,0:T(2,128)} %refs_2_.1, ...), custom_call_target="tpu_custom_call" | custom-call | tf_op jit(solution)/shard_map/column_attention/pallas_call | solution.py:725
  355.4 0.0 copy-done
  355.5 0.0 copy-done.1
  355.5 0.0 copy-done.2
  355.5 0.0 copy-done.3
  355.5 0.0 copy-done.4
  355.5 0.0 copy-done.5
  355.5 0.0 copy-done.6
  355.5 0.0 copy-done.7
  355.5 0.0 copy-done.8
  355.5 6.1 %lamb_step.1 = (bf16[2,64,128,128]{3,2,1,0:T(8,128)(2,1)}, bf16[2,64,128,128]{3,2,1,0:T(8,128)(2,1)}, f32[5,2048]{1,0:T(8,128)}, f32[5,2048]{1,0:T(8,128)}, f32[...) custom-call(bf16[2,2,4,64,16,128]{5,4,3,2,1,0:T(8,128)(2,1)S(1)} %ge, ...), custom_call_target="tpu_custom_call" | custom-call | tf_op jit(solution)/shard_map/lamb_step/pallas_call | solution.py:756
Async XLA Ops:
  0.6 354.8 %copy-start = (f32[5,2048]{1,0:T(8,128)S(1)}, f32[5,2048]{1,0:T(8,128)}, u32[]{:S(2)}) copy-start(f32[5,2048]{1,0:T(8,128)} %refs_4_.3) | copy-start | bytes 122884
  0.7 354.8 %copy-start.1 = (f32[5,2048]{1,0:T(8,128)S(1)}, f32[5,2048]{1,0:T(8,128)}, u32[]{:S(2)}) copy-start(f32[5,2048]{1,0:T(8,128)} %refs_5_.3) | copy-start | bytes 122884
  0.7 354.8 %copy-start.2 = (f32[5,2048]{1,0:T(8,128)S(1)}, f32[5,2048]{1,0:T(8,128)}, u32[]{:S(2)}) copy-start(f32[5,2048]{1,0:T(8,128)} %refs_6_.3) | copy-start | bytes 122884
  0.7 354.8 %copy-start.3 = (f32[128]{0:T(128)S(1)}, f32[128]{0:T(128)}, u32[]{:S(2)}) copy-start(f32[128]{0:T(128)} %param.20) | copy-start | bytes 1540
  0.7 354.8 %copy-start.4 = (f32[4]{0:T(128)S(1)}, f32[4]{0:T(128)}, u32[]{:S(2)}) copy-start(f32[4]{0:T(128)} %refs_8_.1) | copy-start | bytes 52
  0.7 354.8 %copy-start.5 = (f32[128]{0:T(128)S(1)}, f32[128]{0:T(128)}, u32[]{:S(2)}) copy-start(f32[128]{0:T(128)} %param.21) | copy-start | bytes 1540
  0.7 354.8 %copy-start.6 = (f32[128]{0:T(128)S(1)}, f32[128]{0:T(128)}, u32[]{:S(2)}) copy-start(f32[128]{0:T(128)} %param.22) | copy-start | bytes 1540
  0.7 354.8 %copy-start.7 = (f32[4]{0:T(128)S(1)}, f32[4]{0:T(128)}, u32[]{:S(2)}) copy-start(f32[4]{0:T(128)} %param.24) | copy-start | bytes 52
  0.7 354.8 %copy-start.8 = (f32[4]{0:T(128)S(1)}, f32[4]{0:T(128)}, u32[]{:S(2)}) copy-start(f32[4]{0:T(128)} %param.25) | copy-start | bytes 52

commit v4 on v3

--- a/solution.py
+++ b/solution.py
@@ -23,6 +23,7 @@
 LOG2E = math.log2(math.e)
 SEGS = 4
 LEAD, AHEAD, LAG = 8, 2, 2
+LIGHT = 24
 
 
 def dot(a, b, dims=((1,), (0,))):
@@ -38,7 +39,7 @@
     return xhat, inv, (xhat * gain).astype(BF)
 
 
-def attend(z, co, yown, yall, wqg_t, wkv, wkv_t, w4, wqg, augk, augq, hotk, hotq, e_ref, heads):
+def attend(z, co, yown, yall, wqg_t, wkv, wkv_t, w4, wqg, augk, augq, hotk, hotq, heads):
     qn, width = z[0].shape
     hsize = width // heads
     scale = 1.0 / math.sqrt(hsize)
@@ -58,39 +59,60 @@
         qT = projT[:width].astype(BF)
         gT = jax.nn.sigmoid(projT[width:])
         kaug = jnp.concatenate([k, augk[c]], 1)
-        heads_a, heads_r = [], []
+        row16 = lax.broadcasted_iota(jnp.int32, (16, 1), 0)
+        tile_k = jnp.concatenate([hotk[c][:4].astype(F32)] * 4, 0)
+        tile_q = jnp.concatenate([hotq[c][:4].astype(F32)] * 4, 0)
+        hk = [jnp.where(row16 // 4 == h, tile_k, 0.0).astype(BF) for h in range(heads)]
+        hq = [jnp.where(row16 // 4 == h, tile_q, 0.0) for h in range(heads)]
+        es = []
         for h in range(heads):
-            rows = slice(h * hsize, (h + 1) * hsize)
             qaug = jnp.concatenate([jnp.where(head_of == h, qT, jnp.zeros_like(qT)), augq[c][h]], 0)
             s = dot(kaug, qaug) * (scale * LOG2E)
             e = jnp.exp2(s - jnp.max(s, 0, keepdims=True)).astype(BF)
-            e_ref[h] = e
-            a = dot(jnp.concatenate([vT[rows], ones], 0), e)
-            r = 1.0 / a[hsize : hsize + 1]
-            heads_a.append(a[:hsize] * r)
-            heads_r.append(jnp.broadcast_to(r, (hsize, qn)))
-        aT = jnp.concatenate(heads_a, 0)
+            es.append(e)
+        e_all = jnp.concatenate(es, 0)
+        one_row = lax.broadcasted_iota(jnp.int32, (16, 1), 0)
+        lhs = [
+            jnp.concatenate(
+                [
+                    jnp.where(head_of == h, vT, jnp.zeros_like(vT)),
+                    jnp.broadcast_to(jnp.where(one_row == h, 1.0, 0.0).astype(BF), (16, 2 * qn)),
+                ],
+                0,
+            )
+            for h in range(heads)
+        ]
+        a = dot(jnp.concatenate(lhs, 1), e_all)
+        r = 1.0 / a[width : width + heads]
+        rb = jnp.concatenate([jnp.broadcast_to(r[h : h + 1], (hsize, qn)) for h in range(heads)], 0)
+        aT = a[:width] * rb
         oT = (aT * gT).astype(BF)
         outs.append(z[c] + dot(oT, w4, TN))
         dw4 = dw4 + dot(oT, co[c])
         doT = dot(w4, co[c], NT).astype(BF).astype(F32)
         daT = (doT * gT).astype(BF).astype(F32)
         dgT = (doT * aT * gT * (1.0 - gT)).astype(BF)
-        dnT = (daT * jnp.concatenate(heads_r, 0) * scale).astype(BF)
+        dnT = (daT * rb * scale).astype(BF)
         prod = aT * dnT.astype(F32)
-        dq, dk, dv = [], [], []
+        dss, dk, dv, lhs = [], [], [], []
+        dps = dot(v, jnp.concatenate([jnp.where(head_of == h, dnT, jnp.zeros_like(dnT)) for h in range(heads)], 1))
         for h in range(heads):
             rows = slice(h * hsize, (h + 1) * hsize)
             shift = jnp.sum(prod[rows], 0, keepdims=True)
-            masked = jnp.where(head_of == h, dnT, jnp.zeros_like(dnT))
-            e = e_ref[h]
-            ds = (e.astype(F32) * (dot(v, masked) - shift)).astype(BF)
-            x = dot(jnp.concatenate([kT[rows], hotk[c]], 0), ds)
-            dq.append(x[:hsize].astype(BF))
-            db[h] = db[h] + x[hsize : hsize + 8] * hotq[c][:8].astype(F32)
+            e = es[h]
+            ds = (e.astype(F32) * (dps[:, h * qn : (h + 1) * qn] - shift)).astype(BF)
+            dss.append(ds)
             dk.append(dot(qT[rows], ds, NT))
             dv.append(dot(dnT[rows], e, NT) * (1.0 / scale))
-        dqgT.append(jnp.concatenate(dq + [dgT], 0))
+            lhs.append(
+                jnp.concatenate(
+                    [jnp.where(head_of == h, kT, jnp.zeros_like(kT)), hk[h]], 0
+                )
+            )
+        x = dot(jnp.concatenate(lhs, 1), jnp.concatenate(dss, 0))
+        for h in range(heads):
+            db[h] = db[h] + (x[width : width + 16] * hq[h])[:8] + (x[width : width + 16] * hq[h])[8:]
+        dqgT.append(jnp.concatenate([x[:width].astype(BF), dgT], 0))
         dkv = jnp.concatenate(dk + dv, 0)
         dkA.append(dkv[:, :qn].astype(BF))
         dkP = dkv[:, qn:] if dkP is None else dkP + dkv[:, qn:]
@@ -116,7 +138,7 @@
 
 
 def main_kernel(dims, names, *refs):
-    nrow, ncol, crops, cpd, gc, rl, width, heads, wr, direct = dims
+    nrow, ncol, crops, light, heavy, rl, width, heads, wr, direct = dims
     pair_ref, cot_ref, seg_ref, len_ref, w_ref, m1_ref, m2_ref, gain_ref, bias_ref = refs[:9]
     srcs = (pair_ref, cot_ref)
     s = dict(zip(names, refs[9:]))
@@ -128,9 +150,9 @@
     red_ref, nrm_ref = s["red"], s["nrm"]
     half = nrow // 2
     qn = half * rl
-    groups = cpd // gc
+    gc = 16
     ring = xring.shape[0]
-    cols = [s["col%d" % g] for g in range(groups)]
+    cols = s["cols"]
     hsize = width // heads
     scale = 1.0 / math.sqrt(hsize)
     slots = s["wrow"].shape[1]
@@ -138,7 +160,24 @@
     mc = lax.axis_index("col")
     side = me // half
     place = lax.rem(me, half)
-    partner = (lax.rem(me + half, nrow), mc)
+
+    def rank_of(at_side, w):
+        return lax.rem(w + at_side * (half // 2), half)
+
+    def first_of(rank):
+        near_rank = rank - half // 2
+        return jnp.where(near_rank < 0, rank * light, (half // 2) * light + near_rank * heavy)
+
+    rank = rank_of(side, place)
+    is_heavy = rank >= half // 2
+    base = first_of(rank)
+    partner = ((1 - side) * half + rank_of(1 - side, rank), mc)
+
+    def active(heavy_one, n):
+        return heavy_one | (((n + 1) * light) // heavy > (n * light) // heavy)
+
+    def unit_of(heavy_one, n):
+        return jnp.where(heavy_one, n, (n * light) // heavy)
 
     def row_peer(d):
         return lax.rem(me + d, nrow)
@@ -152,22 +191,23 @@
     def device(w):
         return (side * half + w, mc)
 
-    def load_group(g):
-        def load(w, _):
-            first = pl.multiple_of(w * cpd, gc) + g * gc
-            for c in range(crops):
-                for a in range(2):
-                    pltpu.make_async_copy(
-                        srcs[a].at[c, :, pl.ds(pl.multiple_of(first, gc), gc), :],
-                        s["raw"].at[w, c, a],
-                        s["raw_sem"].at[w, c, a],
-                    ).start()
-            return 0
-
-        lax.fori_loop(0, half, load, 0)
+    def load_block(b, slot):
+        for c in range(crops):
+            for a in range(2):
+                pltpu.make_async_copy(
+                    srcs[a].at[c, :, pl.ds(b * gc, gc), :],
+                    s["raw"].at[slot, c, a],
+                    s["raw_sem"].at[slot, c, a],
+                ).start()
 
     if direct:
-        load_group(0)
+        starts = [r * light for r in range(half // 2)]
+        starts += [(half // 2) * light + r * heavy for r in range(half // 2)]
+        early = sorted({(x + n) // gc for x in starts for n in range(LEAD)})
+        order = early + [b for b in range(cols.shape[2] // gc) if b not in early]
+        nslot = s["raw"].shape[0]
+        for n in range(nslot):
+            load_block(order[n], n)
 
     barrier = pltpu.get_barrier_semaphore()
 
@@ -218,56 +258,57 @@
 
     exchange_row(lambda p: s["wsend"].at[pl.ds(mc * slots, slots)], s["wrow"], 0)
 
-    def column_of(u, w):
-        return s["sbuf"].at[lax.rem(u, gc), :, :, w] if direct else pair_ref.at[u, :, :, w]
-
-    def push_to(u, d):
-        w = near(d)
-        remote(column_of(u, w), zin.at[u, :, :, place], send_sem.at[u // gc], in_sem.at[u], device(w))
-
-    def push_column(u):
+    def column_of(col):
+        return s["sbuf"].at[col] if direct else pair_ref.at[col]
+
+    def push_turn(n):
         def to_peer(d, _):
-            push_to(u, d)
+            w = near(d)
+            there = rank_of(side, w)
+            to_heavy = there >= half // 2
+            u = unit_of(to_heavy, n)
+
+            @pl.when(active(to_heavy, n))
+            def _():
+                src = column_of(first_of(there) + u)
+                remote(src, zin.at[u, :, :, place], send_sem.at[0], in_sem.at[u], device(w))
+
             return 0
 
         lax.fori_loop(1, half, to_peer, 0)
-        if not direct:
-            pltpu.make_async_copy(column_of(u, place), zin.at[u, :, :, place], in_sem.at[u]).start()
-
-    def push_columns(first, last):
-        def at_column(u, _):
-            push_column(u)
+        mine = unit_of(is_heavy, n)
+
+        @pl.when(active(is_heavy, n))
+        def _():
+            src = column_of(base + mine)
+            pltpu.make_async_copy(src, zin.at[mine, :, :, place], in_sem.at[mine]).start()
+
+    def push_turns(first, last):
+        def at_turn(n, _):
+            push_turn(n)
             return 0
 
-        lax.fori_loop(first, last, at_column, 0)
-
-    def turn(g, w, mine):
+        lax.fori_loop(first, last, at_turn, 0)
+
+    def turn_block(n):
+        b, slot = order[n], n % nslot
         for c in range(crops):
             for a in range(2):
-                here = s["raw"].at[w, c, a]
-                pltpu.make_async_copy(here, here, s["raw_sem"].at[w, c, a]).wait()
-                s["stage"][a] = s["raw"][w, c, a].astype(F32).reshape(rl * gc, width)
+                here = s["raw"].at[slot, c, a]
+                pltpu.make_async_copy(here, here, s["raw_sem"].at[slot, c, a]).wait()
+                s["stage"][a] = s["raw"][slot, c, a].astype(F32).reshape(rl * gc, width)
                 for j in range(gc):
-                    turned = s["stage"][a, pl.ds(j, rl, stride=gc), :].astype(BF)
-                    if mine:
-                        zin[g * gc + j, c, a, w] = turned
-                    else:
-                        s["sbuf"][j, c, a, w] = turned
+                    s["sbuf"][b * gc + j, c, a] = s["stage"][a, pl.ds(j, rl, stride=gc), :].astype(BF)
+        if n + nslot < len(order):
+            load_block(order[n + nslot], slot)
 
     if direct:
-
-        def first_blocks(d, _):
-            turn(0, near(d), False)
-            push_to(0, d)
-            return 0
-
-        lax.fori_loop(1, half, first_blocks, 0)
-        turn(0, place, True)
-        push_columns(1, LEAD - AHEAD)
-        if groups > 1:
-            load_group(1)
-    else:
-        push_columns(0, min(LEAD - AHEAD, cpd))
+        for n in range(len(early)):
+            turn_block(n)
+    push_turns(0, LEAD - AHEAD)
+    if direct:
+        for n in range(len(early), len(order)):
+            turn_block(n)
 
     landed(s["wrow"], 0)
     exchange_col(lambda p: s["wrow"], s["wall"], 1)
@@ -316,10 +357,8 @@
 
     where_t = lax.broadcasted_iota(jnp.int32, (qn, 1), 0)
 
-    def prepare(u):
-        new = zin.at[u, :, :, pl.ds(0, half - 1)] if direct else zin.at[u]
-        pltpu.make_async_copy(new, new, in_sem.at[u]).wait()
-        at = lax.rem(u, ring)
+    def prepare(u, at):
+        pltpu.make_async_copy(zin.at[u], zin.at[u], in_sem.at[u]).wait()
         for c in range(crops):
             rows = slice(c * qn, (c + 1) * qn)
             xhat, inv, y = normed(zin[u, c, 0].astype(F32).reshape(qn, width), gain_ref[...])
@@ -342,22 +381,17 @@
             remote(part, part, x_send.at[0], y_sem.at[u], partner)
 
     def give(u, a):
-        g = u // gc
-        for n in range(groups):
-
-            @pl.when(g == n)
-            def _():
-                here = cols[n].at[a, :, place, u - n * gc]
-
-                def to_peer(d, _):
-                    w = near(d)
-                    remote(zin.at[u, :, a, w], here, rsend_sem.at[n], ret_sem.at[n], device(w))
-                    return 0
-
-                lax.fori_loop(1, half, to_peer, 0)
-                pltpu.make_async_copy(zin.at[u, :, a, place], here, ret_sem.at[n]).start()
-
-    def work(u):
+        here = cols.at[a, :, base + u]
+
+        def to_peer(d, _):
+            w = near(d)
+            remote(zin.at[u, :, a, w], here, rsend_sem.at[0], ret_sem.at[0], device(w))
+            return 0
+
+        lax.fori_loop(1, half, to_peer, 0)
+        pltpu.make_async_copy(zin.at[u, :, a, place], here, ret_sem.at[0]).start()
+
+    def work(u, at):
         @pl.when(side == 0)
         def _():
             part = y3.at[u, pl.ds(2 * qn, qn)]
@@ -368,7 +402,6 @@
             part = y3.at[u, pl.ds(0, 2 * qn)]
             pltpu.make_async_copy(part, part, y_sem.at[u]).wait()
 
-        at = lax.rem(u, ring)
         outs, dy_own, dy_all, dwqg, dwkv, dw4, db = attend(
             [zin[u, c, 0].astype(F32).reshape(qn, width) for c in range(crops)],
             [zin[u, c, 1].astype(F32).reshape(qn, width).astype(BF) for c in range(crops)],
@@ -383,7 +416,6 @@
             [[s["augq"][c, h] for h in range(heads)] for c in range(crops)],
             [s["hotk"][c] for c in range(crops)],
             [s["hotq"][c] for c in range(crops)],
-            s["prob"],
             heads,
         )
         s["dwqg_acc"][...] += dwqg
@@ -410,8 +442,7 @@
             part = d3.at[u, pl.ds(0, 2 * qn)]
             remote(part, part, x_send.at[1], d_sem.at[u], partner)
 
-    def finish(u):
-        at = lax.rem(u, ring)
+    def finish(u, at):
 
         @pl.when(side == 0)
         def _():
@@ -438,74 +469,22 @@
             zin[u, c, 1] = grad.reshape(half, rl, width).astype(BF)
         give(u, 1)
 
-    def refill():
-        sent = s["sbuf"].at[:, :, :, pl.ds(0, half - 1)]
-        pltpu.make_async_copy(sent, sent, send_sem.at[0]).wait()
-
-        def block(d, _):
-            turn(1, near(d), False)
-            return 0
-
-        lax.fori_loop(1, half, block, 0)
-        turn(1, place, True)
-
-    def turn_back():
-        pltpu.make_async_copy(cols[0], cols[0], ret_sem.at[0]).wait()
-
-        def block(w, _):
-            for c in range(crops):
-                for a in range(2):
-                    for j in range(gc):
-                        s["stage"][a, pl.ds(j, rl, stride=gc), :] = cols[0][a, c, w, j].astype(F32)
-                    s["fin0"][a, c, w] = s["stage"][a].reshape(rl, gc, width).astype(BF)
-            return 0
-
-        lax.fori_loop(0, half, block, 0)
-
-    turn_at = gc + LAG + 5
-    refill_at = gc - 5
-
     def step(n, _):
-        it = n - AHEAD
-        nxt = it + LEAD
-        limit = gc if direct else cpd
-
-        @pl.when(nxt < limit)
-        def _():
-            push_column(nxt)
-
-        if direct and groups > 1:
-
-            @pl.when(it == refill_at)
+        def at_turn(t, act):
+            @pl.when((t >= 0) & (t < heavy) & active(is_heavy, t))
             def _():
-                refill()
-                push_columns(gc, refill_at + LEAD + 1)
-
-            @pl.when((it > refill_at) & (nxt < cpd))
-            def _():
-                push_column(nxt)
-
-        @pl.when(it + AHEAD < cpd)
-        def _():
-            prepare(it + AHEAD)
-
-        @pl.when((it >= 0) & (it < cpd))
-        def _():
-            work(it)
-
-        @pl.when(it >= LAG)
-        def _():
-            finish(it - LAG)
-
-        if direct and groups > 1:
-
-            @pl.when(it == turn_at)
-            def _():
-                turn_back()
-
+                act(unit_of(is_heavy, t), lax.rem(t, ring))
+
+        @pl.when(n - AHEAD + LEAD < heavy)
+        def _():
+            push_turn(n - AHEAD + LEAD)
+
+        at_turn(n, prepare)
+        at_turn(n - AHEAD, work)
+        at_turn(n - AHEAD - LAG, finish)
         return 0
 
-    lax.fori_loop(0, cpd + AHEAD + LAG, step, 0)
+    lax.fori_loop(0, heavy + AHEAD + LAG, step, 0)
 
     gsend = s["gsend"]
     for k, (name, at) in enumerate((("dwqg_acc", 0), ("dwkv_acc", 0), ("dwkv_acc", 1), ("dwqg_acc", 1))):
@@ -542,29 +521,28 @@
     landed(s["nrecv"], 5)
     nrm_ref[...] = total_of(s["nrecv"], nrow)
 
-    most = pl.ds(0, half - 1)
-    for g in range(groups):
-        if not direct or g == groups - 1:
-            sent = s["sbuf"].at[:, :, :, most] if direct else pair_ref.at[:, :, :, most]
-            pltpu.make_async_copy(sent, sent, send_sem.at[g]).wait()
-        gone = cols[g].at[:, :, most]
-        pltpu.make_async_copy(gone, gone, rsend_sem.at[g]).wait()
-        if not direct or groups == 1 or g > 0:
-            pltpu.make_async_copy(cols[g], cols[g], ret_sem.at[g]).wait()
-
-    @pl.when(side == 0)
-    def _():
-        part = y3.at[:, pl.ds(0, 2 * qn)]
-        pltpu.make_async_copy(part, part, x_send.at[0]).wait()
-        part = d3.at[:, pl.ds(2 * qn, qn)]
-        pltpu.make_async_copy(part, part, x_send.at[1]).wait()
-
-    @pl.when(side == 1)
-    def _():
-        part = y3.at[:, pl.ds(2 * qn, qn)]
-        pltpu.make_async_copy(part, part, x_send.at[0]).wait()
-        part = d3.at[:, pl.ds(0, 2 * qn)]
-        pltpu.make_async_copy(part, part, x_send.at[1]).wait()
+    pltpu.make_async_copy(cols, cols, ret_sem.at[0]).wait()
+
+    def ended(count):
+        sent = s["sbuf"] if direct else pair_ref
+        sent = sent.at[pl.ds(0, cols.shape[2] - count)]
+        pltpu.make_async_copy(sent, sent, send_sem.at[0]).wait()
+        gone = zin.at[pl.ds(0, count), :, :, pl.ds(0, half - 1)]
+        pltpu.make_async_copy(gone, gone, rsend_sem.at[0]).wait()
+        for at_side, rows_y, rows_d in ((0, 2 * qn, qn), (1, qn, 2 * qn)):
+
+            @pl.when(side == at_side)
+            def _():
+                part = y3.at[pl.ds(0, count), pl.ds(0, rows_y)]
+                pltpu.make_async_copy(part, part, x_send.at[0]).wait()
+                part = d3.at[pl.ds(0, count), pl.ds(0, rows_d)]
+                pltpu.make_async_copy(part, part, x_send.at[1]).wait()
+
+    for kind, count in ((False, light), (True, heavy)):
+
+        @pl.when(is_heavy == kind)
+        def _():
+            ended(count)
 
     for n, name in enumerate(("wrow", "wall", "grecv", "srecv", "crecv", "nrecv")):
         sent = s[name].at[pl.ds(0, s[name].shape[0] - 1)]
@@ -573,30 +551,26 @@
 
 def step_kernel(direct, *refs):
     if direct:
-        fins, refs = refs[0:2], refs[2:]
+        cols, refs = refs[0], refs[1:]
     red_ref, nrm_ref, w_ref, m1_ref, m2_ref, gain_ref, gm_ref, gv_ref, bias_ref, bm_ref, bv_ref = refs[:11]
     refs = refs[11:]
     if direct:
         bigs, refs = refs[0:2], refs[2:11] + refs[11:]
         refs, (slot, stage, sem) = refs[:9], refs[9:]
-        _, crops, half, rl, gc, width = fins[0].shape
-        cpd = 2 * gc
+        _, crops, cl, rl, width = cols.shape
+        gc = 16
         copies = []
-
-        def put(n, src, a, c, w, g):
-            there = bigs[a].at[c, :, pl.ds(w * cpd + g * gc, gc), :]
-            copy = pltpu.make_async_copy(src, there, sem.at[n])
-            copy.start()
-            copies.append(copy)
-
-        blocks = [(a, c, w) for w in range(half) for c in range(crops) for a in range(2)]
-        for n, (a, c, w) in enumerate(blocks):
-            put(n, fins[0].at[a, c, w], a, c, w, 0)
-        for n, (a, c, w) in enumerate(blocks):
-            for j in range(gc):
-                stage[n % 2, pl.ds(j, rl, stride=gc), :] = fins[1][a, c, w, j].astype(F32)
-            slot[n] = stage[n % 2].reshape(rl, gc, width).astype(BF)
-            put(len(blocks) + n, slot.at[n], a, c, w, 1)
+        for b in range(cl // gc):
+            for c in range(crops):
+                for a in range(2):
+                    n = len(copies)
+                    for j in range(gc):
+                        stage[n % 2, pl.ds(j, rl, stride=gc), :] = cols[a, c, b * gc + j].astype(F32)
+                    slot[n] = stage[n % 2].reshape(rl, gc, width).astype(BF)
+                    there = bigs[a].at[c, :, pl.ds(b * gc, gc), :]
+                    copy = pltpu.make_async_copy(slot.at[n], there, sem.at[n])
+                    copy.start()
+                    copies.append(copy)
     nw_ref, n1_ref, n2_ref, ng_ref, ngm_ref, ngv_ref, nb_ref, nbm_ref, nbv_ref = refs
     width = gain_ref.shape[1]
     heads = bias_ref.shape[1]
@@ -647,30 +621,32 @@
     heads = chain_bias.shape[0]
     half = nrow // 2
     qn = half * rl
-    cpd = cl // half
     wr = weights.shape[1] // width
     slots = -(-8 // ncol)
-    direct = cpd == 32 and rl % 16 == 0
-    gc = 16 if direct else cpd
-    groups = cpd // gc
-    dims = (nrow, ncol, crops, cpd, gc, rl, width, heads, wr, direct)
+    direct = cl % 16 == 0 and rl % 16 == 0
+    pairs = cl // (half // 2)
+    light = LIGHT if direct and pairs == 64 else pairs // 2
+    heavy = pairs - light
+    dims = (nrow, ncol, crops, light, heavy, rl, width, heads, wr, direct)
     wtype = BF if wr % 16 == 0 else F32
     ring = AHEAD + LAG + 1
     hbm = pl.BlockSpec(memory_space=pl.ANY)
     vmem = pl.BlockSpec(memory_space=pltpu.VMEM)
     smem = pl.BlockSpec(memory_space=pltpu.SMEM)
     dma = pltpu.SemaphoreType.DMA
-    held = (2, crops, half, gc, rl, width)
-    outs = {"red": pltpu.VMEM((slots * ncol, wr * width), F32), "nrm": pltpu.VMEM((1, width), F32)}
+    outs = {
+        "red": pltpu.VMEM((slots * ncol, wr * width), F32),
+        "nrm": pltpu.VMEM((1, width), F32),
+        "cols": pltpu.VMEM((2, crops, cl, rl, width), BF),
+    }
     scratch = {
-        "zin": pltpu.VMEM((cpd, crops, 2, half, rl, width), BF),
-        "y3": pltpu.VMEM((cpd, 3 * qn, width), BF),
-        "d3": pltpu.VMEM((cpd, 3 * qn, width), BF),
+        "zin": pltpu.VMEM((heavy, crops, 2, half, rl, width), BF),
+        "y3": pltpu.VMEM((heavy, 3 * qn, width), BF),
+        "d3": pltpu.VMEM((heavy, 3 * qn, width), BF),
         "own": pltpu.VMEM((ring, 3 * qn, width), F32),
         "xring": pltpu.VMEM((ring, 2 * qn, width), F32),
         "iring": pltpu.VMEM((ring, 2 * qn, width), F32),
         "yring": pltpu.VMEM((ring, 2 * qn, width), BF),
-        "prob": pltpu.VMEM((heads, 2 * qn, qn), BF),
         "rev": pltpu.VMEM((qn, qn), BF),
         "wtmp": pltpu.VMEM((8, wr, width), F32),
         "wsend": pltpu.VMEM((slots * ncol, wr, width), wtype),
@@ -698,29 +674,24 @@
         "dw4_acc": pltpu.VMEM((width, width), F32),
         "dg_acc": pltpu.VMEM((8, width), F32),
         "db_acc": pltpu.VMEM((heads, 8, qn), F32),
-        "in_sem": dma((cpd,)),
-        "y_sem": dma((cpd,)),
-        "d_sem": dma((cpd,)),
-        "send_sem": dma((groups,)),
-        "ret_sem": dma((groups,)),
-        "rsend_sem": dma((groups,)),
+        "in_sem": dma((heavy,)),
+        "y_sem": dma((heavy,)),
+        "d_sem": dma((heavy,)),
+        "send_sem": dma((1,)),
+        "ret_sem": dma((1,)),
+        "rsend_sem": dma((1,)),
         "x_send": dma((2,)),
         "misc_recv": dma((6,)),
         "misc_send": dma((6,)),
     }
     if direct:
         sources = (pair, cotangent)
-        outs["fin0"] = pltpu.VMEM((2, crops, half, rl, gc, width), BF)
-        outs["col1"] = pltpu.VMEM(held, BF)
-        scratch["col0"] = pltpu.VMEM(held, BF)
-        scratch["raw"] = pltpu.VMEM((half, crops, 2, rl, gc, width), BF)
-        scratch["sbuf"] = pltpu.VMEM((gc, crops, 2, half, rl, width), BF)
-        scratch["stage"] = pltpu.VMEM((2, rl * gc, width), F32)
-        scratch["raw_sem"] = dma((half, crops, 2))
+        scratch["raw"] = pltpu.VMEM((4, crops, 2, rl, 16, width), BF)
+        scratch["sbuf"] = pltpu.VMEM((cl, crops, 2, rl, width), BF)
+        scratch["stage"] = pltpu.VMEM((2, rl * 16, width), F32)
+        scratch["raw_sem"] = dma((4, crops, 2))
     else:
-        both = jnp.stack([pair, cotangent], 1).reshape(crops, 2, rl, half, cpd, width)
-        sources = (jnp.transpose(both, (4, 0, 1, 3, 2, 5)), cotangent)
-        outs["col0"] = pltpu.VMEM(held, BF)
+        sources = (jnp.transpose(jnp.stack([pair, cotangent], 1), (3, 0, 1, 2, 4)), cotangent)
     names = tuple(outs) + tuple(scratch)
     res1 = pl.pallas_call(
         functools.partial(main_kernel, dims, names),
@@ -729,7 +700,7 @@
         out_specs=(vmem,) * len(outs),
         scratch_shapes=list(scratch.values()),
         compiler_params=pltpu.CompilerParams(
-            collective_id=0, has_side_effects=True, vmem_limit_bytes=50 << 20
+            collective_id=0, has_side_effects=True, vmem_limit_bytes=54 << 20
         ),
         name="column_attention",
     )(
@@ -752,30 +723,29 @@
     ops = [res1["red"], res1["nrm"], weights, moment_one, moment_two] + [a.reshape(1, -1) for a in small]
     fin = jax.ShapeDtypeStruct(pair.shape, BF)
     bigs = [fin, fin] if direct else []
-    count = 2 * crops * half
+    count = 2 * crops * (cl // 16)
     res = pl.pallas_call(
         functools.partial(step_kernel, direct),
         out_shape=bigs
         + [jax.ShapeDtypeStruct(weights.shape, F32)] * 3
         + [jax.ShapeDtypeStruct((1, width), F32)] * 3
         + [jax.ShapeDtypeStruct((1, heads), F32)] * 3,
-        in_specs=[vmem] * (len(bigs) + len(ops)),
+        in_specs=[vmem] * (len(ops) + direct),
         out_specs=[hbm] * len(bigs) + [vmem] * 9,
         scratch_shapes=[
-            pltpu.VMEM((count, rl, gc, width), BF),
-            pltpu.VMEM((2, rl * gc, width), F32),
-            dma((2 * count,)),
+            pltpu.VMEM((count, rl, 16, width), BF),
+            pltpu.VMEM((2, rl * 16, width), F32),
+            dma((count,)),
         ]
         if direct
         else [],
-        compiler_params=pltpu.CompilerParams(vmem_limit_bytes=16 << 20),
+        compiler_params=pltpu.CompilerParams(vmem_limit_bytes=18 << 20),
         name="lamb_step",
-    )(*((res1["fin0"], res1["col1"]) if direct else ()), *ops)
+    )(*((res1["cols"],) if direct else ()), *ops)
     if direct:
         fins, res = res[:2], res[2:]
     else:
-        back = res1["col0"].reshape(2, crops, cl, rl, width)
-        fins = [jnp.swapaxes(back[a], 1, 2) for a in range(2)]
+        fins = [jnp.swapaxes(res1["cols"][a], 1, 2) for a in range(2)]
     return (*fins, *res[:3], *[a.reshape(-1) for a in res[3:]])
 
 

time: 362 us -> 331 us (0.914)
  Pallas kernels: 361 us -> 330 us
    pallas_call x1, Pallas kernels: 355 us -> 319 us  [body(): pl.pallas_call(functools.partial(main_kernel, dims, names), out_shape=tup...]
    pallas_call x1, Pallas kernels: 6.12 us -> 10.5 us  [body(): pl.pallas_call(functools.partial(step_kernel, direct), out_shape=bigs + [...]
where the time goes in v4:
time: 331 us
  Pallas kernels  330 us (100%)
    pallas_call x1, Pallas kernels, body(): pl.pallas_call(functools.partial(main_kernel, dims, names), out_shape=tup...  319 us
    pallas_call x1, Pallas kernels, body(): pl.pallas_call(functools.partial(step_kernel, direct), out_shape=bigs + [...  10.5 us

profile of v4, /device:TPU:0, one launch (start us, length us, event | category | flops | bytes accessed | tf_op | source)
XLA Modules:
  0.0 330.9 jit_solution(10863645339298817224)
XLA Ops:
  0.6 0.0 copy-start
  0.7 0.0 copy-start.1
  0.7 0.0 copy-start.2
  0.7 0.0 copy-start.3
  0.7 0.0 copy-start.4
  0.7 0.0 copy-start.5
  0.7 0.0 copy-start.6
  0.7 0.0 copy-start.7
  0.7 0.0 copy-start.8
  0.7 319.4 %column_attention.1 = (f32[8,2048]{1,0:T(8,128)S(1)}, f32[1,128]{1,0:T(1,128)S(1)}, bf16[2,2,128,64,128]{4,3,2,1,0:T(8,128)(2,1)S(1)}) custom-call(bf16[2,64,128,128]{3,2,1,0:T(8,128)(2,1)} %refs_0_.1, bf16[2,64,128,128]{3,2,1,0:T(8,128)(2,1)} %refs_1_.1, s32[2,512]{1,0:T(2,128)} %refs_2_.1, s32[2]{0:T(128)} %refs_3_.2, f32[5,2048]{1,0:T(8,128)} %refs_3_.3, ...), custom_call_target="tpu_custom_call" | custom-call | tf_op jit(solution)/shard_map/column_attention/pallas_call | solution.py:696
  320.1 0.0 copy-done
  320.2 0.0 copy-done.1
  320.2 0.0 copy-done.2
  320.2 0.0 copy-done.3
  320.2 0.0 copy-done.4
  320.2 0.0 copy-done.5
  320.2 0.0 copy-done.6
  320.2 0.0 copy-done.7
  320.2 0.0 copy-done.8
  320.2 10.5 %lamb_step.1 = (bf16[2,64,128,128]{3,2,1,0:T(8,128)(2,1)}, bf16[2,64,128,128]{3,2,1,0:T(8,128)(2,1)}, f32[5,2048]{1,0:T(8,128)}, f32[5,2048]{1,0:T(8,128)}, f32[...) custom-call(bf16[2,2,128,64,128]{4,3,2,1,0:T(8,128)(2,1)S(1)} %get-t, ...), custom_call_target="tpu_custom_call" | custom-call | tf_op jit(solution)/shard_map/lamb_step/pallas_call | solution.py:727
Async XLA Ops:
  0.6 319.5 %copy-start = (f32[5,2048]{1,0:T(8,128)S(1)}, f32[5,2048]{1,0:T(8,128)}, u32[]{:S(2)}) copy-start(f32[5,2048]{1,0:T(8,128)} %refs_3_.3) | copy-start | bytes 122884
  0.7 319.5 %copy-start.1 = (f32[5,2048]{1,0:T(8,128)S(1)}, f32[5,2048]{1,0:T(8,128)}, u32[]{:S(2)}) copy-start(f32[5,2048]{1,0:T(8,128)} %refs_4_.3) | copy-start | bytes 122884
  0.7 319.5 %copy-start.2 = (f32[5,2048]{1,0:T(8,128)S(1)}, f32[5,2048]{1,0:T(8,128)}, u32[]{:S(2)}) copy-start(f32[5,2048]{1,0:T(8,128)} %refs_5_.3) | copy-start | bytes 122884
  0.7 319.5 %copy-start.3 = (f32[128]{0:T(128)S(1)}, f32[128]{0:T(128)}, u32[]{:S(2)}) copy-start(f32[128]{0:T(128)} %param.20) | copy-start | bytes 1540
  0.7 319.5 %copy-start.4 = (f32[4]{0:T(128)S(1)}, f32[4]{0:T(128)}, u32[]{:S(2)}) copy-start(f32[4]{0:T(128)} %refs_8_.1) | copy-start | bytes 52
  0.7 319.5 %copy-start.5 = (f32[128]{0:T(128)S(1)}, f32[128]{0:T(128)}, u32[]{:S(2)}) copy-start(f32[128]{0:T(128)} %param.21) | copy-start | bytes 1540
  0.7 319.5 %copy-start.6 = (f32[128]{0:T(128)S(1)}, f32[128]{0:T(128)}, u32[]{:S(2)}) copy-start(f32[128]{0:T(128)} %param.22) | copy-start | bytes 1540
  0.7 319.5 %copy-start.7 = (f32[4]{0:T(128)S(1)}, f32[4]{0:T(128)}, u32[]{:S(2)}) copy-start(f32[4]{0:T(128)} %param.24) | copy-start | bytes 52
  0.7 319.5 %copy-start.8 = (f32[4]{0:T(128)S(1)}, f32[4]{0:T(128)}, u32[]{:S(2)}) copy-start(f32[4]{0:T(128)} %param.25) | copy-start | bytes 52

commit v5 on v4

--- a/solution.py
+++ b/solution.py
@@ -22,7 +22,7 @@
 TN = ((0,), (0,))
 LOG2E = math.log2(math.e)
 SEGS = 4
-LEAD, AHEAD, LAG = 8, 2, 2
+LEAD, AHEAD, LAG = 6, 3, 3
 LIGHT = 24
 
 
@@ -137,6 +137,18 @@
     return (first_new, second_new, step_dir)
 
 
+def early_blocks(light, heavy, half, gc):
+    late = set()
+    for r in range(half):
+        first = r * light if r < half // 2 else half // 2 * light + (r - half // 2) * heavy
+        count = light if r < half // 2 else heavy
+        for u in range(count):
+            turn = -(-((u + 1) * heavy) // count)
+            if turn > heavy - 8:
+                late.add((first + u) // gc)
+    return [b for b in range(half // 2 * (light + heavy) // gc) if b not in late]
+
+
 def main_kernel(dims, names, *refs):
     nrow, ncol, crops, light, heavy, rl, width, heads, wr, direct = dims
     pair_ref, cot_ref, seg_ref, len_ref, w_ref, m1_ref, m2_ref, gain_ref, bias_ref = refs[:9]
@@ -150,9 +162,10 @@
     red_ref, nrm_ref = s["red"], s["nrm"]
     half = nrow // 2
     qn = half * rl
-    gc = 16
+    gc = 16 if direct else half // 2 * (light + heavy)
     ring = xring.shape[0]
     cols = s["cols"]
+    nblocks = (half // 2 * (light + heavy)) // gc
     hsize = width // heads
     scale = 1.0 / math.sqrt(hsize)
     slots = s["wrow"].shape[1]
@@ -203,8 +216,11 @@
     if direct:
         starts = [r * light for r in range(half // 2)]
         starts += [(half // 2) * light + r * heavy for r in range(half // 2)]
-        early = sorted({(x + n) // gc for x in starts for n in range(LEAD)})
-        order = early + [b for b in range(cols.shape[2] // gc) if b not in early]
+        order = []
+        for x in starts[half // 2 :] + starts[: half // 2]:
+            order += [b for b in sorted({(x + n) // gc for n in range(LEAD)}) if b not in order]
+        order += [b for b in range(nblocks) if b not in order]
+        done_blocks = 0
         nslot = s["raw"].shape[0]
         for n in range(nslot):
             load_block(order[n], n)
@@ -302,19 +318,78 @@
         if n + nslot < len(order):
             load_block(order[n + nslot], slot)
 
+    def push_one(there, n):
+        to_heavy = there >= half // 2
+        u = unit_of(to_heavy, n)
+
+        @pl.when(active(to_heavy, n) & (there == rank))
+        def _():
+            src = column_of(base + u)
+            pltpu.make_async_copy(src, zin.at[u, :, :, place], in_sem.at[u]).start()
+
+        @pl.when(active(to_heavy, n) & (there != rank))
+        def _():
+            src = column_of(first_of(there) + u)
+            remote(src, zin.at[u, :, :, place], send_sem.at[0], in_sem.at[u], device(rank_of(side, there)))
+
     if direct:
-        for n in range(len(early)):
+        for there in list(range(half // 2, half)) + list(range(half // 2)):
+            for b in sorted({(starts[there] + n) // gc for n in range(LEAD)}):
+                if b in order[:done_blocks]:
+                    continue
+                turn_block(order.index(b))
+                done_blocks += 1
+            push_one(there, 0)
+        push_turns(1, LEAD)
+    else:
+        push_turns(0, LEAD)
+
+    back = lax.broadcasted_iota(jnp.int32, (qn, qn), 0) + lax.broadcasted_iota(jnp.int32, (qn, qn), 1)
+    s["rev"][...] = jnp.where(back == qn - 1, 1.0, 0.0).astype(BF)
+
+    where_t = lax.broadcasted_iota(jnp.int32, (qn, 1), 0)
+
+    def prepare(u, at):
+        pltpu.make_async_copy(zin.at[u], zin.at[u], in_sem.at[u]).wait()
+        for c in range(crops):
+            rows = slice(c * qn, (c + 1) * qn)
+            xhat, inv, y = normed(zin[u, c, 0].astype(F32).reshape(qn, width), gain_ref[...])
+            xring[at, rows, :] = xhat
+            iring[at, rows, :] = jnp.broadcast_to(inv, (qn, width))
+            yring[at, rows, :] = y
+
+        @pl.when(side == 0)
+        def _():
+            y3[u, 0 : 2 * qn, :] = yring[at]
+            part = y3.at[u, pl.ds(0, 2 * qn)]
+            remote(part, part, x_send.at[0], y_sem.at[u], partner)
+
+        @pl.when(side == 1)
+        def _():
+            y1 = dot(s["rev"][...], yring[at, qn : 2 * qn, :])
+            y0 = yring[at, 0:qn, :].astype(F32)
+            y3[u, 2 * qn : 3 * qn, :] = jnp.where(where_t < len_ref[0] - qn, y0, y1).astype(BF)
+            part = y3.at[u, pl.ds(2 * qn, qn)]
+            remote(part, part, x_send.at[0], y_sem.at[u], partner)
+
+    def at_turn(t, act):
+        @pl.when((t >= 0) & (t < heavy) & active(is_heavy, t))
+        def _():
+            act(unit_of(is_heavy, t), lax.rem(t, ring))
+
+    def early_turn(n, _):
+        at_turn(n, prepare)
+        return 0
+
+    lax.fori_loop(0, 1, early_turn, 0)
+    if direct:
+        for n in range(done_blocks, nblocks):
             turn_block(n)
-    push_turns(0, LEAD - AHEAD)
-    if direct:
-        for n in range(len(early), len(order)):
-            turn_block(n)
+    lax.fori_loop(1, AHEAD, early_turn, 0)
 
     landed(s["wrow"], 0)
     exchange_col(lambda p: s["wrow"], s["wall"], 1)
 
-    back = lax.broadcasted_iota(jnp.int32, (qn, qn), 0) + lax.broadcasted_iota(jnp.int32, (qn, qn), 1)
-    s["rev"][...] = jnp.where(back == qn - 1, 1.0, 0.0).astype(BF)
     lane = lax.broadcasted_iota(jnp.int32, (1, qn), 1)
     line = lax.broadcasted_iota(jnp.int32, (width, 1), 0)
     for c in range(crops):
@@ -355,41 +430,17 @@
             s[name][:, at * width : (at + 1) * width] = w.astype(BF)
             s[name + "_t"][at * width : (at + 1) * width, :] = jnp.transpose(w).astype(BF)
 
-    where_t = lax.broadcasted_iota(jnp.int32, (qn, 1), 0)
-
-    def prepare(u, at):
-        pltpu.make_async_copy(zin.at[u], zin.at[u], in_sem.at[u]).wait()
-        for c in range(crops):
-            rows = slice(c * qn, (c + 1) * qn)
-            xhat, inv, y = normed(zin[u, c, 0].astype(F32).reshape(qn, width), gain_ref[...])
-            xring[at, rows, :] = xhat
-            iring[at, rows, :] = jnp.broadcast_to(inv, (qn, width))
-            yring[at, rows, :] = y
-
-        @pl.when(side == 0)
-        def _():
-            y3[u, 0 : 2 * qn, :] = yring[at]
-            part = y3.at[u, pl.ds(0, 2 * qn)]
-            remote(part, part, x_send.at[0], y_sem.at[u], partner)
-
-        @pl.when(side == 1)
-        def _():
-            y1 = dot(s["rev"][...], yring[at, qn : 2 * qn, :])
-            y0 = yring[at, 0:qn, :].astype(F32)
-            y3[u, 2 * qn : 3 * qn, :] = jnp.where(where_t < len_ref[0] - qn, y0, y1).astype(BF)
-            part = y3.at[u, pl.ds(2 * qn, qn)]
-            remote(part, part, x_send.at[0], y_sem.at[u], partner)
-
     def give(u, a):
-        here = cols.at[a, :, base + u]
+        here = cols.at[a, :, pl.ds((base + u) * rl, rl)]
+        landing = ret_sem.at[(base + u) // gc]
 
         def to_peer(d, _):
             w = near(d)
-            remote(zin.at[u, :, a, w], here, rsend_sem.at[0], ret_sem.at[0], device(w))
+            remote(zin.at[u, :, a, w], here, rsend_sem.at[0], landing, device(w))
             return 0
 
         lax.fori_loop(1, half, to_peer, 0)
-        pltpu.make_async_copy(zin.at[u, :, a, place], here, ret_sem.at[0]).start()
+        pltpu.make_async_copy(zin.at[u, :, a, place], here, landing).start()
 
     def work(u, at):
         @pl.when(side == 0)
@@ -469,48 +520,72 @@
             zin[u, c, 1] = grad.reshape(half, rl, width).astype(BF)
         give(u, 1)
 
-    def step(n, _):
-        def at_turn(t, act):
-            @pl.when((t >= 0) & (t < heavy) & active(is_heavy, t))
-            def _():
-                act(unit_of(is_heavy, t), lax.rem(t, ring))
-
-        @pl.when(n - AHEAD + LEAD < heavy)
-        def _():
-            push_turn(n - AHEAD + LEAD)
-
-        at_turn(n, prepare)
-        at_turn(n - AHEAD, work)
-        at_turn(n - AHEAD - LAG, finish)
+    def step(it, _):
+        @pl.when(it + LEAD < heavy)
+        def _():
+            push_turn(it + LEAD)
+
+        at_turn(it + AHEAD, prepare)
+        at_turn(it, work)
+        at_turn(it - LAG, finish)
         return 0
 
-    lax.fori_loop(0, heavy + AHEAD + LAG, step, 0)
+    lax.fori_loop(0, heavy, step, 0)
+
+    def turn_back(b):
+        block = cols.at[:, :, pl.ds(b * gc * rl, gc * rl)]
+        pltpu.make_async_copy(block, block, ret_sem.at[b]).wait()
+        rows = slice(b * gc * rl, (b + 1) * gc * rl)
+        for c in range(crops):
+            for a in range(2):
+                for j in range(gc):
+                    at = (b * gc + j) * rl
+                    s["stage"][a, pl.ds(j, rl, stride=gc), :] = cols[a, c, at : at + rl, :].astype(F32)
+                cols[a, c, rows, :] = s["stage"][a].astype(BF)
+
+    soon = early_blocks(light, heavy, half, gc) if direct else []
 
     gsend = s["gsend"]
     for k, (name, at) in enumerate((("dwqg_acc", 0), ("dwkv_acc", 0), ("dwkv_acc", 1), ("dwqg_acc", 1))):
         gsend[k] = jnp.transpose(s[name][at * width : (at + 1) * width, :])
     gsend[4] = s["dw4_acc"][...]
-    gsend[5] = jnp.broadcast_to(s["dg_acc"][0:1], (width, width))
     spot = lax.broadcasted_iota(jnp.int32, (1, width), 1)
     dbias = jnp.zeros((1, width), F32)
     for h in range(heads):
         total_h = jnp.sum(jnp.sum(s["db_acc"][h], 0, keepdims=True), 1, keepdims=True)
         dbias = jnp.where(spot == h, total_h * (1.0 / scale), dbias)
     gsend[6] = jnp.broadcast_to(dbias, (width, width))
-    for k in range(7, slots * ncol):
+    for k in [5] + list(range(7, slots * ncol)):
         gsend[k] = jnp.zeros((width, width), F32)
     exchange_col(lambda p: gsend.at[pl.ds(p * slots, slots)], s["grecv"], 2)
+
+    def last_turn(t, _):
+        at_turn(t, finish)
+        return 0
+
+    lax.fori_loop(heavy - LAG, heavy, last_turn, 0)
+    s["vsend"][0] = s["dg_acc"][0:1]
+    exchange_row(lambda p: s["vsend"].at[0], s["vrow"], 6)
     landed(s["grecv"], 2)
     share = total_of(s["grecv"], ncol)
     for p in range(nrow):
         s["ssend"][p] = share[:, p * wr : (p + 1) * wr, :]
     exchange_row(lambda p: s["ssend"].at[p], s["srecv"], 3)
+    for b in soon[0::3]:
+        turn_back(b)
+    landed(s["vrow"], 6)
+    s["vsend"][1] = total_of(s["vrow"], nrow)
+    exchange_col(lambda p: s["vsend"].at[1], s["vcol"], 7)
     landed(s["srecv"], 3)
     s["csend"][...] = total_of(s["srecv"], nrow)
     exchange_col(lambda p: s["csend"], s["crecv"], 4)
+    for b in soon[1::3]:
+        turn_back(b)
     landed(s["crecv"], 4)
+    landed(s["vcol"], 7)
     for j in range(wr):
         red_ref[:, j * width : (j + 1) * width] = s["crecv"][:, :, j, :].reshape(slots * ncol, width)
+    red_ref[5:6, 0:width] = total_of(s["vcol"], ncol)
     wval = w_ref[...]
     step_w = moments(wval, red_ref[0:5, :], m1_ref[...], m2_ref[...])[2]
     row5 = lax.broadcasted_iota(jnp.int32, (5, 1), 0)
@@ -518,14 +593,19 @@
     squares += jnp.where(spot == row5 + 8, jnp.sum(step_w * step_w, 1, keepdims=True), 0.0)
     s["nsend"][...] = jnp.sum(squares, 0, keepdims=True)
     exchange_row(lambda p: s["nsend"], s["nrecv"], 5)
+    for b in soon[2::3]:
+        turn_back(b)
     landed(s["nrecv"], 5)
     nrm_ref[...] = total_of(s["nrecv"], nrow)
 
-    pltpu.make_async_copy(cols, cols, ret_sem.at[0]).wait()
+    for b in range(nblocks):
+        if b not in soon:
+            block = cols.at[:, :, pl.ds(b * gc * rl, gc * rl)]
+            pltpu.make_async_copy(block, block, ret_sem.at[b]).wait()
 
     def ended(count):
         sent = s["sbuf"] if direct else pair_ref
-        sent = sent.at[pl.ds(0, cols.shape[2] - count)]
+        sent = sent.at[pl.ds(0, half // 2 * (light + heavy) - count)]
         pltpu.make_async_copy(sent, sent, send_sem.at[0]).wait()
         gone = zin.at[pl.ds(0, count), :, :, pl.ds(0, half - 1)]
         pltpu.make_async_copy(gone, gone, rsend_sem.at[0]).wait()
@@ -544,33 +624,45 @@
         def _():
             ended(count)
 
-    for n, name in enumerate(("wrow", "wall", "grecv", "srecv", "crecv", "nrecv")):
+    for n, name in enumerate(
+        ("wrow", "wall", "grecv", "srecv", "crecv", "nrecv", "vrow", "vcol")
+    ):
         sent = s[name].at[pl.ds(0, s[name].shape[0] - 1)]
         pltpu.make_async_copy(sent, sent, misc_send.at[n]).wait()
 
 
-def step_kernel(direct, *refs):
+def step_kernel(direct, soon, *refs):
     if direct:
-        cols, refs = refs[0], refs[1:]
+        cols, blocks, refs = refs[0], refs[1], refs[2:]
     red_ref, nrm_ref, w_ref, m1_ref, m2_ref, gain_ref, gm_ref, gv_ref, bias_ref, bm_ref, bv_ref = refs[:11]
     refs = refs[11:]
     if direct:
         bigs, refs = refs[0:2], refs[2:11] + refs[11:]
         refs, (slot, stage, sem) = refs[:9], refs[9:]
-        _, crops, cl, rl, width = cols.shape
+        _, crops, _, width = cols.shape
+        _, rl, cl, _ = bigs[0].shape
         gc = 16
         copies = []
-        for b in range(cl // gc):
+
+        def put(src, a, c, b):
+            n = len(copies)
+            copy = pltpu.make_async_copy(src, bigs[a].at[c, :, pl.ds(b * gc, gc), :], sem.at[n])
+            copy.start()
+            copies.append(copy)
+
+        for b in soon:
             for c in range(crops):
                 for a in range(2):
-                    n = len(copies)
+                    put(blocks.at[a, c, b], a, c, b)
+        late = [b for b in range(cl // gc) if b not in soon]
+        for n, b in enumerate(late):
+            for c in range(crops):
+                for a in range(2):
                     for j in range(gc):
-                        stage[n % 2, pl.ds(j, rl, stride=gc), :] = cols[a, c, b * gc + j].astype(F32)
-                    slot[n] = stage[n % 2].reshape(rl, gc, width).astype(BF)
-                    there = bigs[a].at[c, :, pl.ds(b * gc, gc), :]
-                    copy = pltpu.make_async_copy(slot.at[n], there, sem.at[n])
-                    copy.start()
-                    copies.append(copy)
+                        at = (b * gc + j) * rl
+                        stage[a, pl.ds(j, rl, stride=gc), :] = cols[a, c, at : at + rl, :].astype(F32)
+                    slot[n, c, a] = stage[a].reshape(rl, gc, width).astype(BF)
+                    put(slot.at[n, c, a], a, c, b)
     nw_ref, n1_ref, n2_ref, ng_ref, ngm_ref, ngv_ref, nb_ref, nbm_ref, nbv_ref = refs
     width = gain_ref.shape[1]
     heads = bias_ref.shape[1]
@@ -637,7 +729,7 @@
     outs = {
         "red": pltpu.VMEM((slots * ncol, wr * width), F32),
         "nrm": pltpu.VMEM((1, width), F32),
-        "cols": pltpu.VMEM((2, crops, cl, rl, width), BF),
+        "cols": pltpu.VMEM((2, crops, cl * rl, width), BF),
     }
     scratch = {
         "zin": pltpu.VMEM((heavy, crops, 2, half, rl, width), BF),
@@ -658,6 +750,9 @@
         "srecv": pltpu.VMEM((nrow, slots, wr, width), F32),
         "csend": pltpu.VMEM((slots, wr, width), F32),
         "crecv": pltpu.VMEM((ncol, slots, wr, width), F32),
+        "vsend": pltpu.VMEM((2, 1, width), F32),
+        "vrow": pltpu.VMEM((nrow, 1, width), F32),
+        "vcol": pltpu.VMEM((ncol, 1, width), F32),
         "nsend": pltpu.VMEM((1, width), F32),
         "nrecv": pltpu.VMEM((nrow, 1, width), F32),
         "wqg": pltpu.VMEM((width, 2 * width), BF),
@@ -678,11 +773,11 @@
         "y_sem": dma((heavy,)),
         "d_sem": dma((heavy,)),
         "send_sem": dma((1,)),
-        "ret_sem": dma((1,)),
+        "ret_sem": dma((cl // 16 if direct else 1,)),
         "rsend_sem": dma((1,)),
         "x_send": dma((2,)),
-        "misc_recv": dma((6,)),
-        "misc_send": dma((6,)),
+        "misc_recv": dma((8,)),
+        "misc_send": dma((8,)),
     }
     if direct:
         sources = (pair, cotangent)
@@ -724,16 +819,20 @@
     fin = jax.ShapeDtypeStruct(pair.shape, BF)
     bigs = [fin, fin] if direct else []
     count = 2 * crops * (cl // 16)
+    soon = early_blocks(light, heavy, half, 16) if direct else []
+    turned = ()
+    if direct:
+        turned = (res1["cols"], res1["cols"].reshape(2, crops, cl // 16, rl, 16, width))
     res = pl.pallas_call(
-        functools.partial(step_kernel, direct),
+        functools.partial(step_kernel, direct, soon),
         out_shape=bigs
         + [jax.ShapeDtypeStruct(weights.shape, F32)] * 3
         + [jax.ShapeDtypeStruct((1, width), F32)] * 3
         + [jax.ShapeDtypeStruct((1, heads), F32)] * 3,
-        in_specs=[vmem] * (len(ops) + direct),
+        in_specs=[vmem] * (len(ops) + len(turned)),
         out_specs=[hbm] * len(bigs) + [vmem] * 9,
         scratch_shapes=[
-            pltpu.VMEM((count, rl, 16, width), BF),
+            pltpu.VMEM((cl // 16 - len(soon), crops, 2, rl, 16, width), BF),
             pltpu.VMEM((2, rl * 16, width), F32),
             dma((count,)),
         ]
@@ -741,11 +840,11 @@
         else [],
         compiler_params=pltpu.CompilerParams(vmem_limit_bytes=18 << 20),
         name="lamb_step",
-    )(*((res1["cols"],) if direct else ()), *ops)
+    )(*turned, *ops)
     if direct:
         fins, res = res[:2], res[2:]
     else:
-        fins = [jnp.swapaxes(res1["cols"][a], 1, 2) for a in range(2)]
+        fins = [jnp.swapaxes(res1["cols"][a].reshape(crops, cl, rl, width), 1, 2) for a in range(2)]
     return (*fins, *res[:3], *[a.reshape(-1) for a in res[3:]])
 
 

time: 331 us -> 319 us (0.964)
  Pallas kernels: 330 us -> 317 us
    pallas_call x1, Pallas kernels: 319 us -> 311 us  [body(): pl.pallas_call(functools.partial(main_kernel, dims, names), out_shape=tup...]
    pallas_call x1, Pallas kernels: 10.5 us -> 6.12 us  [body(): pl.pallas_call(functools.partial(step_kernel, direct, soon), out_shape=bi...]
where the time goes in v5:
time: 319 us; the launch traced here: 318 us
  Pallas kernels  317 us (99%)
    pallas_call x1, Pallas kernels, body(): pl.pallas_call(functools.partial(main_kernel, dims, names), out_shape=tup...  311 us

profile of v5, /device:TPU:0, one launch (start us, length us, event | category | flops | bytes accessed | tf_op | source)
XLA Modules:
  0.0 318.5 jit_solution(9504023277523774099)
XLA Ops:
  0.6 0.0 copy-start
  0.7 0.0 copy-start.1
  0.7 0.0 copy-start.2
  0.7 0.0 copy-start.3
  0.7 0.0 copy-start.4
  0.7 0.0 copy-start.5
  0.7 0.0 copy-start.6
  0.7 0.0 copy-start.7
  0.7 0.0 copy-start.8
  0.7 311.3 %column_attention.1 = (f32[8,2048]{1,0:T(8,128)S(1)}, f32[1,128]{1,0:T(1,128)S(1)}, bf16[2,2,8192,128]{3,2,1,0:T(8,128)(2,1)S(1)}) custom-call(bf16[2,64,128,128]{3,2,1,0:T(8,128)(2,1)} %refs_0_.1, bf16[2,64,128,128]{3,2,1,0:T(8,128)(2,1)} %refs_1_.1, s32[2,512]{1,0:T(2,128)} %refs_2_.1, s32[2]{0:T(128)} %refs_3_.1, f32[5,2048]{1,0:T(8,128)} %refs_4_.3, ...), custom_call_target="tpu_custom_call" | custom-call | tf_op jit(solution)/shard_map/column_attention/pallas_call | solution.py:791
  312.1 0.0 copy-done
  312.1 0.0 copy-done.1
  312.1 0.0 copy-done.2
  312.1 0.0 copy-done.3
  312.1 0.0 copy-done.4
  312.1 0.0 copy-done.5
  312.1 0.0 copy-done.6
  312.1 0.0 copy-done.7
  312.1 0.0 copy-done.8
  312.2 6.1 %lamb_step.1 = (bf16[2,64,128,128]{3,2,1,0:T(8,128)(2,1)}, bf16[2,64,128,128]{3,2,1,0:T(8,128)(2,1)}, f32[5,2048]{1,0:T(8,128)}, f32[5,2048]{1,0:T(8,128)}, f32[...) custom-call(bf16[2,2,8192,128]{3,2,1,0:T(8,128)(2,1)S(1)} %get-tuple, ...), custom_call_target="tpu_custom_call" | custom-call | tf_op jit(solution)/shard_map/lamb_step/pallas_call | solution.py:826
Async XLA Ops:
  0.6 311.4 %copy-start = (f32[5,2048]{1,0:T(8,128)S(1)}, f32[5,2048]{1,0:T(8,128)}, u32[]{:S(2)}) copy-start(f32[5,2048]{1,0:T(8,128)} %refs_4_.3) | copy-start | bytes 122884
  0.7 311.4 %copy-start.1 = (f32[5,2048]{1,0:T(8,128)S(1)}, f32[5,2048]{1,0:T(8,128)}, u32[]{:S(2)}) copy-start(f32[5,2048]{1,0:T(8,128)} %refs_5_.3) | copy-start | bytes 122884
  0.7 311.4 %copy-start.2 = (f32[5,2048]{1,0:T(8,128)S(1)}, f32[5,2048]{1,0:T(8,128)}, u32[]{:S(2)}) copy-start(f32[5,2048]{1,0:T(8,128)} %refs_6_.3) | copy-start | bytes 122884
  0.7 311.4 %copy-start.3 = (f32[128]{0:T(128)S(1)}, f32[128]{0:T(128)}, u32[]{:S(2)}) copy-start(f32[128]{0:T(128)} %param.20) | copy-start | bytes 1540
  0.7 311.4 %copy-start.4 = (f32[4]{0:T(128)S(1)}, f32[4]{0:T(128)}, u32[]{:S(2)}) copy-start(f32[4]{0:T(128)} %refs_8_.1) | copy-start | bytes 52
  0.7 311.4 %copy-start.5 = (f32[128]{0:T(128)S(1)}, f32[128]{0:T(128)}, u32[]{:S(2)}) copy-start(f32[128]{0:T(128)} %param.21) | copy-start | bytes 1540
  0.7 311.4 %copy-start.6 = (f32[128]{0:T(128)S(1)}, f32[128]{0:T(128)}, u32[]{:S(2)}) copy-start(f32[128]{0:T(128)} %param.22) | copy-start | bytes 1540
  0.7 311.4 %copy-start.7 = (f32[4]{0:T(128)S(1)}, f32[4]{0:T(128)}, u32[]{:S(2)}) copy-start(f32[4]{0:T(128)} %param.24) | copy-start | bytes 52
  0.7 311.4 %copy-start.8 = (f32[4]{0:T(128)S(1)}, f32[4]{0:T(128)}, u32[]{:S(2)}) copy-start(f32[4]{0:T(128)} %param.25) | copy-start | bytes 52

commit v6 on v5

--- a/solution.py
+++ b/solution.py
@@ -22,8 +22,8 @@
 TN = ((0,), (0,))
 LOG2E = math.log2(math.e)
 SEGS = 4
-LEAD, AHEAD, LAG = 6, 3, 3
-LIGHT = 24
+EARLY, LEAD, AHEAD, LAG = 2, 4, 2, 3
+LIGHT = 22
 
 
 def dot(a, b, dims=((1,), (0,))):
@@ -43,77 +43,85 @@
     qn, width = z[0].shape
     hsize = width // heads
     scale = 1.0 / math.sqrt(hsize)
+    head_of = lax.broadcasted_iota(jnp.int32, (width, 1), 0) // hsize
+    row16 = lax.broadcasted_iota(jnp.int32, (16, 1), 0)
+    packed = slice(2 * qn, 3 * qn)
+
+    def spread(xT, last):
+        parts = [jnp.where(head_of == h, xT, jnp.zeros_like(xT)) for h in range(heads)]
+        if last is not None:
+            parts = [jnp.concatenate([p, x], 0) for p, x in zip(parts, last)]
+        return jnp.concatenate(parts, 1)
+
     kv = dot(yall, wkv).astype(BF)
     kvT = dot(wkv_t, yall, NT).astype(BF)
-    head_of = lax.broadcasted_iota(jnp.int32, (width, 1), 0) // hsize
-    ones = jnp.ones((16, 2 * qn), BF)
+    ones = [jnp.broadcast_to(jnp.where(row16 == h, 1.0, 0.0).astype(BF), (16, 2 * qn)) for h in range(heads)]
+    crops = range(2)
+    st = [{} for c in crops]
+    for c in crops:
+        t = st[c]
+        first = slice(c * qn, (c + 1) * qn)
+        t["k"] = jnp.concatenate([kv[first, :width], kv[packed, :width]], 0)
+        t["v"] = jnp.concatenate([kv[first, width:], kv[packed, width:]], 0)
+        bothT = jnp.concatenate([kvT[:, first], kvT[:, packed]], 1)
+        t["kT"], t["vT"] = bothT[:width], bothT[width:]
+        projT = dot(wqg_t, yown[c], NT)
+        t["qT"] = projT[:width].astype(BF)
+        t["gT"] = jax.nn.sigmoid(projT[width:])
+        t["doT"] = dot(w4, co[c], NT).astype(BF).astype(F32)
     outs, dqgT, dkA, dkP = [], [], [], None
     dw4, db = 0.0, [0.0] * heads
-    for c in range(2):
-        first, packed = slice(c * qn, (c + 1) * qn), slice(2 * qn, 3 * qn)
-        k = jnp.concatenate([kv[first, :width], kv[packed, :width]], 0)
-        v = jnp.concatenate([kv[first, width:], kv[packed, width:]], 0)
-        bothT = jnp.concatenate([kvT[:, first], kvT[:, packed]], 1)
-        kT, vT = bothT[:width], bothT[width:]
-        projT = dot(wqg_t, yown[c], NT)
-        qT = projT[:width].astype(BF)
-        gT = jax.nn.sigmoid(projT[width:])
-        kaug = jnp.concatenate([k, augk[c]], 1)
-        row16 = lax.broadcasted_iota(jnp.int32, (16, 1), 0)
+    for c in crops:
+        t = st[c]
+        kaug = jnp.concatenate([t["k"], augk[c]], 1)
+        es = []
+        for h in range(heads):
+            qaug = jnp.concatenate([jnp.where(head_of == h, t["qT"], jnp.zeros_like(t["qT"])), augq[c][h]], 0)
+            s = dot(kaug, qaug) * (scale * LOG2E)
+            es.append(jnp.exp2(s - jnp.max(s, 0, keepdims=True)).astype(BF))
+        t["es"] = es
+        t = st[c]
+        a = dot(spread(t["vT"], ones), jnp.concatenate(t["es"], 0))
+        r = 1.0 / a[width : width + heads]
+        t["rb"] = jnp.concatenate([jnp.broadcast_to(r[h : h + 1], (hsize, qn)) for h in range(heads)], 0)
+        t["aT"] = a[:width] * t["rb"]
+        t = st[c]
+        aT, gT, doT = t["aT"], t["gT"], t["doT"]
+        daT = (doT * gT).astype(BF).astype(F32)
+        t["dgT"] = (doT * aT * gT * (1.0 - gT)).astype(BF)
+        t["dnT"] = (daT * t["rb"] * scale).astype(BF)
+        prod = aT * t["dnT"].astype(F32)
+        t["shift"] = [jnp.sum(prod[h * hsize : (h + 1) * hsize], 0, keepdims=True) for h in range(heads)]
+    for c in crops:
+        t = st[c]
+        dps = dot(t["v"], spread(t["dnT"], None))
+        t["ds"] = [
+            (t["es"][h].astype(F32) * (dps[:, h * qn : (h + 1) * qn] - t["shift"][h])).astype(BF) for h in range(heads)
+        ]
+        t = st[c]
+        oT = (t["aT"] * t["gT"]).astype(BF)
+        outs.append(z[c] + dot(oT, w4, TN))
+        dw4 = dw4 + dot(oT, co[c])
+        t = st[c]
+        dk, dv = [], []
+        for h in range(heads):
+            rows = slice(h * hsize, (h + 1) * hsize)
+            dk.append(dot(t["qT"][rows], t["ds"][h], NT))
+            dv.append(dot(t["dnT"][rows], t["es"][h], NT) * (1.0 / scale))
+        t["dkv"] = jnp.concatenate(dk + dv, 0)
+    for c in crops:
+        t = st[c]
         tile_k = jnp.concatenate([hotk[c][:4].astype(F32)] * 4, 0)
         tile_q = jnp.concatenate([hotq[c][:4].astype(F32)] * 4, 0)
-        hk = [jnp.where(row16 // 4 == h, tile_k, 0.0).astype(BF) for h in range(heads)]
-        hq = [jnp.where(row16 // 4 == h, tile_q, 0.0) for h in range(heads)]
-        es = []
+        x = dot(
+            spread(t["kT"], [jnp.where(row16 // 4 == h, tile_k, 0.0).astype(BF) for h in range(heads)]),
+            jnp.concatenate(t["ds"], 0),
+        )
         for h in range(heads):
-            qaug = jnp.concatenate([jnp.where(head_of == h, qT, jnp.zeros_like(qT)), augq[c][h]], 0)
-            s = dot(kaug, qaug) * (scale * LOG2E)
-            e = jnp.exp2(s - jnp.max(s, 0, keepdims=True)).astype(BF)
-            es.append(e)
-        e_all = jnp.concatenate(es, 0)
-        one_row = lax.broadcasted_iota(jnp.int32, (16, 1), 0)
-        lhs = [
-            jnp.concatenate(
-                [
-                    jnp.where(head_of == h, vT, jnp.zeros_like(vT)),
-                    jnp.broadcast_to(jnp.where(one_row == h, 1.0, 0.0).astype(BF), (16, 2 * qn)),
-                ],
-                0,
-            )
-            for h in range(heads)
-        ]
-        a = dot(jnp.concatenate(lhs, 1), e_all)
-        r = 1.0 / a[width : width + heads]
-        rb = jnp.concatenate([jnp.broadcast_to(r[h : h + 1], (hsize, qn)) for h in range(heads)], 0)
-        aT = a[:width] * rb
-        oT = (aT * gT).astype(BF)
-        outs.append(z[c] + dot(oT, w4, TN))
-        dw4 = dw4 + dot(oT, co[c])
-        doT = dot(w4, co[c], NT).astype(BF).astype(F32)
-        daT = (doT * gT).astype(BF).astype(F32)
-        dgT = (doT * aT * gT * (1.0 - gT)).astype(BF)
-        dnT = (daT * rb * scale).astype(BF)
-        prod = aT * dnT.astype(F32)
-        dss, dk, dv, lhs = [], [], [], []
-        dps = dot(v, jnp.concatenate([jnp.where(head_of == h, dnT, jnp.zeros_like(dnT)) for h in range(heads)], 1))
-        for h in range(heads):
-            rows = slice(h * hsize, (h + 1) * hsize)
-            shift = jnp.sum(prod[rows], 0, keepdims=True)
-            e = es[h]
-            ds = (e.astype(F32) * (dps[:, h * qn : (h + 1) * qn] - shift)).astype(BF)
-            dss.append(ds)
-            dk.append(dot(qT[rows], ds, NT))
-            dv.append(dot(dnT[rows], e, NT) * (1.0 / scale))
-            lhs.append(
-                jnp.concatenate(
-                    [jnp.where(head_of == h, kT, jnp.zeros_like(kT)), hk[h]], 0
-                )
-            )
-        x = dot(jnp.concatenate(lhs, 1), jnp.concatenate(dss, 0))
-        for h in range(heads):
-            db[h] = db[h] + (x[width : width + 16] * hq[h])[:8] + (x[width : width + 16] * hq[h])[8:]
-        dqgT.append(jnp.concatenate([x[:width].astype(BF), dgT], 0))
-        dkv = jnp.concatenate(dk + dv, 0)
+            part = jnp.where(row16 // 4 == h, x[width : width + 16] * tile_q, 0.0)
+            db[h] = db[h] + part[:8] + part[8:]
+        dqgT.append(jnp.concatenate([x[:width].astype(BF), t["dgT"]], 0))
+        dkv = t["dkv"]
         dkA.append(dkv[:, :qn].astype(BF))
         dkP = dkv[:, qn:] if dkP is None else dkP + dkv[:, qn:]
     dqgT = jnp.concatenate(dqgT, 1)
@@ -137,15 +145,19 @@
     return (first_new, second_new, step_dir)
 
 
+def blocks_of(rank, units, light, heavy, half, gc):
+    far = rank < half // 2
+    first = rank * light if far else half // 2 * light + (rank - half // 2) * heavy
+    count = light if far else heavy
+    return sorted({(first + (count - 1 - u if rank % 2 else u)) // gc for u in units if u < count})
+
+
 def early_blocks(light, heavy, half, gc):
     late = set()
     for r in range(half):
-        first = r * light if r < half // 2 else half // 2 * light + (r - half // 2) * heavy
         count = light if r < half // 2 else heavy
-        for u in range(count):
-            turn = -(-((u + 1) * heavy) // count)
-            if turn > heavy - 8:
-                late.add((first + u) // gc)
+        units = [u for u in range(count) if -(-((u + 1) * heavy) // count) > heavy - 8]
+        late |= set(blocks_of(r, units, light, heavy, half, gc))
     return [b for b in range(half // 2 * (light + heavy) // gc) if b not in late]
 
 
@@ -181,9 +193,12 @@
         near_rank = rank - half // 2
         return jnp.where(near_rank < 0, rank * light, (half // 2) * light + near_rank * heavy)
 
+    def column_at(there, u):
+        count = jnp.where(there < half // 2, light, heavy)
+        return first_of(there) + jnp.where(lax.rem(there, 2) == 1, count - 1 - u, u)
+
     rank = rank_of(side, place)
     is_heavy = rank >= half // 2
-    base = first_of(rank)
     partner = ((1 - side) * half + rank_of(1 - side, rank), mc)
 
     def active(heavy_one, n):
@@ -214,11 +229,10 @@
                 ).start()
 
     if direct:
-        starts = [r * light for r in range(half // 2)]
-        starts += [(half // 2) * light + r * heavy for r in range(half // 2)]
+        needs = [blocks_of(r, range(LEAD), light, heavy, half, gc) for r in range(half)]
         order = []
-        for x in starts[half // 2 :] + starts[: half // 2]:
-            order += [b for b in sorted({(x + n) // gc for n in range(LEAD)}) if b not in order]
+        for need in needs[half // 2 :] + needs[: half // 2]:
+            order += [b for b in need if b not in order]
         order += [b for b in range(nblocks) if b not in order]
         done_blocks = 0
         nslot = s["raw"].shape[0]
@@ -270,7 +284,7 @@
         pltpu.make_async_copy(dst, dst, misc_recv.at[n]).wait()
 
     def total_of(ref, n):
-        return lax.fori_loop(1, n, lambda r, t: t + ref[r], ref[0])
+        return lax.fori_loop(1, n, lambda r, t: t + ref[r].astype(F32), ref[0].astype(F32))
 
     exchange_row(lambda p: s["wsend"].at[pl.ds(mc * slots, slots)], s["wrow"], 0)
 
@@ -286,7 +300,7 @@
 
             @pl.when(active(to_heavy, n))
             def _():
-                src = column_of(first_of(there) + u)
+                src = column_of(column_at(there, u))
                 remote(src, zin.at[u, :, :, place], send_sem.at[0], in_sem.at[u], device(w))
 
             return 0
@@ -296,7 +310,7 @@
 
         @pl.when(active(is_heavy, n))
         def _():
-            src = column_of(base + mine)
+            src = column_of(column_at(rank, mine))
             pltpu.make_async_copy(src, zin.at[mine, :, :, place], in_sem.at[mine]).start()
 
     def push_turns(first, last):
@@ -324,23 +338,24 @@
 
         @pl.when(active(to_heavy, n) & (there == rank))
         def _():
-            src = column_of(base + u)
+            src = column_of(column_at(rank, u))
             pltpu.make_async_copy(src, zin.at[u, :, :, place], in_sem.at[u]).start()
 
         @pl.when(active(to_heavy, n) & (there != rank))
         def _():
-            src = column_of(first_of(there) + u)
+            src = column_of(column_at(there, u))
             remote(src, zin.at[u, :, :, place], send_sem.at[0], in_sem.at[u], device(rank_of(side, there)))
 
     if direct:
         for there in list(range(half // 2, half)) + list(range(half // 2)):
-            for b in sorted({(starts[there] + n) // gc for n in range(LEAD)}):
+            for b in needs[there]:
                 if b in order[:done_blocks]:
                     continue
                 turn_block(order.index(b))
                 done_blocks += 1
-            push_one(there, 0)
-        push_turns(1, LEAD)
+            for n in range(EARLY):
+                push_one(there, n)
+        push_turns(EARLY, LEAD)
     else:
         push_turns(0, LEAD)
 
@@ -431,8 +446,9 @@
             s[name + "_t"][at * width : (at + 1) * width, :] = jnp.transpose(w).astype(BF)
 
     def give(u, a):
-        here = cols.at[a, :, pl.ds((base + u) * rl, rl)]
-        landing = ret_sem.at[(base + u) // gc]
+        col = column_at(rank, u)
+        here = cols.at[a, :, pl.ds(col * rl, rl)]
+        landing = ret_sem.at[col // gc]
 
         def to_peer(d, _):
             w = near(d)
@@ -474,10 +490,6 @@
         s["dw4_acc"][...] += dw4
         for h in range(heads):
             s["db_acc"][h] += db[h]
-        for c in range(crops):
-            zin[u, c, 0] = outs[c].reshape(half, rl, width).astype(BF)
-        give(u, 0)
-
         @pl.when(side == 0)
         def _():
             own[at, 0 : 2 * qn, :] = dy_own + dy_all[0 : 2 * qn]
@@ -492,6 +504,10 @@
             d3[u, 0 : 2 * qn, :] = dy_all[0 : 2 * qn].astype(BF)
             part = d3.at[u, pl.ds(0, 2 * qn)]
             remote(part, part, x_send.at[1], d_sem.at[u], partner)
+
+        for c in range(crops):
+            zin[u, c, 0] = outs[c].reshape(half, rl, width).astype(BF)
+        give(u, 0)
 
     def finish(u, at):
 
@@ -521,11 +537,12 @@
         give(u, 1)
 
     def step(it, _):
+        at_turn(it + AHEAD, prepare)
+
         @pl.when(it + LEAD < heavy)
         def _():
             push_turn(it + LEAD)
 
-        at_turn(it + AHEAD, prepare)
         at_turn(it, work)
         at_turn(it - LAG, finish)
         return 0
@@ -547,16 +564,15 @@
 
     gsend = s["gsend"]
     for k, (name, at) in enumerate((("dwqg_acc", 0), ("dwkv_acc", 0), ("dwkv_acc", 1), ("dwqg_acc", 1))):
-        gsend[k] = jnp.transpose(s[name][at * width : (at + 1) * width, :])
-    gsend[4] = s["dw4_acc"][...]
+        gsend[k] = jnp.transpose(s[name][at * width : (at + 1) * width, :]).astype(gsend.dtype)
+    gsend[4] = s["dw4_acc"][...].astype(gsend.dtype)
     spot = lax.broadcasted_iota(jnp.int32, (1, width), 1)
     dbias = jnp.zeros((1, width), F32)
     for h in range(heads):
         total_h = jnp.sum(jnp.sum(s["db_acc"][h], 0, keepdims=True), 1, keepdims=True)
         dbias = jnp.where(spot == h, total_h * (1.0 / scale), dbias)
-    gsend[6] = jnp.broadcast_to(dbias, (width, width))
-    for k in [5] + list(range(7, slots * ncol)):
-        gsend[k] = jnp.zeros((width, width), F32)
+    for k in range(5, slots * ncol):
+        gsend[k] = jnp.zeros((width, width), gsend.dtype)
     exchange_col(lambda p: gsend.at[pl.ds(p * slots, slots)], s["grecv"], 2)
 
     def last_turn(t, _):
@@ -564,12 +580,13 @@
         return 0
 
     lax.fori_loop(heavy - LAG, heavy, last_turn, 0)
-    s["vsend"][0] = s["dg_acc"][0:1]
+    s["vsend"][0, 0:1, :] = s["dg_acc"][0:1]
+    s["vsend"][0, 1:2, :] = dbias
     exchange_row(lambda p: s["vsend"].at[0], s["vrow"], 6)
     landed(s["grecv"], 2)
     share = total_of(s["grecv"], ncol)
     for p in range(nrow):
-        s["ssend"][p] = share[:, p * wr : (p + 1) * wr, :]
+        s["ssend"][p] = share[:, p * wr : (p + 1) * wr, :].astype(s["ssend"].dtype)
     exchange_row(lambda p: s["ssend"].at[p], s["srecv"], 3)
     for b in soon[0::3]:
         turn_back(b)
@@ -585,7 +602,7 @@
     landed(s["vcol"], 7)
     for j in range(wr):
         red_ref[:, j * width : (j + 1) * width] = s["crecv"][:, :, j, :].reshape(slots * ncol, width)
-    red_ref[5:6, 0:width] = total_of(s["vcol"], ncol)
+    red_ref[5:7, 0:width] = total_of(s["vcol"], ncol)
     wval = w_ref[...]
     step_w = moments(wval, red_ref[0:5, :], m1_ref[...], m2_ref[...])[2]
     row5 = lax.broadcasted_iota(jnp.int32, (5, 1), 0)
@@ -744,15 +761,15 @@
         "wsend": pltpu.VMEM((slots * ncol, wr, width), wtype),
         "wrow": pltpu.VMEM((nrow, slots, wr, width), wtype),
         "wall": pltpu.VMEM((ncol, nrow, slots, wr, width), wtype),
-        "gsend": pltpu.VMEM((slots * ncol, width, width), F32),
-        "grecv": pltpu.VMEM((ncol, slots, width, width), F32),
-        "ssend": pltpu.VMEM((nrow, slots, wr, width), F32),
-        "srecv": pltpu.VMEM((nrow, slots, wr, width), F32),
+        "gsend": pltpu.VMEM((slots * ncol, width, width), wtype),
+        "grecv": pltpu.VMEM((ncol, slots, width, width), wtype),
+        "ssend": pltpu.VMEM((nrow, slots, wr, width), wtype),
+        "srecv": pltpu.VMEM((nrow, slots, wr, width), wtype),
         "csend": pltpu.VMEM((slots, wr, width), F32),
         "crecv": pltpu.VMEM((ncol, slots, wr, width), F32),
-        "vsend": pltpu.VMEM((2, 1, width), F32),
-        "vrow": pltpu.VMEM((nrow, 1, width), F32),
-        "vcol": pltpu.VMEM((ncol, 1, width), F32),
+        "vsend": pltpu.VMEM((2, 2, width), F32),
+        "vrow": pltpu.VMEM((nrow, 2, width), F32),
+        "vcol": pltpu.VMEM((ncol, 2, width), F32),
         "nsend": pltpu.VMEM((1, width), F32),
         "nrecv": pltpu.VMEM((nrow, 1, width), F32),
         "wqg": pltpu.VMEM((width, 2 * width), BF),
@@ -781,10 +798,10 @@
     }
     if direct:
         sources = (pair, cotangent)
-        scratch["raw"] = pltpu.VMEM((4, crops, 2, rl, 16, width), BF)
+        scratch["raw"] = pltpu.VMEM((3, crops, 2, rl, 16, width), BF)
         scratch["sbuf"] = pltpu.VMEM((cl, crops, 2, rl, width), BF)
         scratch["stage"] = pltpu.VMEM((2, rl * 16, width), F32)
-        scratch["raw_sem"] = dma((4, crops, 2))
+        scratch["raw_sem"] = dma((3, crops, 2))
     else:
         sources = (jnp.transpose(jnp.stack([pair, cotangent], 1), (3, 0, 1, 2, 4)), cotangent)
     names = tuple(outs) + tuple(scratch)
@@ -795,7 +812,7 @@
         out_specs=(vmem,) * len(outs),
         scratch_shapes=list(scratch.values()),
         compiler_params=pltpu.CompilerParams(
-            collective_id=0, has_side_effects=True, vmem_limit_bytes=54 << 20
+            collective_id=0, has_side_effects=True, vmem_limit_bytes=55 << 20
         ),
         name="column_attention",
     )(

time: 319 us -> 312 us (0.978)
  Pallas kernels: 317 us -> 310 us
    pallas_call x1, Pallas kernels: 311 us -> 305 us  [body(): pl.pallas_call(functools.partial(main_kernel, dims, names), out_shape=tup...]
where the time goes in v6:
time: 312 us; the launch traced here: 311 us
  Pallas kernels  310 us (99%)
    pallas_call x1, Pallas kernels, body(): pl.pallas_call(functools.partial(main_kernel, dims, names), out_shape=tup...  305 us

profile of v6, /device:TPU:0, one launch (start us, length us, event | category | flops | bytes accessed | tf_op | source)
XLA Modules:
  0.0 311.4 jit_solution(464080961554461730)
XLA Ops:
  0.6 0.0 copy-start
  0.7 0.0 copy-start.1
  0.7 0.0 copy-start.2
  0.7 0.0 copy-start.3
  0.7 0.0 copy-start.4
  0.7 0.0 copy-start.5
  0.7 0.0 copy-start.6
  0.7 0.0 copy-start.7
  0.7 0.0 copy-start.8
  0.7 305.4 %column_attention.1 = (f32[8,2048]{1,0:T(8,128)S(1)}, f32[1,128]{1,0:T(1,128)S(1)}, bf16[2,2,8192,128]{3,2,1,0:T(8,128)(2,1)S(1)}) custom-call(bf16[2,64,128,128]{3,2,1,0:T(8,128)(2,1)} %refs_0_.1, bf16[2,64,128,128]{3,2,1,0:T(8,128)(2,1)} %refs_1_.1, s32[2,512]{1,0:T(2,128)} %refs_2_.1, s32[2]{0:T(128)} %refs_3_.1, f32[5,2048]{1,0:T(8,128)} %refs_4_.3, ...), custom_call_target="tpu_custom_call" | custom-call | tf_op jit(solution)/shard_map/column_attention/pallas_call | solution.py:808
  306.2 0.0 copy-done
  306.2 0.0 copy-done.1
  306.2 0.0 copy-done.2
  306.2 0.0 copy-done.3
  306.2 0.0 copy-done.4
  306.2 0.0 copy-done.5
  306.2 0.0 copy-done.6
  306.2 0.0 copy-done.7
  306.2 0.0 copy-done.8
  306.3 5.0 %lamb_step.1 = (bf16[2,64,128,128]{3,2,1,0:T(8,128)(2,1)}, bf16[2,64,128,128]{3,2,1,0:T(8,128)(2,1)}, f32[5,2048]{1,0:T(8,128)}, f32[5,2048]{1,0:T(8,128)}, f32[...) custom-call(bf16[2,2,8192,128]{3,2,1,0:T(8,128)(2,1)S(1)} %get-tuple, ...), custom_call_target="tpu_custom_call" | custom-call | tf_op jit(solution)/shard_map/lamb_step/pallas_call | solution.py:843
Async XLA Ops:
  0.6 305.5 %copy-start = (f32[5,2048]{1,0:T(8,128)S(1)}, f32[5,2048]{1,0:T(8,128)}, u32[]{:S(2)}) copy-start(f32[5,2048]{1,0:T(8,128)} %refs_4_.3) | copy-start | bytes 122884
  0.7 305.5 %copy-start.1 = (f32[5,2048]{1,0:T(8,128)S(1)}, f32[5,2048]{1,0:T(8,128)}, u32[]{:S(2)}) copy-start(f32[5,2048]{1,0:T(8,128)} %refs_5_.3) | copy-start | bytes 122884
  0.7 305.5 %copy-start.2 = (f32[5,2048]{1,0:T(8,128)S(1)}, f32[5,2048]{1,0:T(8,128)}, u32[]{:S(2)}) copy-start(f32[5,2048]{1,0:T(8,128)} %refs_6_.3) | copy-start | bytes 122884
  0.7 305.5 %copy-start.3 = (f32[128]{0:T(128)S(1)}, f32[128]{0:T(128)}, u32[]{:S(2)}) copy-start(f32[128]{0:T(128)} %param.20) | copy-start | bytes 1540
  0.7 305.5 %copy-start.4 = (f32[4]{0:T(128)S(1)}, f32[4]{0:T(128)}, u32[]{:S(2)}) copy-start(f32[4]{0:T(128)} %refs_8_.1) | copy-start | bytes 52
  0.7 305.5 %copy-start.5 = (f32[128]{0:T(128)S(1)}, f32[128]{0:T(128)}, u32[]{:S(2)}) copy-start(f32[128]{0:T(128)} %param.21) | copy-start | bytes 1540
  0.7 305.5 %copy-start.6 = (f32[128]{0:T(128)S(1)}, f32[128]{0:T(128)}, u32[]{:S(2)}) copy-start(f32[128]{0:T(128)} %param.22) | copy-start | bytes 1540
  0.7 305.5 %copy-start.7 = (f32[4]{0:T(128)S(1)}, f32[4]{0:T(128)}, u32[]{:S(2)}) copy-start(f32[4]{0:T(128)} %param.24) | copy-start | bytes 52
  0.7 305.5 %copy-start.8 = (f32[4]{0:T(128)S(1)}, f32[4]{0:T(128)}, u32[]{:S(2)}) copy-start(f32[4]{0:T(128)} %param.25) | copy-start | bytes 52

commit v7 on v6

--- a/solution.py
+++ b/solution.py
@@ -156,7 +156,7 @@
     late = set()
     for r in range(half):
         count = light if r < half // 2 else heavy
-        units = [u for u in range(count) if -(-((u + 1) * heavy) // count) > heavy - 8]
+        units = [u for u in range(count) if -(-((u + 1) * heavy) // count) > heavy - 6]
         late |= set(blocks_of(r, units, light, heavy, half, gc))
     return [b for b in range(half // 2 * (light + heavy) // gc) if b not in late]
 

time: 312 us -> 311 us (level)
  no operation moved by 1% of the time
where the time goes in v7:
time: 311 us
  Pallas kernels  310 us (100%)
    pallas_call x1, Pallas kernels, body(): pl.pallas_call(functools.partial(main_kernel, dims, names), out_shape=tup...  305 us

profile of v7, /device:TPU:0, one launch (start us, length us, event | category | flops | bytes accessed | tf_op | source)
XLA Modules:
  0.0 310.7 jit_solution(17176301828776155601)
XLA Ops:
  0.6 0.0 copy-start
  0.7 0.0 copy-start.1
  0.7 0.0 copy-start.2
  0.7 0.0 copy-start.3
  0.7 0.0 copy-start.4
  0.7 0.0 copy-start.5
  0.7 0.0 copy-start.6
  0.7 0.0 copy-start.7
  0.7 0.0 copy-start.8
  0.7 305.4 %column_attention.1 = (f32[8,2048]{1,0:T(8,128)S(1)}, f32[1,128]{1,0:T(1,128)S(1)}, bf16[2,2,8192,128]{3,2,1,0:T(8,128)(2,1)S(1)}) custom-call(bf16[2,64,128,128]{3,2,1,0:T(8,128)(2,1)} %refs_0_.1, bf16[2,64,128,128]{3,2,1,0:T(8,128)(2,1)} %refs_1_.1, s32[2,512]{1,0:T(2,128)} %refs_2_.1, s32[2]{0:T(128)} %refs_3_.1, f32[5,2048]{1,0:T(8,128)} %refs_4_.3, ...), custom_call_target="tpu_custom_call" | custom-call | tf_op jit(solution)/shard_map/column_attention/pallas_call | solution.py:808
  306.2 0.0 copy-done
  306.2 0.0 copy-done.1
  306.2 0.0 copy-done.2
  306.2 0.0 copy-done.3
  306.2 0.0 copy-done.4
  306.2 0.0 copy-done.5
  306.2 0.0 copy-done.6
  306.2 0.0 copy-done.7
  306.2 0.0 copy-done.8
  306.3 4.2 %lamb_step.1 = (bf16[2,64,128,128]{3,2,1,0:T(8,128)(2,1)}, bf16[2,64,128,128]{3,2,1,0:T(8,128)(2,1)}, f32[5,2048]{1,0:T(8,128)}, f32[5,2048]{1,0:T(8,128)}, f32[...) custom-call(bf16[2,2,8192,128]{3,2,1,0:T(8,128)(2,1)S(1)} %get-tuple, ...), custom_call_target="tpu_custom_call" | custom-call | tf_op jit(solution)/shard_map/lamb_step/pallas_call | solution.py:843
Async XLA Ops:
  0.6 305.5 %copy-start = (f32[5,2048]{1,0:T(8,128)S(1)}, f32[5,2048]{1,0:T(8,128)}, u32[]{:S(2)}) copy-start(f32[5,2048]{1,0:T(8,128)} %refs_4_.3) | copy-start | bytes 122884
  0.7 305.5 %copy-start.1 = (f32[5,2048]{1,0:T(8,128)S(1)}, f32[5,2048]{1,0:T(8,128)}, u32[]{:S(2)}) copy-start(f32[5,2048]{1,0:T(8,128)} %refs_5_.3) | copy-start | bytes 122884
  0.7 305.5 %copy-start.2 = (f32[5,2048]{1,0:T(8,128)S(1)}, f32[5,2048]{1,0:T(8,128)}, u32[]{:S(2)}) copy-start(f32[5,2048]{1,0:T(8,128)} %refs_6_.3) | copy-start | bytes 122884
  0.7 305.5 %copy-start.3 = (f32[128]{0:T(128)S(1)}, f32[128]{0:T(128)}, u32[]{:S(2)}) copy-start(f32[128]{0:T(128)} %param.20) | copy-start | bytes 1540
  0.7 305.5 %copy-start.4 = (f32[4]{0:T(128)S(1)}, f32[4]{0:T(128)}, u32[]{:S(2)}) copy-start(f32[4]{0:T(128)} %refs_8_.1) | copy-start | bytes 52
  0.7 305.5 %copy-start.5 = (f32[128]{0:T(128)S(1)}, f32[128]{0:T(128)}, u32[]{:S(2)}) copy-start(f32[128]{0:T(128)} %param.21) | copy-start | bytes 1540
  0.7 305.5 %copy-start.6 = (f32[128]{0:T(128)S(1)}, f32[128]{0:T(128)}, u32[]{:S(2)}) copy-start(f32[128]{0:T(128)} %param.22) | copy-start | bytes 1540
  0.7 305.5 %copy-start.7 = (f32[4]{0:T(128)S(1)}, f32[4]{0:T(128)}, u32[]{:S(2)}) copy-start(f32[4]{0:T(128)} %param.24) | copy-start | bytes 52
  0.7 305.5 %copy-start.8 = (f32[4]{0:T(128)S(1)}, f32[4]{0:T(128)}, u32[]{:S(2)}) copy-start(f32[4]{0:T(128)} %param.25) | copy-start | bytes 52

commit v8 on v7

--- a/solution.py
+++ b/solution.py
@@ -22,7 +22,7 @@
 TN = ((0,), (0,))
 LOG2E = math.log2(math.e)
 SEGS = 4
-EARLY, LEAD, AHEAD, LAG = 2, 4, 2, 3
+EARLY, LEAD, AHEAD, LAG = 3, 4, 2, 3
 LIGHT = 22
 
 

time: 311 us -> 312 us (level)
  no operation moved by 1% of the time
where the time goes in v8:
time: 312 us
  Pallas kernels  311 us (100%)
    pallas_call x1, Pallas kernels, body(): pl.pallas_call(functools.partial(main_kernel, dims, names), out_shape=tup...  307 us

profile of v8, /device:TPU:0, one launch (start us, length us, event | category | flops | bytes accessed | tf_op | source)
XLA Modules:
  0.0 312.0 jit_solution(14755910991398259734)
XLA Ops:
  0.6 0.0 copy-start
  0.7 0.0 copy-start.1
  0.7 0.0 copy-start.2
  0.7 0.0 copy-start.3
  0.7 0.0 copy-start.4
  0.7 0.0 copy-start.5
  0.7 0.0 copy-start.6
  0.7 0.0 copy-start.7
  0.7 0.0 copy-start.8
  0.7 306.7 %column_attention.1 = (f32[8,2048]{1,0:T(8,128)S(1)}, f32[1,128]{1,0:T(1,128)S(1)}, bf16[2,2,8192,128]{3,2,1,0:T(8,128)(2,1)S(1)}) custom-call(bf16[2,64,128,128]{3,2,1,0:T(8,128)(2,1)} %refs_0_.1, bf16[2,64,128,128]{3,2,1,0:T(8,128)(2,1)} %refs_1_.1, s32[2,512]{1,0:T(2,128)} %refs_2_.1, s32[2]{0:T(128)} %refs_3_.1, f32[5,2048]{1,0:T(8,128)} %refs_4_.3, ...), custom_call_target="tpu_custom_call" | custom-call | tf_op jit(solution)/shard_map/column_attention/pallas_call | solution.py:808
  307.5 0.0 copy-done
  307.5 0.0 copy-done.1
  307.5 0.0 copy-done.2
  307.5 0.0 copy-done.3
  307.5 0.0 copy-done.4
  307.5 0.0 copy-done.5
  307.5 0.0 copy-done.6
  307.6 0.0 copy-done.7
  307.6 0.0 copy-done.8
  307.6 4.2 %lamb_step.1 = (bf16[2,64,128,128]{3,2,1,0:T(8,128)(2,1)}, bf16[2,64,128,128]{3,2,1,0:T(8,128)(2,1)}, f32[5,2048]{1,0:T(8,128)}, f32[5,2048]{1,0:T(8,128)}, f32[...) custom-call(bf16[2,2,8192,128]{3,2,1,0:T(8,128)(2,1)S(1)} %get-tuple, ...), custom_call_target="tpu_custom_call" | custom-call | tf_op jit(solution)/shard_map/lamb_step/pallas_call | solution.py:843
Async XLA Ops:
  0.6 306.8 %copy-start = (f32[5,2048]{1,0:T(8,128)S(1)}, f32[5,2048]{1,0:T(8,128)}, u32[]{:S(2)}) copy-start(f32[5,2048]{1,0:T(8,128)} %refs_4_.3) | copy-start | bytes 122884
  0.7 306.8 %copy-start.1 = (f32[5,2048]{1,0:T(8,128)S(1)}, f32[5,2048]{1,0:T(8,128)}, u32[]{:S(2)}) copy-start(f32[5,2048]{1,0:T(8,128)} %refs_5_.3) | copy-start | bytes 122884
  0.7 306.8 %copy-start.2 = (f32[5,2048]{1,0:T(8,128)S(1)}, f32[5,2048]{1,0:T(8,128)}, u32[]{:S(2)}) copy-start(f32[5,2048]{1,0:T(8,128)} %refs_6_.3) | copy-start | bytes 122884
  0.7 306.8 %copy-start.3 = (f32[128]{0:T(128)S(1)}, f32[128]{0:T(128)}, u32[]{:S(2)}) copy-start(f32[128]{0:T(128)} %param.20) | copy-start | bytes 1540
  0.7 306.8 %copy-start.4 = (f32[4]{0:T(128)S(1)}, f32[4]{0:T(128)}, u32[]{:S(2)}) copy-start(f32[4]{0:T(128)} %refs_8_.1) | copy-start | bytes 52
  0.7 306.8 %copy-start.5 = (f32[128]{0:T(128)S(1)}, f32[128]{0:T(128)}, u32[]{:S(2)}) copy-start(f32[128]{0:T(128)} %param.21) | copy-start | bytes 1540
  0.7 306.8 %copy-start.6 = (f32[128]{0:T(128)S(1)}, f32[128]{0:T(128)}, u32[]{:S(2)}) copy-start(f32[128]{0:T(128)} %param.22) | copy-start | bytes 1540
  0.7 306.8 %copy-start.7 = (f32[4]{0:T(128)S(1)}, f32[4]{0:T(128)}, u32[]{:S(2)}) copy-start(f32[4]{0:T(128)} %param.24) | copy-start | bytes 52
  0.7 306.8 %copy-start.8 = (f32[4]{0:T(128)S(1)}, f32[4]{0:T(128)}, u32[]{:S(2)}) copy-start(f32[4]{0:T(128)} %param.25) | copy-start | bytes 52
